TPU v7x, 32 devices: a whole 2x2x4 slice. The times are simulated.
32 devices in a mesh: patch: 8 (over z, x), sect: 4 (over y, core).
Axes of the slice: x: 2, y: 2, z: 4, core: 2. Of those that a mesh axis runs over, the one named last changes fastest.
Arguments:
- displacement: float32 [16, 3, 128, 4096], P('patch', None, 'sect'), may hold values from -6 to 6
- lame_params: float32 [16, 2], replicated, may hold values from 0.5 to 2
- patch_sizes: int32 [16, 2], P('patch'), may hold values from 34 to 61, as said below
- partners: int32 [16, 4], P('patch'), may hold values from 0 to 63, as said below
- transfer: float32 [16, 4, 64, 64], P('patch'), may hold values from -0.75 to 0.75
Outputs:
- first_apply: float32 [16, 3, 128, 4096], P('patch', None, 'sect')
- second_apply: float32 [16, 3, 128, 4096], P('patch', None, 'sect')
Inputs may be any that keep to these rules, and one draw needn't show every extreme that they name: patch_sizes[p, 0] and patch_sizes[p, 1] count the active control points of patch p along x and y. The relation of faces is symmetric: if partners[p, f] = 4 q + g then partners[q, g] = 4 p + f. The patches 2 i to 2 i + 1 form group i; the faces of group i meet faces of groups i - 1 and i + 1 (modulo the number of groups) only, 4 faces with each.
All inputs are finite; a program needn't handle non-finite values.
Results may differ from a plain program's by a relative error of at most 0.000054.
Values sent between devices are 32-bit elements; how exact they have to be, the bound alone decides.
No kernel may reach another device: no remote copies, remote signals or barrier semaphores. Data moves between devices by JAX's collectives and lax.ppermute only.
A program may use at most 64 MiB of HBM per device.

v0:
```python
import functools

import jax
import jax.numpy as jnp
import ml_dtypes
import numpy as np
from jax import lax
from jax.experimental import pallas as pl
from jax.experimental.pallas import tpu as pltpu
from jax.sharding import PartitionSpec as P

PAD = 64
LANES = 128
HALO = 3
COMPS = 3
FACES = 4
MASS_INT = (2416.0, 1191.0, 120.0, 1.0)
STIFF_INT = (80.0, -15.0, -24.0, -1.0)
SLOPE_INT = (245.0, 56.0, 1.0)
MASS_DEN = 5040.0
STIFF_DEN = 120.0
SLOPE_DEN = 720.0
PENALTY = 3.0
XBLOCK = 16
XROWS = 8
VMEM_BYTES = 56 * 1024 * 1024
F32 = jnp.float32
BF16 = jnp.bfloat16


def split_np(table):
    high = table.astype(ml_dtypes.bfloat16)
    low = (table - high.astype(np.float64)).astype(ml_dtypes.bfloat16)
    return high, low


def band_np(size, kind):
    table = np.zeros((size, size))
    for i in range(size):
        for d in range(0, 4):
            for sign in (1, -1):
                j = i + sign * d
                if 0 <= j < size:
                    if kind == "slope":
                        if d:
                            table[i, j] = sign * SLOPE_INT[d - 1] / SLOPE_DEN
                    elif kind == "mass":
                        table[i, j] = MASS_INT[d] / MASS_DEN
                    else:
                        table[i, j] = STIFF_INT[d] / STIFF_DEN
    return table


def depth_table(depth):
    table = np.concatenate([band_np(depth, k) for k in ("mass", "stiff", "slope")], axis=0)
    high, low = split_np(table)
    return np.concatenate([high, high, low], axis=1)


def plane_tables():
    out = []
    for kind in ("mass", "stiff", "slope"):
        one = band_np(PAD, kind).T
        both = np.zeros((LANES, LANES))
        both[:PAD, :PAD] = one
        both[PAD:, PAD:] = one
        out.append(both)
    return np.stack(out).astype(np.float32)


def order_table():
    table = np.zeros((512, 512))
    for g in range(4):
        for x16 in range(16):
            for p in range(2):
                for layer in range(4):
                    row = g * 128 + x16 * 8 + p * 4 + layer
                    col = ((p * 2 + layer // 2) * 2 + layer % 2) * 64 + 16 * g + x16
                    table[row, col] = 1.0
    return table


def split(values):
    high = values.astype(BF16)
    low = (values - high.astype(F32)).astype(BF16)
    return high, low


def lane_iota(shape=(1, LANES)):
    return lax.broadcasted_iota(jnp.int32, shape, len(shape) - 1)


def swap_halves(values):
    return pltpu.roll(values, PAD, axis=values.ndim - 1)


def merge(low_half, high_half):
    return jnp.where(lane_iota() < PAD, low_half, high_half)


def dot(a, b):
    return jnp.dot(a, b, preferred_element_type=F32)


def face_sides(partners_ref, me, groups):
    before = lax.rem(me + groups - 1, groups)
    codes = [partners_ref[k // FACES, k % FACES] for k in range(2 * FACES)]
    sides = [jnp.where(code // (2 * FACES) == before, 0, 1) for code in codes]
    return codes, sides


def send_sources(partners_ref, me, groups):
    codes, sides = face_sides(partners_ref, me, groups)
    sources = [[jnp.int32(0)] * FACES for _ in range(2)]
    for k in range(2 * FACES):
        rank = jnp.int32(0)
        for other in range(2 * FACES):
            if other != k:
                below = (sides[other] == sides[k]) & (codes[other] < codes[k])
                rank = rank + jnp.where(below, 1, 0)
        for side in range(2):
            for slot in range(FACES):
                hit = (sides[k] == side) & (rank == slot)
                sources[side][slot] = jnp.where(hit, k, sources[side][slot])
    return sources


def receive_slots(partners_ref, me, groups):
    _, sides = face_sides(partners_ref, me, groups)
    slots = []
    for k in range(2 * FACES):
        rank = jnp.int32(0)
        for other in range(k):
            rank = rank + jnp.where(sides[other] == sides[k], 1, 0)
        slots.append(rank)
    return sides, slots


def layer_select(sizes_ref):
    rows = lax.broadcasted_iota(jnp.int32, (LANES, LANES), 0)
    cols = lax.broadcasted_iota(jnp.int32, (LANES, LANES), 1)
    patch = (cols // 4) % 2
    layer = cols % 4
    size_y = jnp.where(patch == 0, sizes_ref[0, 1], sizes_ref[1, 1])
    at = jnp.where(layer < 2, layer, size_y + 1 - layer)
    base = jnp.where(rows == patch * PAD + at, 1.0, 0.0)
    return [jnp.where(cols // 8 == j, base, 0.0).astype(BF16) for j in range(16)]


def row_at(ref, x, depth):
    parts = []
    for c in range(COMPS):
        start = c * PAD * depth + x * depth
        if not isinstance(x, int):
            start = pl.multiple_of(start, depth)
        parts.append(ref[pl.ds(start, depth), :])
    return jnp.concatenate(parts, axis=0)


def send_layers(field, sizes_ref, partners_ref, order, own, to_before, to_after, low, high, me, groups, depth):
    for c in range(COMPS):
        for d in range(HALO):
            low[c, d] = field[pl.ds(c * PAD * depth + d, PAD, stride=depth), :]
            high[c, d] = field[pl.ds(c * PAD * depth + depth - HALO + d, PAD, stride=depth), :]
    outer, inner = row_at(field, 0, depth), row_at(field, 1, depth)
    own[0] = merge(outer, swap_halves(inner))
    own[FACES] = merge(swap_halves(outer), inner)
    outer, inner = [row_at(field, sizes_ref[0, 0] - 1 - i, depth) for i in range(2)]
    own[1] = merge(outer, swap_halves(inner))
    outer, inner = [row_at(field, sizes_ref[1, 0] - 1 - i, depth) for i in range(2)]
    own[FACES + 1] = merge(swap_halves(outer), inner)
    select = jnp.concatenate(layer_select(sizes_ref), axis=0)
    groups_rows = []
    for g in range(4):
        for c in range(COMPS):
            base = c * PAD * depth + 16 * g * depth
            wide = [field[base + j * depth : base + (j + 1) * depth, :] for j in range(16)]
            groups_rows.append(jnp.concatenate(wide, axis=1))
    rows = jnp.concatenate(groups_rows, axis=0)
    count = rows.shape[0]
    row_high, row_low = split(rows)
    picked = dot(jnp.concatenate([row_high, row_low], axis=0), select)
    picked = picked[:count] + picked[count:]
    per = COMPS * depth
    picked = jnp.concatenate([picked[g * per : (g + 1) * per] for g in range(4)], axis=1)
    pick_high, pick_low = split(picked)
    sorted_layers = dot(jnp.concatenate([pick_high, pick_low], axis=0), order[...])
    sorted_layers = sorted_layers[:per] + sorted_layers[per:]
    for p in range(2):
        for f in range(2):
            at = (p * 2 + f) * LANES
            own[p * FACES + 2 + f] = sorted_layers[:, at : at + LANES]
    sources = send_sources(partners_ref, me, groups)
    for slot in range(FACES):
        to_before[slot] = own[sources[0][slot]]
        to_after[slot] = own[sources[1][slot]]


def active_lanes(sizes_ref):
    lane = lane_iota()
    size_x = jnp.where(lane < PAD, sizes_ref[0, 0], sizes_ref[1, 0])
    size_y = jnp.where(lane < PAD, sizes_ref[0, 1], sizes_ref[1, 1])
    return size_x, (lane % PAD) < size_y


def start_kernel(groups, depth, me_ref, sizes_ref, partners_ref, disp, order, field, own, to_before, to_after, low, high):
    me = me_ref[0]
    size_x, in_y = active_lanes(sizes_ref)
    for k in range(PAD // 2):
        keep_even = in_y & (2 * k < size_x)
        keep_odd = in_y & (2 * k + 1 < size_x)
        for c in range(COMPS):
            one = disp[0, c, :, k * LANES : (k + 1) * LANES]
            two = disp[1, c, :, k * LANES : (k + 1) * LANES]
            even = merge(one, swap_halves(two))
            odd = merge(swap_halves(one), two)
            base = (c * PAD + 2 * k) * depth
            field[base : base + depth, :] = jnp.where(keep_even, even, 0.0)
            field[base + depth : base + 2 * depth, :] = jnp.where(keep_odd, odd, 0.0)
    send_layers(field, sizes_ref, partners_ref, order, own, to_before, to_after, low, high, me, groups, depth)


MASS, STIFF, SLOPE = 0, 1, 2
TILES = (
    (((0, MASS), (0, STIFF)), ((0, STIFF), (0, MASS))),
    (((1, MASS), (1, STIFF)), ((1, STIFF), (1, MASS))),
    (((2, MASS), (2, STIFF)), ((2, STIFF), (2, MASS))),
    (((1, MASS), (2, SLOPE)), ((0, SLOPE), (1, MASS))),
    (((0, SLOPE), (1, SLOPE)), ((2, SLOPE), (2, MASS))),
    (((0, MASS), None), ((1, SLOPE), None)),
)
TERMS = {
    ((0, MASS), (0, STIFF)): (MASS, "both"),
    ((0, MASS), (0, MASS)): (STIFF, "mu"),
    ((0, STIFF), (0, MASS)): (MASS, "mu"),
    ((1, MASS), (0, SLOPE)): (SLOPE, "grad"),
    ((2, SLOPE), (0, SLOPE)): (MASS, "grad"),
    ((1, MASS), (1, STIFF)): (MASS, "mu"),
    ((1, MASS), (1, MASS)): (STIFF, "both"),
    ((1, STIFF), (1, MASS)): (MASS, "mu"),
    ((2, SLOPE), (1, MASS)): (SLOPE, "grad"),
    ((0, MASS), (1, SLOPE)): (SLOPE, "grad"),
    ((2, MASS), (2, STIFF)): (MASS, "mu"),
    ((2, MASS), (2, MASS)): (STIFF, "mu"),
    ((2, STIFF), (2, MASS)): (MASS, "both"),
    ((1, SLOPE), (2, MASS)): (SLOPE, "grad"),
    ((0, SLOPE), (2, SLOPE)): (MASS, "grad"),
}
OUT_SCALE = {STIFF: 1.0 / STIFF_DEN, MASS: 1.0 / MASS_DEN, SLOPE: 1.0 / SLOPE_DEN}


def weights_kernel(lame_ref, me_ref, tables, weights):
    first = me_ref[0] * 2
    lane = lane_iota()

    def per_lane(one, two):
        return jnp.where(lane < PAD, one, two)

    mu = per_lane(lame_ref[first, 0], lame_ref[first + 1, 0])
    grad = mu + per_lane(lame_ref[first, 1], lame_ref[first + 1, 1])
    factors = {"mu": mu, "both": mu + grad, "grad": -grad}
    placed = set()
    for t, (sources, targets) in enumerate(TILES):
        for i, source in enumerate(sources):
            for o, target in enumerate(targets):
                term = TERMS.get((source, target))
                if term is None or (source, target) in placed:
                    block = jnp.zeros((LANES, LANES), F32)
                else:
                    placed.add((source, target))
                    block = tables[term[0]] * (factors[term[1]] * OUT_SCALE[target[1]])
                block_high, block_low = split(block)
                cols = slice(o * LANES, (o + 1) * LANES)
                for part, piece in enumerate((block_high, block_high, block_low)):
                    at = part * 2 * LANES + i * LANES
                    weights[t, at : at + LANES, cols] = piece


def plane_sums(fields, weights):
    sums = {}
    for t, (sources, targets) in enumerate(TILES):
        if sources[1] is None:
            high, low = fields[sources[0]]
            weight = jnp.concatenate(
                [weights[t, part * 2 * LANES : part * 2 * LANES + LANES, :LANES] for part in range(3)], axis=0
            )
        else:
            high, low = [jnp.concatenate([fields[s][part] for s in sources], axis=1) for part in range(2)]
            weight = weights[t]
        out = dot(jnp.concatenate([high, low, high], axis=1), weight)
        for o, target in enumerate(targets):
            if target is not None:
                piece = out[:, o * LANES : (o + 1) * LANES]
                sums[target] = piece if target not in sums else sums[target] + piece
    return sums


def band_x(stiff, mass, slope):
    total = STIFF_INT[0] * stiff(0) + MASS_INT[0] * mass(0)
    for d in (1, 2):
        total = total + STIFF_INT[d] * (stiff(d) + stiff(-d))
        total = total + MASS_INT[d] * (mass(d) + mass(-d))
        total = total + SLOPE_INT[d - 1] * (slope(d) - slope(-d))
    return total + ((mass(3) + mass(-3)) - (stiff(3) + stiff(-3))) + (slope(3) - slope(-3))


def volume_kernel(depth, field, z_table, weights, out, sums_ref):
    for i in range(9):
        for x in (0, 1, 2, PAD + 3, PAD + 4, PAD + 5):
            sums_ref[i, x] = jnp.zeros((depth, LANES), F32)

    def in_plane(block, carry):
        x0 = block * XBLOCK
        fields = {}
        for c in range(COMPS):
            start = pl.multiple_of((c * PAD + x0) * depth, XBLOCK * depth)
            rows = field[pl.ds(start, XBLOCK * depth), :]
            wide = jnp.concatenate([rows[j * depth : (j + 1) * depth] for j in range(XBLOCK)], axis=1)
            high, low = split(wide)
            banded = dot(z_table[...], jnp.concatenate([high, low, high], axis=0))
            parts = split(banded)
            for kind in range(3):
                fields[(c, kind)] = tuple(
                    jnp.concatenate(
                        [
                            part[kind * depth : (kind + 1) * depth, j * LANES : (j + 1) * LANES]
                            for j in range(XBLOCK)
                        ],
                        axis=0,
                    )
                    for part in parts
                )
        sums = plane_sums(fields, weights)
        for (c, kind), value in sums.items():
            sums_ref[c * 3 + kind, pl.ds(x0 + 3, XBLOCK)] = value.reshape(XBLOCK, depth, LANES)
        return carry

    lax.fori_loop(0, PAD // XBLOCK, in_plane, 0)

    def along_x(step, carry):
        x0 = (step // (depth // 8)) * XROWS
        z0 = pl.multiple_of((step % (depth // 8)) * 8, 8)
        for c in range(COMPS):
            held = [sums_ref[c * 3 + kind, pl.ds(x0, XROWS + 6), pl.ds(z0, 8), :] for kind in range(3)]

            def at(kind):
                return lambda d: held[kind][3 + d : 3 + d + XROWS]

            result = band_x(at(STIFF), at(MASS), at(SLOPE))
            for j in range(XROWS):
                start = pl.multiple_of((c * PAD + x0 + j) * depth + z0, 8)
                out[pl.ds(start, 8), :] = result[j]
        return carry

    lax.fori_loop(0, (PAD // XROWS) * (depth // 8), along_x, 0)


def depth_edges(before, after):
    mass, stiff, slope = [], [], []
    for table, den, out, sign in (
        (MASS_INT[1:], MASS_DEN, mass, 1.0),
        (STIFF_INT[1:], STIFF_DEN, stiff, 1.0),
        (SLOPE_INT, SLOPE_DEN, slope, -1.0),
    ):
        coef = [value / den for value in table]
        for z in range(3):
            total = None
            for d in range(z + 1, 4):
                piece = (sign * coef[d - 1]) * before[3 + z - d]
                total = piece if total is None else total + piece
            out.append(total)
        for z in range(3):
            total = None
            for d in range(3 - z, 4):
                piece = coef[d - 1] * after[z + d - 3]
                total = piece if total is None else total + piece
            out.append(total)
    return [jnp.concatenate(parts, axis=0) for parts in (mass, stiff, slope)]


EDGE_ROWS = 80


def finish_kernel(
    groups,
    depth,
    last,
    me_ref,
    sizes_ref,
    partners_ref,
    lame_ref,
    volume,
    own,
    from_before,
    from_after,
    z_before,
    z_after,
    transfer,
    weights,
    order,
    order_back,
    result,
    *rest,
):
    if last:
        field, edge = rest
    else:
        field, own_next, to_before, to_after, low, high, edge = rest
    me = me_ref[0]
    sides, slots = receive_slots(partners_ref, me, groups)
    terms = []
    for p in range(2):
        for f in range(FACES):
            k = p * FACES + f
            far = jnp.where(sides[k] == 0, from_before[slots[k]], from_after[slots[k]])
            mu_face = 0.5 * (lame_ref[me * 2 + p, 0] + lame_ref[partners_ref[p, f] // FACES, 0])
            mat = transfer[p, f]
            zero = jnp.zeros((PAD, PAD), F32)
            both = jnp.concatenate(
                [jnp.concatenate([mat, zero], axis=1), jnp.concatenate([zero, mat], axis=1)], axis=0
            )
            far_high, far_low = split(far)
            mat_high, mat_low = split(both)
            moved = lax.dot_general(
                jnp.concatenate([far_high, far_low, far_high], axis=1),
                jnp.concatenate([mat_high, mat_high, mat_low], axis=1),
                (((1,), (1,)), ((), ())),
                preferred_element_type=F32,
            )
            terms.append(((PENALTY - 1.5) * mu_face) * (own[k] - moved))
    per = COMPS * depth
    stacked = jnp.concatenate([swap_halves(terms[p * FACES + 2 + f]) for p in range(2) for f in range(2)], axis=1)
    term_high, term_low = split(stacked)
    placed = dot(jnp.concatenate([term_high, term_low], axis=0), order_back[...])
    placed = placed[:per] + placed[per:]
    placed = jnp.concatenate([placed[:, g * LANES : (g + 1) * LANES] for g in range(4)], axis=0)
    placed_parts = jnp.concatenate(split(placed), axis=1)
    select = layer_select(sizes_ref)
    for j in range(0, 16, 2):
        pair = jnp.concatenate([select[j], select[j + 1]], axis=0)
        spread = lax.dot_general(
            placed_parts,
            jnp.concatenate([pair, pair], axis=1),
            (((1,), (1,)), ((), ())),
            preferred_element_type=F32,
        )
        for g in range(4):
            for c in range(COMPS):
                for i in range(2):
                    base = (c * PAD + 16 * g + j + i) * depth
                    at = (g * COMPS + c) * depth
                    piece = spread[at : at + depth, i * LANES : (i + 1) * LANES]
                    field[base : base + depth, :] = volume[base : base + depth, :] + piece
    def add_row(x, addend):
        for c in range(COMPS):
            start = c * PAD * depth + x * depth
            if not isinstance(x, int):
                start = pl.multiple_of(start, depth)
            field[pl.ds(start, depth), :] += addend[c * depth : (c + 1) * depth]

    zero = jnp.zeros((per, LANES), F32)
    one, two = terms[0], terms[FACES]
    add_row(0, merge(swap_halves(one), two))
    add_row(1, merge(one, swap_halves(two)))
    one, two = terms[1], terms[FACES + 1]
    add_row(sizes_ref[0, 0] - 1, merge(swap_halves(one), zero))
    add_row(sizes_ref[0, 0] - 2, merge(one, zero))
    add_row(sizes_ref[1, 0] - 1, merge(zero, two))
    add_row(sizes_ref[1, 0] - 2, merge(zero, swap_halves(two)))
    fields = {}
    for c in range(COMPS):
        banded = depth_edges([z_before[c, d] for d in range(HALO)], [z_after[c, d] for d in range(HALO)])
        for kind in range(3):
            fields[(c, kind)] = split(banded[kind])
    sums = plane_sums(fields, weights)
    for (c, kind), value in sums.items():
        for z in range(2 * HALO):
            base = ((c * 3 + kind) * 2 * HALO + z) * EDGE_ROWS
            edge[base : base + 8, :] = jnp.zeros((8, LANES), F32)
            edge[base + 8 + PAD : base + EDGE_ROWS, :] = jnp.zeros((8, LANES), F32)
            edge[base + 8 : base + 8 + PAD, :] = value[z * PAD : (z + 1) * PAD]
    for c in range(COMPS):
        for z in range(2 * HALO):

            def at(kind):
                base = ((c * 3 + kind) * 2 * HALO + z) * EDGE_ROWS + 8
                return lambda d: edge[base + d : base + d + PAD, :]

            plane = z if z < HALO else depth - 2 * HALO + z
            rows = pl.ds(c * PAD * depth + plane, PAD, stride=depth)
            field[rows, :] += band_x(at(STIFF), at(MASS), at(SLOPE))
    size_x, in_y = active_lanes(sizes_ref)
    for k in range(PAD // 2):
        keep_even = in_y & (2 * k < size_x)
        keep_odd = in_y & (2 * k + 1 < size_x)
        for c in range(COMPS):
            base = (c * PAD + 2 * k) * depth
            even = jnp.where(keep_even, field[base : base + depth, :], 0.0)
            odd = jnp.where(keep_odd, field[base + depth : base + 2 * depth, :], 0.0)
            if not last:
                field[base : base + depth, :] = even
                field[base + depth : base + 2 * depth, :] = odd
            result[0, c, :, k * LANES : (k + 1) * LANES] = merge(even, swap_halves(odd))
            result[1, c, :, k * LANES : (k + 1) * LANES] = merge(swap_halves(even), odd)
    if not last:
        send_layers(
            field, sizes_ref, partners_ref, order, own_next, to_before, to_after, low, high, me, groups, depth
        )


def shards(displacement, lame_params, patch_sizes, partners, transfer):
    depth = displacement.shape[2]
    groups = lax.axis_size("patch")
    sections = lax.axis_size("sect")
    me = lax.axis_index("patch").astype(jnp.int32).reshape(1)
    rows = COMPS * PAD * depth
    per = COMPS * depth
    smem = pl.BlockSpec(memory_space=pltpu.SMEM)
    vmem = pl.BlockSpec(memory_space=pltpu.VMEM)
    params = pltpu.CompilerParams(vmem_limit_bytes=VMEM_BYTES)
    z_table = jnp.asarray(depth_table(depth))
    order = jnp.asarray(order_table().astype(ml_dtypes.bfloat16))
    order_back = jnp.asarray(order_table().T.astype(ml_dtypes.bfloat16))

    def shape(*dims, dtype=F32):
        return jax.ShapeDtypeStruct(dims, dtype)

    field_shape = shape(rows, LANES)
    layer_shapes = (
        shape(2 * FACES, per, LANES),
        shape(FACES, per, LANES),
        shape(FACES, per, LANES),
        shape(COMPS, HALO, PAD, LANES),
        shape(COMPS, HALO, PAD, LANES),
    )

    def exchange(layers):
        own, to_before, to_after, low, high = layers
        forward = [(i, (i + 1) % groups) for i in range(groups)]
        backward = [((i + 1) % groups, i) for i in range(groups)]
        from_before = lax.ppermute(to_after, "patch", forward)
        from_after = lax.ppermute(to_before, "patch", backward)
        z_before = lax.ppermute(high, "sect", [(i, i + 1) for i in range(sections - 1)])
        z_after = lax.ppermute(low, "sect", [(i + 1, i) for i in range(sections - 1)])
        return own, from_before, from_after, z_before, z_after

    weights = pl.pallas_call(
        weights_kernel,
        out_shape=shape(len(TILES), 6 * LANES, 2 * LANES, dtype=BF16),
        in_specs=[smem, smem, vmem],
        out_specs=vmem,
        compiler_params=params,
        name="plane_weights",
    )(lame_params, me, jnp.asarray(plane_tables()))

    field, *layers = pl.pallas_call(
        functools.partial(start_kernel, groups, depth),
        out_shape=(field_shape,) + layer_shapes,
        in_specs=[smem, smem, smem, vmem, vmem],
        out_specs=(vmem,) * 6,
        compiler_params=params,
        name="start_layers",
    )(me, patch_sizes, partners, displacement, order)

    def volume(values):
        return pl.pallas_call(
            functools.partial(volume_kernel, depth),
            out_shape=field_shape,
            in_specs=[vmem] * 3,
            out_specs=vmem,
            scratch_shapes=[pltpu.VMEM((9, PAD + 6, depth, LANES), F32)],
            compiler_params=params,
            cost_estimate=pl.CostEstimate(flops=10**10, bytes_accessed=8 * 10**6, transcendentals=0),
            name="volume_terms",
        )(values, z_table, weights)

    def finish(volume_part, exchanged, last):
        scratch = [pltpu.VMEM((9 * 2 * HALO * EDGE_ROWS, LANES), F32)]
        out_shape = (shape(*displacement.shape),)
        if last:
            scratch = [pltpu.VMEM((rows, LANES), F32)] + scratch
        else:
            out_shape = out_shape + (field_shape,) + layer_shapes
        return pl.pallas_call(
            functools.partial(finish_kernel, groups, depth, last),
            out_shape=out_shape,
            in_specs=[smem] * 4 + [vmem] * 10,
            out_specs=(vmem,) * len(out_shape),
            scratch_shapes=scratch,
            compiler_params=params,
            name="finish_last" if last else "finish_first",
        )(me, patch_sizes, partners, lame_params, volume_part, *exchanged, transfer, weights, order, order_back)

    first_apply, field, *next_layers = finish(volume(field), exchange(layers), False)
    (second_apply,) = finish(volume(field), exchange(next_layers), True)
    return first_apply, second_apply


def solution(mesh):
    return jax.shard_map(
        shards,
        mesh=mesh,
        in_specs=(
            P("patch", None, "sect", None),
            P(),
            P("patch", None),
            P("patch", None),
            P("patch", None, None, None),
        ),
        out_specs=(P("patch", None, "sect", None), P("patch", None, "sect", None)),
        check_vma=False,
    )
```

profile of v0, /device:TPU:1, one launch (start us, length us, event | category | flops | bytes accessed | tf_op | source)
XLA Modules:
  0.0 82.5 jit_solution(6775283051432973129)
XLA Ops:
  0.6 5.7 %start_layers.1 = (f32[6144,128]{1,0:T(8,128)}, f32[8,96,128]{2,1,0:T(8,128)}, f32[4,96,128]{2,1,0:T(8,128)}, f32[4,96,128]{2,1,0:T(8,128)}, f32[3,3,64,128]{3,2,1,0:T(8,128)}, /*index=5*/f32[3,3,64,128]{3,2,1,0:T(8,128)}) custom-call(s32[1]{0:T(128)} %bitcast.me_ref, s32[2,2]{1,0:T(2,128)} %sizes_ref.5, s32[2,4]{1,0:T(2,128)} %partners_ref.5, ...), custom_call_target="tpu_custom_call" | custom-call | tf_op jit(solution)/shard_map/start_layers/pallas_call | solution.py:556
  6.3 2.0 %collective-permute-start = (f32[4,96,128]{2,1,0:T(8,128)}, f32[4,96,128]{2,1,0:T(8,128)S(1)}, u32[]{:S(2)}, u32[]{:S(2)}) collective-permute-start(f32[4,96,128]{2,1,0:T(8,128)} %get-tuple-element.17), channel_id=1, source_target_pairs={{0,4},{4,8},{8,12},{12,16},{16,20},{20,24},{24,28},{28,0},{1,5},{5... | collective-permute-start | bytes 589832 | tf_op jit(solution)/shard_map/ppermute | solution.py:541
  8.4 3.1 %collective-permute-start.1 = (f32[4,96,128]{2,1,0:T(8,128)}, f32[4,96,128]{2,1,0:T(8,128)S(1)}, u32[]{:S(2)}, u32[]{:S(2)}) collective-permute-start(f32[4,96,128]{2,1,0:T(8,128)} %get-tuple-element.18), channel_id=1, source_target_pairs={{4,0},{8,4},{12,8},{16,12},{20,16},{24,20},{28,24},{0,28},{5,1},{9... | collective-permute-start | bytes 589832 | tf_op jit(solution)/shard_map/ppermute | solution.py:542
  11.4 4.1 %collective-permute-start.2 = (f32[3,3,64,128]{3,2,1,0:T(8,128)}, f32[3,3,64,128]{3,2,1,0:T(8,128)S(1)}, u32[]{:S(2)}, u32[]{:S(2)}) collective-permute-start(f32[3,3,64,128]{3,2,1,0:T(8,128)} %get-tuple-element.19), channel_id=1, source_target_pairs={{0,1},{1,2},{2,3},{4,5},{5,6},{6,7},{8,9},{9,10},{10,11},{12,13},{... | collective-permute-start | bytes 884744 | tf_op jit(solution)/shard_map/ppermute | solution.py:543
  15.6 1.9 %collective-permute-start.3 = (f32[3,3,64,128]{3,2,1,0:T(8,128)}, f32[3,3,64,128]{3,2,1,0:T(8,128)S(1)}, u32[]{:S(2)}, u32[]{:S(2)}) collective-permute-start(f32[3,3,64,128]{3,2,1,0:T(8,128)} %get-tuple-element.20), channel_id=1, source_target_pairs={{1,0},{2,1},{3,2},{5,4},{6,5},{7,6},{9,8},{10,9},{11,10},{13,12},{... | collective-permute-start | bytes 884744 | tf_op jit(solution)/shard_map/ppermute | solution.py:544
  17.5 0.0 copy-done.8
  17.5 0.7 copy.12.lame_ref
  18.2 2.7 %plane_weights.1.weights = bf16[6,768,256]{2,1,0:T(8,128)(2,1)} custom-call(f32[16,2]{1,0:T(8,128)} %copy.12.lame_ref, s32[1]{0:T(128)} %bitcast.me_ref, f32[3,128,128]{2,1,0:T(8,128)} %constant.17.clone.tables), custom_call_target="tpu_custom_call" | custom-call | tf_op jit(solution)/shard_map/plane_weights/pallas_call | solution.py:547
  20.9 14.0 %volume_terms.2.volume = f32[6144,128]{1,0:T(8,128)} custom-call(f32[6144,128]{1,0:T(8,128)} %get-tuple-element.15.field, bf16[96,96]{1,0:T(8,128)(2,1)} %constant.14.clone.z_table, bf16[6,768,256]{2,1,0:T(8,128)(2,1)} %plane_weights.1.weights), custom_call_target="tpu_custom_call" | custom-call | flops 10000000000 | bytes 8000000 | tf_op jit(solution)/shard_map/volume_terms/pallas_call | solution.py:566
  34.9 0.0 collective-permute-done.from_before
  34.9 0.0 collective-permute-done.1.from_after
  34.9 0.0 collective-permute-done.2.z_before
  35.0 0.0 collective-permute-done.3.z_after
  35.0 0.6 copy-done.4
  35.6 0.1 copy-done.5
  35.7 0.1 copy-done
  35.8 0.1 copy-done.1
  35.9 12.0 %finish_first.1 = (f32[2,3,32,4096]{3,2,1,0:T(8,128)}, f32[6144,128]{1,0:T(8,128)}, f32[8,96,128]{2,1,0:T(8,128)}, f32[4,96,128]{2,1,0:T(8,128)}, f32[4,96,128]{...) custom-call(s32[1]{0:T(128)} %bitcast.me_ref, s32[2,2]{1,0:T(2,128)} %sizes_ref.5, ...), custom_call_target="tpu_custom_call" | custom-call | tf_op jit(solution)/shard_map/finish_first/pallas_call | solution.py:584
  47.9 0.0 collective-permute-start.4
  47.9 4.2 %collective-permute-start.5 = (f32[4,96,128]{2,1,0:T(8,128)}, f32[4,96,128]{2,1,0:T(8,128)S(1)}, u32[]{:S(2)}, u32[]{:S(2)}) collective-permute-start(f32[4,96,128]{2,1,0:T(8,128)} %get-tuple-element.25), channel_id=1, source_target_pairs={{4,0},{8,4},{12,8},{16,12},{20,16},{24,20},{28,24},{0,28},{5,1},{9... | collective-permute-start | bytes 589832 | tf_op jit(solution)/shard_map/ppermute | solution.py:542
  52.1 4.2 %collective-permute-start.6 = (f32[3,3,64,128]{3,2,1,0:T(8,128)}, f32[3,3,64,128]{3,2,1,0:T(8,128)S(1)}, u32[]{:S(2)}, u32[]{:S(2)}) collective-permute-start(f32[3,3,64,128]{3,2,1,0:T(8,128)} %get-tuple-element.26), channel_id=1, source_target_pairs={{0,1},{1,2},{2,3},{4,5},{5,6},{6,7},{8,9},{9,10},{10,11},{12,13},{... | collective-permute-start | bytes 884744 | tf_op jit(solution)/shard_map/ppermute | solution.py:543
  56.3 2.1 %collective-permute-start.7 = (f32[3,3,64,128]{3,2,1,0:T(8,128)}, f32[3,3,64,128]{3,2,1,0:T(8,128)S(1)}, u32[]{:S(2)}, u32[]{:S(2)}) collective-permute-start(f32[3,3,64,128]{3,2,1,0:T(8,128)} %get-tuple-element.27), channel_id=1, source_target_pairs={{1,0},{2,1},{3,2},{5,4},{6,5},{7,6},{9,8},{10,9},{11,10},{13,12},{... | collective-permute-start | bytes 884744 | tf_op jit(solution)/shard_map/ppermute | solution.py:544
  58.4 14.0 %volume_terms.3.volume = f32[6144,128]{1,0:T(8,128)} custom-call(f32[6144,128]{1,0:T(8,128)} %get-tuple-element.22.field, bf16[96,96]{1,0:T(8,128)(2,1)} %constant.14.clone.z_table, bf16[6,768,256]{2,1,0:T(8,128)(2,1)} %plane_weights.1.weights), custom_call_target="tpu_custom_call" | custom-call | flops 10000000000 | bytes 8000000 | tf_op jit(solution)/shard_map/volume_terms/pallas_call | solution.py:566
  72.4 0.0 collective-permute-done.4.from_before
  72.4 0.0 collective-permute-done.5.from_after
  72.4 0.0 collective-permute-done.6.z_before
  72.5 0.0 collective-permute-done.7.z_after
  72.5 0.6 copy-done.6
  73.1 0.1 copy-done.7
  73.2 0.1 copy-done.2
  73.3 0.1 copy-done.3
  73.4 9.1 %finish_last.1 = f32[2,3,32,4096]{3,2,1,0:T(8,128)} custom-call(s32[1]{0:T(128)} %bitcast.me_ref, s32[2,2]{1,0:T(2,128)} %sizes_ref.5, s32[2,4]{1,0:T(2,128)} %partners_ref.5, f32[16,2]{1,0:T(8,128)} %copy.12.lame_ref, f32[6144,128]{1,0:T(8,128)} %volume_terms.3.volume, f32[8,96,128]{2,1,0:T(8,128)} %get-tuple-element.23.own, f32[4,96,128]{2,1,0:T(8,128)} %copy-done.6, ...), custom_call_target="tpu_custom_call" | custom-call | tf_op jit(solution)/shard_map/finish_last/pallas_call | solution.py:584
  (9 shorter events, 0.0 us)
Async XLA Ops:
  0.6 16.9 %copy-start.8 = (f32[16,2]{0,1:T(2,128)S(1)}, f32[16,2]{0,1:T(2,128)}, u32[]{:S(2)}) copy-start(f32[16,2]{0,1:T(2,128)} %param.10) | copy-start | bytes 388
  6.3 28.6 %collective-permute-start = (f32[4,96,128]{2,1,0:T(8,128)}, f32[4,96,128]{2,1,0:T(8,128)S(1)}, u32[]{:S(2)}, u32[]{:S(2)}) collective-permute-start(f32[4,96,128]{2,1,0:T(8,128)} %get-tuple-element.17), channel_id=1, source_target_pairs={{0,4},{4,8},{8,12},{12,16},{16,20},{20,24},{24,28},{28,0},{1,5},{5... | collective-permute-start | bytes 589832 | tf_op jit(solution)/shard_map/ppermute | solution.py:541
  8.4 26.6 %collective-permute-start.1 = (f32[4,96,128]{2,1,0:T(8,128)}, f32[4,96,128]{2,1,0:T(8,128)S(1)}, u32[]{:S(2)}, u32[]{:S(2)}) collective-permute-start(f32[4,96,128]{2,1,0:T(8,128)} %get-tuple-element.18), channel_id=1, source_target_pairs={{4,0},{8,4},{12,8},{16,12},{20,16},{24,20},{28,24},{0,28},{5,1},{9... | collective-permute-start | bytes 589832 | tf_op jit(solution)/shard_map/ppermute | solution.py:542
  11.4 23.5 %collective-permute-start.2 = (f32[3,3,64,128]{3,2,1,0:T(8,128)}, f32[3,3,64,128]{3,2,1,0:T(8,128)S(1)}, u32[]{:S(2)}, u32[]{:S(2)}) collective-permute-start(f32[3,3,64,128]{3,2,1,0:T(8,128)} %get-tuple-element.19), channel_id=1, source_target_pairs={{0,1},{1,2},{2,3},{4,5},{5,6},{6,7},{8,9},{9,10},{10,11},{12,13},{... | collective-permute-start | bytes 884744 | tf_op jit(solution)/shard_map/ppermute | solution.py:543
  15.6 19.4 %collective-permute-start.3 = (f32[3,3,64,128]{3,2,1,0:T(8,128)}, f32[3,3,64,128]{3,2,1,0:T(8,128)S(1)}, u32[]{:S(2)}, u32[]{:S(2)}) collective-permute-start(f32[3,3,64,128]{3,2,1,0:T(8,128)} %get-tuple-element.20), channel_id=1, source_target_pairs={{1,0},{2,1},{3,2},{5,4},{6,5},{7,6},{9,8},{10,9},{11,10},{13,12},{... | collective-permute-start | bytes 884744 | tf_op jit(solution)/shard_map/ppermute | solution.py:544
  34.9 0.7 copy-start.4
  34.9 0.8 copy-start.5
  34.9 0.9 %copy-start = (f32[3,3,64,128]{3,2,1,0:T(8,128)}, f32[3,3,64,128]{3,2,1,0:T(8,128)S(1)}, u32[]{:S(2)}) copy-start(f32[3,3,64,128]{3,2,1,0:T(8,128)S(1)} %collective-permute-done.2.z_before) | copy-start | bytes 884740
  35.0 0.9 %copy-start.1 = (f32[3,3,64,128]{3,2,1,0:T(8,128)}, f32[3,3,64,128]{3,2,1,0:T(8,128)S(1)}, u32[]{:S(2)}) copy-start(f32[3,3,64,128]{3,2,1,0:T(8,128)S(1)} %collective-permute-done.3.z_after) | copy-start | bytes 884740
  47.9 24.5 %collective-permute-start.4 = (f32[4,96,128]{2,1,0:T(8,128)}, f32[4,96,128]{2,1,0:T(8,128)S(1)}, u32[]{:S(2)}, u32[]{:S(2)}) collective-permute-start(f32[4,96,128]{2,1,0:T(8,128)} %get-tuple-element.24), channel_id=1, source_target_pairs={{0,4},{4,8},{8,12},{12,16},{16,20},{20,24},{24,28},{28,0},{1,5},{5... | collective-permute-start | bytes 589832 | tf_op jit(solution)/shard_map/ppermute | solution.py:541
  47.9 24.5 %collective-permute-start.5 = (f32[4,96,128]{2,1,0:T(8,128)}, f32[4,96,128]{2,1,0:T(8,128)S(1)}, u32[]{:S(2)}, u32[]{:S(2)}) collective-permute-start(f32[4,96,128]{2,1,0:T(8,128)} %get-tuple-element.25), channel_id=1, source_target_pairs={{4,0},{8,4},{12,8},{16,12},{20,16},{24,20},{28,24},{0,28},{5,1},{9... | collective-permute-start | bytes 589832 | tf_op jit(solution)/shard_map/ppermute | solution.py:542
  52.1 20.4 %collective-permute-start.6 = (f32[3,3,64,128]{3,2,1,0:T(8,128)}, f32[3,3,64,128]{3,2,1,0:T(8,128)S(1)}, u32[]{:S(2)}, u32[]{:S(2)}) collective-permute-start(f32[3,3,64,128]{3,2,1,0:T(8,128)} %get-tuple-element.26), channel_id=1, source_target_pairs={{0,1},{1,2},{2,3},{4,5},{5,6},{6,7},{8,9},{9,10},{10,11},{12,13},{... | collective-permute-start | bytes 884744 | tf_op jit(solution)/shard_map/ppermute | solution.py:543
  56.3 16.2 %collective-permute-start.7 = (f32[3,3,64,128]{3,2,1,0:T(8,128)}, f32[3,3,64,128]{3,2,1,0:T(8,128)S(1)}, u32[]{:S(2)}, u32[]{:S(2)}) collective-permute-start(f32[3,3,64,128]{3,2,1,0:T(8,128)} %get-tuple-element.27), channel_id=1, source_target_pairs={{1,0},{2,1},{3,2},{5,4},{6,5},{7,6},{9,8},{10,9},{11,10},{13,12},{... | collective-permute-start | bytes 884744 | tf_op jit(solution)/shard_map/ppermute | solution.py:544
  72.4 0.7 copy-start.6
  72.4 0.7 copy-start.7
  72.4 0.8 copy-start.2
  72.5 0.9 %copy-start.3 = (f32[3,3,64,128]{3,2,1,0:T(8,128)}, f32[3,3,64,128]{3,2,1,0:T(8,128)S(1)}, u32[]{:S(2)}) copy-start(f32[3,3,64,128]{3,2,1,0:T(8,128)S(1)} %collective-permute-done.7.z_after) | copy-start | bytes 884740
where the time goes:
time: 82.8 us; the launch traced here: 82.5 us
  Pallas kernels  57.6 us (70%)
  starting transfers between devices  21.6 us (26%)
  local copies, waits for them, and re-layouts  2.5 us (3%)
    pallas_call x2, Pallas kernels, volume(): pl.pallas_call(functools.partial(volume_kernel, depth), out_shape=field_s...  28.1 us
    pallas_call x2, Pallas kernels, finish(): pl.pallas_call(functools.partial(finish_kernel, groups, depth, last), out...  21.2 us
    ppermute x2, starting transfers between devices, exchange(): lax.ppermute(high, 'sect', [(i, i + 1) for i in range(sections - 1)])  8.31 us
    ppermute x2, starting transfers between devices, exchange(): from_after = lax.ppermute(to_before, 'patch', backward)  7.24 us
    pallas_call x1, Pallas kernels, shards(): pl.pallas_call(functools.partial(start_kernel, groups, depth), out_shape=...  5.67 us
    ppermute x2, starting transfers between devices, exchange(): lax.ppermute(low, 'sect', [(i + 1, i) for i in range(sections - 1)])  4.02 us
    pallas_call x1, Pallas kernels, shards(): pl.pallas_call(weights_kernel, out_shape=shape(len(TILES), 6 * LANES, 2 *...  2.7 us
    unnamed x19, local copies, waits for them, and re-layouts  2.5 us
  transfers between devices with their start and end apart: 8, of which 0 were waited for; matrix products, arithmetic and copies ran while one was open for 1% of the time, Pallas kernels for 37%

commit v1 on v0

--- a/solution.py
+++ b/solution.py
@@ -23,7 +23,7 @@
 PENALTY = 3.0
 XBLOCK = 16
 XROWS = 8
-VMEM_BYTES = 56 * 1024 * 1024
+MIB = 1024 * 1024
 F32 = jnp.float32
 BF16 = jnp.bfloat16
 
@@ -57,27 +57,27 @@
     return np.concatenate([high, high, low], axis=1)
 
 
-def plane_tables():
-    out = []
-    for kind in ("mass", "stiff", "slope"):
-        one = band_np(PAD, kind).T
-        both = np.zeros((LANES, LANES))
-        both[:PAD, :PAD] = one
-        both[PAD:, PAD:] = one
-        out.append(both)
-    return np.stack(out).astype(np.float32)
-
-
-def order_table():
-    table = np.zeros((512, 512))
-    for g in range(4):
-        for x16 in range(16):
-            for p in range(2):
-                for layer in range(4):
-                    row = g * 128 + x16 * 8 + p * 4 + layer
-                    col = ((p * 2 + layer // 2) * 2 + layer % 2) * 64 + 16 * g + x16
-                    table[row, col] = 1.0
-    return table
+def in_kernel_bands():
+    rows = lax.broadcasted_iota(jnp.int32, (LANES, LANES), 0)
+    cols = lax.broadcasted_iota(jnp.int32, (LANES, LANES), 1)
+    ahead = jnp.where(rows // PAD == cols // PAD, rows - cols, PAD)
+    apart = jnp.abs(ahead)
+    mass = jnp.zeros((LANES, LANES), F32)
+    stiff, slope = mass, mass
+    for d in range(4):
+        mass = jnp.where(apart == d, MASS_INT[d] / MASS_DEN, mass)
+        stiff = jnp.where(apart == d, STIFF_INT[d] / STIFF_DEN, stiff)
+        if d:
+            slope = jnp.where(ahead == d, SLOPE_INT[d - 1] / SLOPE_DEN, slope)
+            slope = jnp.where(ahead == -d, -SLOPE_INT[d - 1] / SLOPE_DEN, slope)
+    return mass, stiff, slope
+
+
+def layer_order():
+    rows = lax.broadcasted_iota(jnp.int32, (512, 512), 0)
+    cols = lax.broadcasted_iota(jnp.int32, (512, 512), 1)
+    x = (rows // 128) * 16 + (rows // 8) % 16
+    return jnp.where(cols == (rows % 8) * 64 + x, 1.0, 0.0).astype(BF16)
 
 
 def split(values):
@@ -157,11 +157,15 @@
     return jnp.concatenate(parts, axis=0)
 
 
-def send_layers(field, sizes_ref, partners_ref, order, own, to_before, to_after, low, high, me, groups, depth):
+def send_layers(field, sizes_ref, partners_ref, order, own, to_pair, to_ring, z_pair, z_ring, me_ref, groups, depth):
+    me = me_ref[0]
+    even_section = me_ref[1] % 2 == 0
     for c in range(COMPS):
         for d in range(HALO):
-            low[c, d] = field[pl.ds(c * PAD * depth + d, PAD, stride=depth), :]
-            high[c, d] = field[pl.ds(c * PAD * depth + depth - HALO + d, PAD, stride=depth), :]
+            low = field[pl.ds(c * PAD * depth + d, PAD, stride=depth), :]
+            high = field[pl.ds(c * PAD * depth + depth - HALO + d, PAD, stride=depth), :]
+            z_pair[c, d] = jnp.where(even_section, high, low)
+            z_ring[c, d] = jnp.where(even_section, low, high)
     outer, inner = row_at(field, 0, depth), row_at(field, 1, depth)
     own[0] = merge(outer, swap_halves(inner))
     own[FACES] = merge(swap_halves(outer), inner)
@@ -191,9 +195,10 @@
             at = (p * 2 + f) * LANES
             own[p * FACES + 2 + f] = sorted_layers[:, at : at + LANES]
     sources = send_sources(partners_ref, me, groups)
+    even = me % 2 == 0
     for slot in range(FACES):
-        to_before[slot] = own[sources[0][slot]]
-        to_after[slot] = own[sources[1][slot]]
+        to_pair[slot] = own[jnp.where(even, sources[1][slot], sources[0][slot])]
+        to_ring[slot] = own[jnp.where(even, sources[0][slot], sources[1][slot])]
 
 
 def active_lanes(sizes_ref):
@@ -201,23 +206,6 @@
     size_x = jnp.where(lane < PAD, sizes_ref[0, 0], sizes_ref[1, 0])
     size_y = jnp.where(lane < PAD, sizes_ref[0, 1], sizes_ref[1, 1])
     return size_x, (lane % PAD) < size_y
-
-
-def start_kernel(groups, depth, me_ref, sizes_ref, partners_ref, disp, order, field, own, to_before, to_after, low, high):
-    me = me_ref[0]
-    size_x, in_y = active_lanes(sizes_ref)
-    for k in range(PAD // 2):
-        keep_even = in_y & (2 * k < size_x)
-        keep_odd = in_y & (2 * k + 1 < size_x)
-        for c in range(COMPS):
-            one = disp[0, c, :, k * LANES : (k + 1) * LANES]
-            two = disp[1, c, :, k * LANES : (k + 1) * LANES]
-            even = merge(one, swap_halves(two))
-            odd = merge(swap_halves(one), two)
-            base = (c * PAD + 2 * k) * depth
-            field[base : base + depth, :] = jnp.where(keep_even, even, 0.0)
-            field[base + depth : base + 2 * depth, :] = jnp.where(keep_odd, odd, 0.0)
-    send_layers(field, sizes_ref, partners_ref, order, own, to_before, to_after, low, high, me, groups, depth)
 
 
 MASS, STIFF, SLOPE = 0, 1, 2
@@ -249,15 +237,16 @@
 OUT_SCALE = {STIFF: 1.0 / STIFF_DEN, MASS: 1.0 / MASS_DEN, SLOPE: 1.0 / SLOPE_DEN}
 
 
-def weights_kernel(lame_ref, me_ref, tables, weights):
-    first = me_ref[0] * 2
+def fill_weights(lame_ref, me, weights):
+    first = me * 2
     lane = lane_iota()
+    tables = in_kernel_bands()
 
     def per_lane(one, two):
         return jnp.where(lane < PAD, one, two)
 
-    mu = per_lane(lame_ref[first, 0], lame_ref[first + 1, 0])
-    grad = mu + per_lane(lame_ref[first, 1], lame_ref[first + 1, 1])
+    mu = per_lane(lame_ref[0, first], lame_ref[0, first + 1])
+    grad = mu + per_lane(lame_ref[1, first], lame_ref[1, first + 1])
     factors = {"mu": mu, "both": mu + grad, "grad": -grad}
     placed = set()
     for t, (sources, targets) in enumerate(TILES):
@@ -274,6 +263,42 @@
                 for part, piece in enumerate((block_high, block_high, block_low)):
                     at = part * 2 * LANES + i * LANES
                     weights[t, at : at + LANES, cols] = piece
+
+
+def start_kernel(
+    groups, depth, me_ref, sizes_any, partners_any, lame_any, disp_any,
+    field, own, to_pair, to_ring, z_pair, z_ring, weights, order,
+    sizes_ref, partners_ref, lame_ref, disp, sems,
+):
+    copies = []
+    for c in range(COMPS):
+        copies.append(pltpu.make_async_copy(disp_any.at[:, c], disp.at[:, c], sems.at[c]))
+    small = [
+        pltpu.make_async_copy(sizes_any, sizes_ref, sems.at[COMPS]),
+        pltpu.make_async_copy(partners_any, partners_ref, sems.at[COMPS + 1]),
+        pltpu.make_async_copy(lame_any, lame_ref, sems.at[COMPS + 2]),
+    ]
+    for copy in small + copies:
+        copy.start()
+    order[...] = layer_order()
+    for copy in small:
+        copy.wait()
+    me = me_ref[0]
+    fill_weights(lame_ref, me, weights)
+    size_x, in_y = active_lanes(sizes_ref)
+    for c in range(COMPS):
+        copies[c].wait()
+        for k in range(PAD // 2):
+            keep_even = in_y & (2 * k < size_x)
+            keep_odd = in_y & (2 * k + 1 < size_x)
+            one = disp[0, c, :, k * LANES : (k + 1) * LANES]
+            two = disp[1, c, :, k * LANES : (k + 1) * LANES]
+            even = merge(one, swap_halves(two))
+            odd = merge(swap_halves(one), two)
+            base = (c * PAD + 2 * k) * depth
+            field[base : base + depth, :] = jnp.where(keep_even, even, 0.0)
+            field[base + depth : base + 2 * depth, :] = jnp.where(keep_odd, odd, 0.0)
+    send_layers(field, sizes_ref, partners_ref, order, own, to_pair, to_ring, z_pair, z_ring, me_ref, groups, depth)
 
 
 def plane_sums(fields, weights):
@@ -391,29 +416,30 @@
     lame_ref,
     volume,
     own,
-    from_before,
-    from_after,
-    z_before,
-    z_after,
+    from_pair,
+    from_ring,
+    z_pair,
+    z_ring,
     transfer,
     weights,
     order,
-    order_back,
-    result,
+    result_any,
     *rest,
 ):
     if last:
-        field, edge = rest
+        field, edge, result, sems = rest
     else:
-        field, own_next, to_before, to_after, low, high, edge = rest
+        field, *sends, edge, result, sems = rest
     me = me_ref[0]
+    pair_side = 1 - me % 2
+    even_section = me_ref[1] % 2 == 0
     sides, slots = receive_slots(partners_ref, me, groups)
     terms = []
     for p in range(2):
         for f in range(FACES):
             k = p * FACES + f
-            far = jnp.where(sides[k] == 0, from_before[slots[k]], from_after[slots[k]])
-            mu_face = 0.5 * (lame_ref[me * 2 + p, 0] + lame_ref[partners_ref[p, f] // FACES, 0])
+            far = jnp.where(sides[k] == pair_side, from_pair[slots[k]], from_ring[slots[k]])
+            mu_face = 0.5 * (lame_ref[0, me * 2 + p] + lame_ref[0, partners_ref[p, f] // FACES])
             mat = transfer[p, f]
             zero = jnp.zeros((PAD, PAD), F32)
             both = jnp.concatenate(
@@ -431,7 +457,12 @@
     per = COMPS * depth
     stacked = jnp.concatenate([swap_halves(terms[p * FACES + 2 + f]) for p in range(2) for f in range(2)], axis=1)
     term_high, term_low = split(stacked)
-    placed = dot(jnp.concatenate([term_high, term_low], axis=0), order_back[...])
+    placed = lax.dot_general(
+        jnp.concatenate([term_high, term_low], axis=0),
+        order[...],
+        (((1,), (1,)), ((), ())),
+        preferred_element_type=F32,
+    )
     placed = placed[:per] + placed[per:]
     placed = jnp.concatenate([placed[:, g * LANES : (g + 1) * LANES] for g in range(4)], axis=0)
     placed_parts = jnp.concatenate(split(placed), axis=1)
@@ -469,7 +500,9 @@
     add_row(sizes_ref[1, 0] - 2, merge(zero, swap_halves(two)))
     fields = {}
     for c in range(COMPS):
-        banded = depth_edges([z_before[c, d] for d in range(HALO)], [z_after[c, d] for d in range(HALO)])
+        before = [jnp.where(even_section, z_ring[c, d], z_pair[c, d]) for d in range(HALO)]
+        after = [jnp.where(even_section, z_pair[c, d], z_ring[c, d]) for d in range(HALO)]
+        banded = depth_edges(before, after)
         for kind in range(3):
             fields[(c, kind)] = split(banded[kind])
     sums = plane_sums(fields, weights)
@@ -479,6 +512,8 @@
             edge[base : base + 8, :] = jnp.zeros((8, LANES), F32)
             edge[base + 8 + PAD : base + EDGE_ROWS, :] = jnp.zeros((8, LANES), F32)
             edge[base + 8 : base + 8 + PAD, :] = value[z * PAD : (z + 1) * PAD]
+    size_x, in_y = active_lanes(sizes_ref)
+    copies = []
     for c in range(COMPS):
         for z in range(2 * HALO):
 
@@ -489,11 +524,9 @@
             plane = z if z < HALO else depth - 2 * HALO + z
             rows = pl.ds(c * PAD * depth + plane, PAD, stride=depth)
             field[rows, :] += band_x(at(STIFF), at(MASS), at(SLOPE))
-    size_x, in_y = active_lanes(sizes_ref)
-    for k in range(PAD // 2):
-        keep_even = in_y & (2 * k < size_x)
-        keep_odd = in_y & (2 * k + 1 < size_x)
-        for c in range(COMPS):
+        for k in range(PAD // 2):
+            keep_even = in_y & (2 * k < size_x)
+            keep_odd = in_y & (2 * k + 1 < size_x)
             base = (c * PAD + 2 * k) * depth
             even = jnp.where(keep_even, field[base : base + depth, :], 0.0)
             odd = jnp.where(keep_odd, field[base + depth : base + 2 * depth, :], 0.0)
@@ -502,28 +535,38 @@
                 field[base + depth : base + 2 * depth, :] = odd
             result[0, c, :, k * LANES : (k + 1) * LANES] = merge(even, swap_halves(odd))
             result[1, c, :, k * LANES : (k + 1) * LANES] = merge(swap_halves(even), odd)
+        copies.append(pltpu.make_async_copy(result.at[:, c], result_any.at[:, c], sems.at[c]))
+        copies[-1].start()
     if not last:
-        send_layers(
-            field, sizes_ref, partners_ref, order, own_next, to_before, to_after, low, high, me, groups, depth
-        )
+        send_layers(field, sizes_ref, partners_ref, order, *sends, me_ref, groups, depth)
+    for copy in copies:
+        copy.wait()
 
 
 def shards(displacement, lame_params, patch_sizes, partners, transfer):
     depth = displacement.shape[2]
     groups = lax.axis_size("patch")
     sections = lax.axis_size("sect")
-    me = lax.axis_index("patch").astype(jnp.int32).reshape(1)
+    me = jnp.stack([lax.axis_index("patch"), lax.axis_index("sect")]).astype(jnp.int32)
     rows = COMPS * PAD * depth
     per = COMPS * depth
     smem = pl.BlockSpec(memory_space=pltpu.SMEM)
     vmem = pl.BlockSpec(memory_space=pltpu.VMEM)
-    params = pltpu.CompilerParams(vmem_limit_bytes=VMEM_BYTES)
+    away = pl.BlockSpec(memory_space=pl.ANY)
     z_table = jnp.asarray(depth_table(depth))
-    order = jnp.asarray(order_table().astype(ml_dtypes.bfloat16))
-    order_back = jnp.asarray(order_table().T.astype(ml_dtypes.bfloat16))
+    lame = lame_params.T
 
     def shape(*dims, dtype=F32):
-        return jax.ShapeDtypeStruct(dims, dtype)
+        return pltpu.VMEM(dims, dtype)
+
+    def near(values):
+        return pltpu.with_memory_space_constraint(values, pltpu.VMEM)
+
+    def far(values):
+        return pltpu.with_memory_space_constraint(values, pltpu.HBM)
+
+    def params(mib):
+        return pltpu.CompilerParams(vmem_limit_bytes=mib * MIB)
 
     field_shape = shape(rows, LANES)
     layer_shapes = (
@@ -534,33 +577,34 @@
         shape(COMPS, HALO, PAD, LANES),
     )
 
+    def both_ways(pairs):
+        return pairs + [(j, i) for i, j in pairs]
+
     def exchange(layers):
-        own, to_before, to_after, low, high = layers
-        forward = [(i, (i + 1) % groups) for i in range(groups)]
-        backward = [((i + 1) % groups, i) for i in range(groups)]
-        from_before = lax.ppermute(to_after, "patch", forward)
-        from_after = lax.ppermute(to_before, "patch", backward)
-        z_before = lax.ppermute(high, "sect", [(i, i + 1) for i in range(sections - 1)])
-        z_after = lax.ppermute(low, "sect", [(i + 1, i) for i in range(sections - 1)])
-        return own, from_before, from_after, z_before, z_after
-
-    weights = pl.pallas_call(
-        weights_kernel,
-        out_shape=shape(len(TILES), 6 * LANES, 2 * LANES, dtype=BF16),
-        in_specs=[smem, smem, vmem],
-        out_specs=vmem,
-        compiler_params=params,
-        name="plane_weights",
-    )(lame_params, me, jnp.asarray(plane_tables()))
-
-    field, *layers = pl.pallas_call(
+        own, to_pair, to_ring, z_pair, z_ring = layers
+        z_pair = lax.ppermute(z_pair, "sect", both_ways([(i, i + 1) for i in range(0, sections - 1, 2)]))
+        z_ring = lax.ppermute(z_ring, "sect", both_ways([(i, i + 1) for i in range(1, sections - 1, 2)]))
+        from_pair = lax.ppermute(to_pair, "patch", both_ways([(i, i + 1) for i in range(0, groups, 2)]))
+        from_ring = lax.ppermute(to_ring, "patch", both_ways([(i, (i + 1) % groups) for i in range(1, groups, 2)]))
+        return own, from_pair, from_ring, z_pair, z_ring
+
+    field, *layers, weights, order = pl.pallas_call(
         functools.partial(start_kernel, groups, depth),
-        out_shape=(field_shape,) + layer_shapes,
-        in_specs=[smem, smem, smem, vmem, vmem],
-        out_specs=(vmem,) * 6,
-        compiler_params=params,
+        out_shape=(field_shape,)
+        + layer_shapes
+        + (shape(len(TILES), 6 * LANES, 2 * LANES, dtype=BF16), shape(512, 512, dtype=BF16)),
+        in_specs=[smem] + [away] * 4,
+        out_specs=(vmem,) * 8,
+        scratch_shapes=[
+            pltpu.SMEM(patch_sizes.shape, jnp.int32),
+            pltpu.SMEM(partners.shape, jnp.int32),
+            pltpu.SMEM(lame.shape, F32),
+            pltpu.VMEM(displacement.shape, F32),
+            pltpu.SemaphoreType.DMA((COMPS + 3,)),
+        ],
+        compiler_params=params(24),
         name="start_layers",
-    )(me, patch_sizes, partners, displacement, order)
+    )(me, far(patch_sizes), far(partners), far(lame), far(displacement))
 
     def volume(values):
         return pl.pallas_call(
@@ -569,14 +613,18 @@
             in_specs=[vmem] * 3,
             out_specs=vmem,
             scratch_shapes=[pltpu.VMEM((9, PAD + 6, depth, LANES), F32)],
-            compiler_params=params,
+            compiler_params=params(28),
             cost_estimate=pl.CostEstimate(flops=10**10, bytes_accessed=8 * 10**6, transcendentals=0),
             name="volume_terms",
-        )(values, z_table, weights)
+        )(near(values), z_table, near(weights))
 
     def finish(volume_part, exchanged, last):
-        scratch = [pltpu.VMEM((9 * 2 * HALO * EDGE_ROWS, LANES), F32)]
-        out_shape = (shape(*displacement.shape),)
+        scratch = [
+            pltpu.VMEM((9 * 2 * HALO * EDGE_ROWS, LANES), F32),
+            pltpu.VMEM(displacement.shape, F32),
+            pltpu.SemaphoreType.DMA((COMPS,)),
+        ]
+        out_shape = (jax.ShapeDtypeStruct(displacement.shape, F32),)
         if last:
             scratch = [pltpu.VMEM((rows, LANES), F32)] + scratch
         else:
@@ -584,12 +632,22 @@
         return pl.pallas_call(
             functools.partial(finish_kernel, groups, depth, last),
             out_shape=out_shape,
-            in_specs=[smem] * 4 + [vmem] * 10,
-            out_specs=(vmem,) * len(out_shape),
+            in_specs=[smem] * 4 + [vmem] * 9,
+            out_specs=(away,) + (vmem,) * (len(out_shape) - 1),
             scratch_shapes=scratch,
-            compiler_params=params,
+            compiler_params=params(28),
             name="finish_last" if last else "finish_first",
-        )(me, patch_sizes, partners, lame_params, volume_part, *exchanged, transfer, weights, order, order_back)
+        )(
+            me,
+            far(patch_sizes),
+            far(partners),
+            far(lame),
+            near(volume_part),
+            *[near(part) for part in exchanged],
+            transfer,
+            near(weights),
+            near(order),
+        )
 
     first_apply, field, *next_layers = finish(volume(field), exchange(layers), False)
     (second_apply,) = finish(volume(field), exchange(next_layers), True)

time: 82.8 us -> 54.3 us (0.66)
  Pallas kernels: 57.6 us -> 38.7 us
  starting transfers between devices: 21.6 us -> 14.3 us
  local copies, waits for them, and re-layouts: 2.5 us -> 0.01 us
    pallas_call x2, Pallas kernels: 28.1 us -> 19.7 us  [volume(): pl.pallas_call(functools.partial(volume_kernel, depth), out_shape=field_s...]
    ppermute x8, starting transfers between devices: 21.6 us -> 14.3 us  [the longest x2 6.27 us: exchange(): lax.ppermute(z_ring, 'sect', both_ways([(i, i + 1) for i in range(1, sect...]
    pallas_call x2, Pallas kernels: 21.2 us -> 14.6 us  [finish(): pl.pallas_call(functools.partial(finish_kernel, groups, depth, last), out...]
    pallas_call x1 -> x0, Pallas kernels: 2.7 us -> none  [shards(): pl.pallas_call(weights_kernel, out_shape=shape(len(TILES), 6 * LANES, 2 *...]
    unnamed x19 -> x4, local copies, waits for them, and re-layouts: 2.5 us -> 0.01 us
    pallas_call x1, Pallas kernels: 5.67 us -> 4.42 us  [shards(): pl.pallas_call(functools.partial(start_kernel, groups, depth), out_shape=...]
  transfers between devices with their start and end apart: 8 -> 8, of which waited for: 0 -> 0; matrix products, arithmetic and copies ran while one was open for 1% -> 0% of each run, Pallas kernels for 37% -> 36%
where the time goes in v1:
time: 54.3 us; the launch traced here: 54.1 us
  Pallas kernels  38.7 us (71%)
  starting transfers between devices  14.3 us (26%)
  between operations  0.95 us (2%)
    pallas_call x2, Pallas kernels, volume(): pl.pallas_call(functools.partial(volume_kernel, depth), out_shape=field_s...  19.7 us
    pallas_call x2, Pallas kernels, finish(): pl.pallas_call(functools.partial(finish_kernel, groups, depth, last), out...  14.6 us
    ppermute x2, starting transfers between devices, exchange(): lax.ppermute(z_ring, 'sect', both_ways([(i, i + 1) for i in range(1, sect...  6.27 us
    ppermute x2, starting transfers between devices, exchange(): lax.ppermute(to_ring, 'patch', both_ways([(i, (i + 1) % groups) for i in...  4.64 us
    pallas_call x1, Pallas kernels, shards(): pl.pallas_call(functools.partial(start_kernel, groups, depth), out_shape=...  4.42 us
    ppermute x2, starting transfers between devices, exchange(): lax.ppermute(to_pair, 'patch', both_ways([(i, i + 1) for i in range(0, gr...  2.18 us
    ppermute x2, starting transfers between devices, exchange(): lax.ppermute(z_pair, 'sect', both_ways([(i, i + 1) for i in range(0, sect...  1.24 us
  transfers between devices with their start and end apart: 8, of which 0 were waited for; matrix products, arithmetic and copies ran while one was open for 0% of the time, Pallas kernels for 36%

profile of v1, /device:TPU:1, one launch (start us, length us, event | category | flops | bytes accessed | tf_op | source)
XLA Modules:
  0.0 54.1 jit_solution(15261586897375825228)
XLA Ops:
  0.6 0.0 copy-start.1
  0.6 0.1 pad_add_fusion.me_ref
  0.7 4.4 %start_layers.1 = (f32[6144,128]{1,0:T(8,128)S(1)}, f32[8,96,128]{2,1,0:T(8,128)S(1)}, f32[4,96,128]{2,1,0:T(8,128)S(1)}, f32[4,96,128]{2,1,0:T(8,128)S(1)}, f32...) custom-call(s32[2]{0:T(128)S(1)} %pad_add_fusion.me_ref, ...), custom_call_target="tpu_custom_call" | custom-call | tf_op jit(solution)/shard_map/start_layers/pallas_call | solution.py:591
  5.1 2.1 %collective-permute-start = (f32[4,96,128]{2,1,0:T(8,128)S(1)}, f32[4,96,128]{2,1,0:T(8,128)S(1)}, u32[]{:S(2)}, u32[]{:S(2)}) collective-permute-start(f32[4,96,128]{2,1,0:T(8,128)S(1)} %get-tuple-element.20), channel_id=1, source_target_pairs={{0,4},{8,12},{16,20},{24,28},{4,0},{12,8},{20,16},{28,24},{1,5},{9... | collective-permute-start | bytes 589832 | tf_op jit(solution)/shard_map/ppermute | solution.py:587
  7.3 3.3 %collective-permute-start.1 = (f32[4,96,128]{2,1,0:T(8,128)S(1)}, f32[4,96,128]{2,1,0:T(8,128)S(1)}, u32[]{:S(2)}, u32[]{:S(2)}) collective-permute-start(f32[4,96,128]{2,1,0:T(8,128)S(1)} %get-tuple-element.21), channel_id=1, source_target_pairs={{4,8},{12,16},{20,24},{28,0},{8,4},{16,12},{24,20},{0,28},{5,9},{1... | collective-permute-start | bytes 589832 | tf_op jit(solution)/shard_map/ppermute | solution.py:588
  10.5 1.2 %collective-permute-start.2 = (f32[3,3,64,128]{3,2,1,0:T(8,128)S(1)}, f32[3,3,64,128]{3,2,1,0:T(8,128)S(1)}, u32[]{:S(2)}, u32[]{:S(2)}) collective-permute-start(f32[3,3,64,128]{3,2,1,0:T(8,128)S(1)} %get-tuple-element.22), channel_id=1, source_target_pairs={{0,1},{2,3},{1,0},{3,2},{4,5},{6,7},{5,4},{7,6},{8,9},{10,11},{9,8... | collective-permute-start | bytes 884744 | tf_op jit(solution)/shard_map/ppermute | solution.py:585
  11.8 3.0 %collective-permute-start.3 = (f32[3,3,64,128]{3,2,1,0:T(8,128)S(1)}, f32[3,3,64,128]{3,2,1,0:T(8,128)S(1)}, u32[]{:S(2)}, u32[]{:S(2)}) collective-permute-start(f32[3,3,64,128]{3,2,1,0:T(8,128)S(1)} %get-tuple-element.23), channel_id=1, source_target_pairs={{1,2},{2,1},{5,6},{6,5},{9,10},{10,9},{13,14},{14,13},{17,18},{18,... | collective-permute-start | bytes 884744 | tf_op jit(solution)/shard_map/ppermute | solution.py:586
  14.8 0.0 copy-done.1
  14.8 0.0 copy-start
  14.8 9.8 %volume_terms.2.volume = f32[6144,128]{1,0:T(8,128)S(1)} custom-call(f32[6144,128]{1,0:T(8,128)S(1)} %get-tuple-element.17.field, bf16[96,96]{1,0:T(8,128)(2,1)S(1)} %copy-done.1, bf16[6,768,256]{2,1,0:T(8,128)(2,1)S(1)} %get-tuple-element.18.weights), custom_call_target="tpu_custom_call" | custom-call | flops 10000000000 | bytes 8000000 | tf_op jit(solution)/shard_map/volume_terms/pallas_call | solution.py:610
  24.7 0.0 collective-permute-done.from_pair
  24.7 0.0 collective-permute-done.1.from_ring
  24.7 0.0 collective-permute-done.2.z_pair
  24.7 0.0 collective-permute-done.3.z_ring
  24.7 0.0 copy-done
  24.7 8.1 %finish_first.1 = (f32[2,3,32,4096]{3,2,1,0:T(8,128)}, f32[6144,128]{1,0:T(8,128)S(1)}, f32[8,96,128]{2,1,0:T(8,128)S(1)}, f32[4,96,128]{2,1,0:T(8,128)S(1)}, f3...) custom-call(s32[2]{0:T(128)S(1)} %pad_add_fusion.me_ref, s32[2,2]{1,0:T(2,128)} %sizes_ref.3, ...), custom_call_target="tpu_custom_call" | custom-call | tf_op jit(solution)/shard_map/finish_first/pallas_call | solution.py:632
  32.9 0.1 collective-permute-start.4
  32.9 1.3 %collective-permute-start.5 = (f32[4,96,128]{2,1,0:T(8,128)S(1)}, f32[4,96,128]{2,1,0:T(8,128)S(1)}, u32[]{:S(2)}, u32[]{:S(2)}) collective-permute-start(f32[4,96,128]{2,1,0:T(8,128)S(1)} %get-tuple-element.29), channel_id=1, source_target_pairs={{4,8},{12,16},{20,24},{28,0},{8,4},{16,12},{24,20},{0,28},{5,9},{1... | collective-permute-start | bytes 589832 | tf_op jit(solution)/shard_map/ppermute | solution.py:588
  34.3 0.0 collective-permute-start.6
  34.3 3.2 %collective-permute-start.7 = (f32[3,3,64,128]{3,2,1,0:T(8,128)S(1)}, f32[3,3,64,128]{3,2,1,0:T(8,128)S(1)}, u32[]{:S(2)}, u32[]{:S(2)}) collective-permute-start(f32[3,3,64,128]{3,2,1,0:T(8,128)S(1)} %get-tuple-element.31), channel_id=1, source_target_pairs={{1,2},{2,1},{5,6},{6,5},{9,10},{10,9},{13,14},{14,13},{17,18},{18,... | collective-permute-start | bytes 884744 | tf_op jit(solution)/shard_map/ppermute | solution.py:586
  37.6 9.8 %volume_terms.3.volume = f32[6144,128]{1,0:T(8,128)S(1)} custom-call(f32[6144,128]{1,0:T(8,128)S(1)} %get-tuple-element.26.field, bf16[96,96]{1,0:T(8,128)(2,1)S(1)} %copy-done.1, bf16[6,768,256]{2,1,0:T(8,128)(2,1)S(1)} %get-tuple-element.18.weights), custom_call_target="tpu_custom_call" | custom-call | flops 10000000000 | bytes 8000000 | tf_op jit(solution)/shard_map/volume_terms/pallas_call | solution.py:610
  47.4 0.0 collective-permute-done.4.from_pair
  47.4 0.0 collective-permute-done.5.from_ring
  47.4 0.0 collective-permute-done.6.z_pair
  47.4 0.0 collective-permute-done.7.z_ring
  47.4 6.5 %finish_last.1 = f32[2,3,32,4096]{3,2,1,0:T(8,128)} custom-call(s32[2]{0:T(128)S(1)} %pad_add_fusion.me_ref, s32[2,2]{1,0:T(2,128)} %sizes_ref.3, s32[2,4]{1,0:T(2,128)} %partners_ref.3, f32[2,16]{1,0:T(2,128)} %bitcast.5, f32[6144,128]{1,0:T(8,128)S(1)} %volume_terms.3.volume, f32[8,96,128]{2,1,0:T(8,128)S(1)} %get-tuple-element.27.own, ...), custom_call_target="tpu_custom_call" | custom-call | tf_op jit(solution)/shard_map/finish_last/pallas_call | solution.py:632
Async XLA Ops:
  0.6 14.2 %copy-start.1 = (bf16[96,96]{1,0:T(8,128)(2,1)S(1)}, bf16[96,96]{1,0:T(8,128)(2,1)}, u32[]{:S(2)}) copy-start(bf16[96,96]{1,0:T(8,128)(2,1)} %constant.11.clone.z_table) | copy-start | bytes 55300
  5.1 19.5 %collective-permute-start = (f32[4,96,128]{2,1,0:T(8,128)S(1)}, f32[4,96,128]{2,1,0:T(8,128)S(1)}, u32[]{:S(2)}, u32[]{:S(2)}) collective-permute-start(f32[4,96,128]{2,1,0:T(8,128)S(1)} %get-tuple-element.20), channel_id=1, source_target_pairs={{0,4},{8,12},{16,20},{24,28},{4,0},{12,8},{20,16},{28,24},{1,5},{9... | collective-permute-start | bytes 589832 | tf_op jit(solution)/shard_map/ppermute | solution.py:587
  7.3 17.4 %collective-permute-start.1 = (f32[4,96,128]{2,1,0:T(8,128)S(1)}, f32[4,96,128]{2,1,0:T(8,128)S(1)}, u32[]{:S(2)}, u32[]{:S(2)}) collective-permute-start(f32[4,96,128]{2,1,0:T(8,128)S(1)} %get-tuple-element.21), channel_id=1, source_target_pairs={{4,8},{12,16},{20,24},{28,0},{8,4},{16,12},{24,20},{0,28},{5,9},{1... | collective-permute-start | bytes 589832 | tf_op jit(solution)/shard_map/ppermute | solution.py:588
  10.5 14.2 %collective-permute-start.2 = (f32[3,3,64,128]{3,2,1,0:T(8,128)S(1)}, f32[3,3,64,128]{3,2,1,0:T(8,128)S(1)}, u32[]{:S(2)}, u32[]{:S(2)}) collective-permute-start(f32[3,3,64,128]{3,2,1,0:T(8,128)S(1)} %get-tuple-element.22), channel_id=1, source_target_pairs={{0,1},{2,3},{1,0},{3,2},{4,5},{6,7},{5,4},{7,6},{8,9},{10,11},{9,8... | collective-permute-start | bytes 884744 | tf_op jit(solution)/shard_map/ppermute | solution.py:585
  11.8 12.9 %collective-permute-start.3 = (f32[3,3,64,128]{3,2,1,0:T(8,128)S(1)}, f32[3,3,64,128]{3,2,1,0:T(8,128)S(1)}, u32[]{:S(2)}, u32[]{:S(2)}) collective-permute-start(f32[3,3,64,128]{3,2,1,0:T(8,128)S(1)} %get-tuple-element.23), channel_id=1, source_target_pairs={{1,2},{2,1},{5,6},{6,5},{9,10},{10,9},{13,14},{14,13},{17,18},{18,... | collective-permute-start | bytes 884744 | tf_op jit(solution)/shard_map/ppermute | solution.py:586
  14.8 9.9 %copy-start = (f32[2,4,64,64]{3,2,1,0:T(8,128)S(1)}, f32[2,4,64,64]{3,2,1,0:T(8,128)}, u32[]{:S(2)}) copy-start(f32[2,4,64,64]{3,2,1,0:T(8,128)} %transfer.3) | copy-start | bytes 393220
  32.9 14.5 %collective-permute-start.4 = (f32[4,96,128]{2,1,0:T(8,128)S(1)}, f32[4,96,128]{2,1,0:T(8,128)S(1)}, u32[]{:S(2)}, u32[]{:S(2)}) collective-permute-start(f32[4,96,128]{2,1,0:T(8,128)S(1)} %get-tuple-element.28), channel_id=1, source_target_pairs={{0,4},{8,12},{16,20},{24,28},{4,0},{12,8},{20,16},{28,24},{1,5},{9... | collective-permute-start | bytes 589832 | tf_op jit(solution)/shard_map/ppermute | solution.py:587
  32.9 14.5 %collective-permute-start.5 = (f32[4,96,128]{2,1,0:T(8,128)S(1)}, f32[4,96,128]{2,1,0:T(8,128)S(1)}, u32[]{:S(2)}, u32[]{:S(2)}) collective-permute-start(f32[4,96,128]{2,1,0:T(8,128)S(1)} %get-tuple-element.29), channel_id=1, source_target_pairs={{4,8},{12,16},{20,24},{28,0},{8,4},{16,12},{24,20},{0,28},{5,9},{1... | collective-permute-start | bytes 589832 | tf_op jit(solution)/shard_map/ppermute | solution.py:588
  34.3 13.1 %collective-permute-start.6 = (f32[3,3,64,128]{3,2,1,0:T(8,128)S(1)}, f32[3,3,64,128]{3,2,1,0:T(8,128)S(1)}, u32[]{:S(2)}, u32[]{:S(2)}) collective-permute-start(f32[3,3,64,128]{3,2,1,0:T(8,128)S(1)} %get-tuple-element.30), channel_id=1, source_target_pairs={{0,1},{2,3},{1,0},{3,2},{4,5},{6,7},{5,4},{7,6},{8,9},{10,11},{9,8... | collective-permute-start | bytes 884744 | tf_op jit(solution)/shard_map/ppermute | solution.py:585
  34.3 13.1 %collective-permute-start.7 = (f32[3,3,64,128]{3,2,1,0:T(8,128)S(1)}, f32[3,3,64,128]{3,2,1,0:T(8,128)S(1)}, u32[]{:S(2)}, u32[]{:S(2)}) collective-permute-start(f32[3,3,64,128]{3,2,1,0:T(8,128)S(1)} %get-tuple-element.31), channel_id=1, source_target_pairs={{1,2},{2,1},{5,6},{6,5},{9,10},{10,9},{13,14},{14,13},{17,18},{18,... | collective-permute-start | bytes 884744 | tf_op jit(solution)/shard_map/ppermute | solution.py:586

commit v2 on v1

--- a/solution.py
+++ b/solution.py
@@ -157,9 +157,9 @@
     return jnp.concatenate(parts, axis=0)
 
 
-def send_layers(field, sizes_ref, partners_ref, order, own, to_pair, to_ring, z_pair, z_ring, me_ref, groups, depth):
-    me = me_ref[0]
-    even_section = me_ref[1] % 2 == 0
+def send_layers(field, sizes_ref, partners_ref, order, own, to_pair, to_ring, z_pair, z_ring, groups, depth):
+    me = lax.axis_index("patch")
+    even_section = lax.axis_index("sect") % 2 == 0
     for c in range(COMPS):
         for d in range(HALO):
             low = field[pl.ds(c * PAD * depth + d, PAD, stride=depth), :]
@@ -266,7 +266,7 @@
 
 
 def start_kernel(
-    groups, depth, me_ref, sizes_any, partners_any, lame_any, disp_any,
+    groups, depth, sizes_any, partners_any, lame_any, disp_any,
     field, own, to_pair, to_ring, z_pair, z_ring, weights, order,
     sizes_ref, partners_ref, lame_ref, disp, sems,
 ):
@@ -283,8 +283,7 @@
     order[...] = layer_order()
     for copy in small:
         copy.wait()
-    me = me_ref[0]
-    fill_weights(lame_ref, me, weights)
+    fill_weights(lame_ref, lax.axis_index("patch"), weights)
     size_x, in_y = active_lanes(sizes_ref)
     for c in range(COMPS):
         copies[c].wait()
@@ -298,7 +297,7 @@
             base = (c * PAD + 2 * k) * depth
             field[base : base + depth, :] = jnp.where(keep_even, even, 0.0)
             field[base + depth : base + 2 * depth, :] = jnp.where(keep_odd, odd, 0.0)
-    send_layers(field, sizes_ref, partners_ref, order, own, to_pair, to_ring, z_pair, z_ring, me_ref, groups, depth)
+    send_layers(field, sizes_ref, partners_ref, order, own, to_pair, to_ring, z_pair, z_ring, groups, depth)
 
 
 def plane_sums(fields, weights):
@@ -334,13 +333,13 @@
         for x in (0, 1, 2, PAD + 3, PAD + 4, PAD + 5):
             sums_ref[i, x] = jnp.zeros((depth, LANES), F32)
 
-    def in_plane(block, carry):
-        x0 = block * XBLOCK
+    def along_z(x0):
         fields = {}
         for c in range(COMPS):
-            start = pl.multiple_of((c * PAD + x0) * depth, XBLOCK * depth)
-            rows = field[pl.ds(start, XBLOCK * depth), :]
-            wide = jnp.concatenate([rows[j * depth : (j + 1) * depth] for j in range(XBLOCK)], axis=1)
+            start = (c * PAD + x0) * depth
+            wide = jnp.concatenate(
+                [field[start + j * depth : start + (j + 1) * depth, :] for j in range(XBLOCK)], axis=1
+            )
             high, low = split(wide)
             banded = dot(z_table[...], jnp.concatenate([high, low, high], axis=0))
             parts = split(banded)
@@ -355,29 +354,32 @@
                     )
                     for part in parts
                 )
-        sums = plane_sums(fields, weights)
-        for (c, kind), value in sums.items():
-            sums_ref[c * 3 + kind, pl.ds(x0 + 3, XBLOCK)] = value.reshape(XBLOCK, depth, LANES)
-        return carry
-
-    lax.fori_loop(0, PAD // XBLOCK, in_plane, 0)
-
-    def along_x(step, carry):
-        x0 = (step // (depth // 8)) * XROWS
-        z0 = pl.multiple_of((step % (depth // 8)) * 8, 8)
-        for c in range(COMPS):
-            held = [sums_ref[c * 3 + kind, pl.ds(x0, XROWS + 6), pl.ds(z0, 8), :] for kind in range(3)]
-
-            def at(kind):
-                return lambda d: held[kind][3 + d : 3 + d + XROWS]
-
-            result = band_x(at(STIFF), at(MASS), at(SLOPE))
-            for j in range(XROWS):
-                start = pl.multiple_of((c * PAD + x0 + j) * depth + z0, 8)
-                out[pl.ds(start, 8), :] = result[j]
-        return carry
-
-    lax.fori_loop(0, (PAD // XROWS) * (depth // 8), along_x, 0)
+        return fields
+
+    def along_x(x0, c, z0):
+        held = [sums_ref[c * 3 + kind, x0 : x0 + XROWS + 6, z0 : z0 + 8, :] for kind in range(3)]
+
+        def at(kind):
+            return lambda d: held[kind][3 + d : 3 + d + XROWS]
+
+        result = band_x(at(STIFF), at(MASS), at(SLOPE))
+        for j in range(XROWS):
+            start = (c * PAD + x0 + j) * depth + z0
+            out[start : start + 8, :] = result[j]
+
+    done = 0
+    for block in range(PAD // XBLOCK + 1):
+        x0 = block * XBLOCK
+        pieces = []
+        while done < PAD and (done + XROWS + 3 <= x0 or x0 == PAD):
+            pieces += [(done, c, z0) for c in range(COMPS) for z0 in range(0, depth, 8)]
+            done += XROWS
+        if x0 < PAD:
+            sums = plane_sums(along_z(x0), weights)
+            for (c, kind), value in sums.items():
+                sums_ref[c * 3 + kind, x0 + 3 : x0 + 3 + XBLOCK] = value.reshape(XBLOCK, depth, LANES)
+        for piece in pieces:
+            along_x(*piece)
 
 
 def depth_edges(before, after):
@@ -403,36 +405,44 @@
     return [jnp.concatenate(parts, axis=0) for parts in (mass, stiff, slope)]
 
 
-EDGE_ROWS = 80
+EDGE_X = PAD + 2 * HALO
 
 
 def finish_kernel(
-    groups,
-    depth,
-    last,
-    me_ref,
-    sizes_ref,
-    partners_ref,
-    lame_ref,
-    volume,
-    own,
-    from_pair,
-    from_ring,
-    z_pair,
-    z_ring,
-    transfer,
-    weights,
-    order,
-    result_any,
-    *rest,
+    groups, depth, last, sizes_any, partners_any, lame_any, volume, own, from_pair, from_ring, z_pair, z_ring,
+    transfer, weights, order, result_any, *rest,
 ):
     if last:
-        field, edge, result, sems = rest
+        field, edge, result, sizes_ref, partners_ref, lame_ref, sems = rest
     else:
-        field, *sends, edge, result, sems = rest
-    me = me_ref[0]
+        field, *sends, edge, result, sizes_ref, partners_ref, lame_ref, sems = rest
+    small = [
+        pltpu.make_async_copy(sizes_any, sizes_ref, sems.at[0]),
+        pltpu.make_async_copy(partners_any, partners_ref, sems.at[1]),
+        pltpu.make_async_copy(lame_any, lame_ref, sems.at[2]),
+    ]
+    for copy in small:
+        copy.start()
+    me = lax.axis_index("patch")
     pair_side = 1 - me % 2
-    even_section = me_ref[1] % 2 == 0
+    even_section = lax.axis_index("sect") % 2 == 0
+    fields = {}
+    for c in range(COMPS):
+        before = [jnp.where(even_section, z_ring[c, d], z_pair[c, d]) for d in range(HALO)]
+        after = [jnp.where(even_section, z_pair[c, d], z_ring[c, d]) for d in range(HALO)]
+        banded = depth_edges(before, after)
+        for kind in range(3):
+            fields[(c, kind)] = split(banded[kind])
+    sums = plane_sums(fields, weights)
+    for (c, kind), value in sums.items():
+        base = (c * 3 + kind) * EDGE_X * 8
+        edge[base : base + HALO * 8, :] = jnp.zeros((HALO * 8, LANES), F32)
+        edge[base + (HALO + PAD) * 8 : base + EDGE_X * 8, :] = jnp.zeros((HALO * 8, LANES), F32)
+        for z in range(2 * HALO):
+            slot = z if z < HALO else z + 2
+            edge[pl.ds(base + HALO * 8 + slot, PAD, stride=8), :] = value[z * PAD : (z + 1) * PAD]
+    for copy in small:
+        copy.wait()
     sides, slots = receive_slots(partners_ref, me, groups)
     terms = []
     for p in range(2):
@@ -498,47 +508,50 @@
     add_row(sizes_ref[0, 0] - 2, merge(one, zero))
     add_row(sizes_ref[1, 0] - 1, merge(zero, two))
     add_row(sizes_ref[1, 0] - 2, merge(zero, swap_halves(two)))
-    fields = {}
-    for c in range(COMPS):
-        before = [jnp.where(even_section, z_ring[c, d], z_pair[c, d]) for d in range(HALO)]
-        after = [jnp.where(even_section, z_pair[c, d], z_ring[c, d]) for d in range(HALO)]
-        banded = depth_edges(before, after)
-        for kind in range(3):
-            fields[(c, kind)] = split(banded[kind])
-    sums = plane_sums(fields, weights)
-    for (c, kind), value in sums.items():
-        for z in range(2 * HALO):
-            base = ((c * 3 + kind) * 2 * HALO + z) * EDGE_ROWS
-            edge[base : base + 8, :] = jnp.zeros((8, LANES), F32)
-            edge[base + 8 + PAD : base + EDGE_ROWS, :] = jnp.zeros((8, LANES), F32)
-            edge[base + 8 : base + 8 + PAD, :] = value[z * PAD : (z + 1) * PAD]
     size_x, in_y = active_lanes(sizes_ref)
+    slot_rows = lax.broadcasted_iota(jnp.int32, (8, LANES), 0)
     copies = []
     for c in range(COMPS):
-        for z in range(2 * HALO):
+        for x0 in range(0, PAD, XROWS):
+            held = []
+            for kind in range(3):
+                base = ((c * 3 + kind) * EDGE_X + x0) * 8
+                held.append(edge[base : base + (XROWS + 2 * HALO) * 8, :].reshape(XROWS + 2 * HALO, 8, LANES))
 
             def at(kind):
-                base = ((c * 3 + kind) * 2 * HALO + z) * EDGE_ROWS + 8
-                return lambda d: edge[base + d : base + d + PAD, :]
-
-            plane = z if z < HALO else depth - 2 * HALO + z
-            rows = pl.ds(c * PAD * depth + plane, PAD, stride=depth)
-            field[rows, :] += band_x(at(STIFF), at(MASS), at(SLOPE))
-        for k in range(PAD // 2):
-            keep_even = in_y & (2 * k < size_x)
-            keep_odd = in_y & (2 * k + 1 < size_x)
-            base = (c * PAD + 2 * k) * depth
-            even = jnp.where(keep_even, field[base : base + depth, :], 0.0)
-            odd = jnp.where(keep_odd, field[base + depth : base + 2 * depth, :], 0.0)
-            if not last:
-                field[base : base + depth, :] = even
-                field[base + depth : base + 2 * depth, :] = odd
-            result[0, c, :, k * LANES : (k + 1) * LANES] = merge(even, swap_halves(odd))
-            result[1, c, :, k * LANES : (k + 1) * LANES] = merge(swap_halves(even), odd)
-        copies.append(pltpu.make_async_copy(result.at[:, c], result_any.at[:, c], sems.at[c]))
-        copies[-1].start()
+                return lambda d: held[kind][HALO + d : HALO + d + XROWS]
+
+            edges = band_x(at(STIFF), at(MASS), at(SLOPE))
+
+            def whole(x):
+                start = (c * PAD + x) * depth
+                edge_x = edges[x - x0]
+                value = jnp.concatenate(
+                    [
+                        field[start : start + 8, :] + jnp.where(slot_rows < HALO, edge_x, 0.0),
+                        field[start + 8 : start + depth - 8, :],
+                        field[start + depth - 8 : start + depth, :] + jnp.where(slot_rows >= 8 - HALO, edge_x, 0.0),
+                    ],
+                    axis=0,
+                )
+                value = jnp.where(in_y & (x < size_x), value, 0.0)
+                if not last:
+                    field[start : start + depth, :] = value
+                return value
+
+            for k in range(x0 // 2, (x0 + XROWS) // 2):
+                even, odd = whole(2 * k), whole(2 * k + 1)
+                result[0, c, :, k * LANES : (k + 1) * LANES] = merge(even, swap_halves(odd))
+                result[1, c, :, k * LANES : (k + 1) * LANES] = merge(swap_halves(even), odd)
+            if (x0 + XROWS) % (PAD // 2) == 0:
+                lanes = pl.ds((x0 + XROWS - PAD // 2) * PAD, PAD * PAD // 2)
+                copy = pltpu.make_async_copy(
+                    result.at[:, c, :, lanes], result_any.at[:, c, :, lanes], sems.at[3 + len(copies)]
+                )
+                copy.start()
+                copies.append(copy)
     if not last:
-        send_layers(field, sizes_ref, partners_ref, order, *sends, me_ref, groups, depth)
+        send_layers(field, sizes_ref, partners_ref, order, *sends, groups, depth)
     for copy in copies:
         copy.wait()
 
@@ -547,10 +560,8 @@
     depth = displacement.shape[2]
     groups = lax.axis_size("patch")
     sections = lax.axis_size("sect")
-    me = jnp.stack([lax.axis_index("patch"), lax.axis_index("sect")]).astype(jnp.int32)
     rows = COMPS * PAD * depth
     per = COMPS * depth
-    smem = pl.BlockSpec(memory_space=pltpu.SMEM)
     vmem = pl.BlockSpec(memory_space=pltpu.VMEM)
     away = pl.BlockSpec(memory_space=pl.ANY)
     z_table = jnp.asarray(depth_table(depth))
@@ -593,7 +604,7 @@
         out_shape=(field_shape,)
         + layer_shapes
         + (shape(len(TILES), 6 * LANES, 2 * LANES, dtype=BF16), shape(512, 512, dtype=BF16)),
-        in_specs=[smem] + [away] * 4,
+        in_specs=[away] * 4,
         out_specs=(vmem,) * 8,
         scratch_shapes=[
             pltpu.SMEM(patch_sizes.shape, jnp.int32),
@@ -604,7 +615,7 @@
         ],
         compiler_params=params(24),
         name="start_layers",
-    )(me, far(patch_sizes), far(partners), far(lame), far(displacement))
+    )(far(patch_sizes), far(partners), far(lame), far(displacement))
 
     def volume(values):
         return pl.pallas_call(
@@ -620,9 +631,12 @@
 
     def finish(volume_part, exchanged, last):
         scratch = [
-            pltpu.VMEM((9 * 2 * HALO * EDGE_ROWS, LANES), F32),
+            pltpu.VMEM((9 * EDGE_X * 8, LANES), F32),
             pltpu.VMEM(displacement.shape, F32),
-            pltpu.SemaphoreType.DMA((COMPS,)),
+            pltpu.SMEM(patch_sizes.shape, jnp.int32),
+            pltpu.SMEM(partners.shape, jnp.int32),
+            pltpu.SMEM(lame.shape, F32),
+            pltpu.SemaphoreType.DMA((3 + 2 * COMPS,)),
         ]
         out_shape = (jax.ShapeDtypeStruct(displacement.shape, F32),)
         if last:
@@ -632,13 +646,12 @@
         return pl.pallas_call(
             functools.partial(finish_kernel, groups, depth, last),
             out_shape=out_shape,
-            in_specs=[smem] * 4 + [vmem] * 9,
+            in_specs=[away] * 3 + [vmem] * 9,
             out_specs=(away,) + (vmem,) * (len(out_shape) - 1),
             scratch_shapes=scratch,
             compiler_params=params(28),
             name="finish_last" if last else "finish_first",
         )(
-            me,
             far(patch_sizes),
             far(partners),
             far(lame),

time: 54.3 us -> 46.4 us (0.85)
  Pallas kernels: 38.7 us -> 30.9 us
    pallas_call x2, Pallas kernels: 19.7 us -> 14.8 us  [volume(): pl.pallas_call(functools.partial(volume_kernel, depth), out_shape=field_s...]
    pallas_call x2, Pallas kernels: 14.6 us -> 12.4 us  [finish(): pl.pallas_call(functools.partial(finish_kernel, groups, depth, last), out...]
    pallas_call x1, Pallas kernels: 4.42 us -> 3.79 us  [shards(): pl.pallas_call(functools.partial(start_kernel, groups, depth), out_shape=...]
  transfers between devices with their start and end apart: 8 -> 8, of which waited for: 0 -> 0; matrix products, arithmetic and copies ran while one was open for 0% -> 0% of each run, Pallas kernels for 36% -> 32%
where the time goes in v2:
time: 46.4 us; the launch traced here: 46.2 us
  Pallas kernels  30.9 us (67%)
  starting transfers between devices  14.3 us (31%)
  between operations  0.96 us (2%)
    pallas_call x2, Pallas kernels, volume(): pl.pallas_call(functools.partial(volume_kernel, depth), out_shape=field_s...  14.8 us
    pallas_call x2, Pallas kernels, finish(): pl.pallas_call(functools.partial(finish_kernel, groups, depth, last), out...  12.4 us
    ppermute x2, starting transfers between devices, exchange(): lax.ppermute(z_ring, 'sect', both_ways([(i, i + 1) for i in range(1, sect...  6.27 us
    ppermute x2, starting transfers between devices, exchange(): lax.ppermute(to_ring, 'patch', both_ways([(i, (i + 1) % groups) for i in...  4.62 us
    pallas_call x1, Pallas kernels, shards(): pl.pallas_call(functools.partial(start_kernel, groups, depth), out_shape=...  3.79 us
    ppermute x2, starting transfers between devices, exchange(): lax.ppermute(to_pair, 'patch', both_ways([(i, i + 1) for i in range(0, gr...  2.18 us
    ppermute x2, starting transfers between devices, exchange(): lax.ppermute(z_pair, 'sect', both_ways([(i, i + 1) for i in range(0, sect...  1.24 us
  transfers between devices with their start and end apart: 8, of which 0 were waited for; matrix products, arithmetic and copies ran while one was open for 0% of the time, Pallas kernels for 32%

profile of v2, /device:TPU:1, one launch (start us, length us, event | category | flops | bytes accessed | tf_op | source)
XLA Modules:
  0.0 46.2 jit_solution(12993320326712136779)
XLA Ops:
  0.6 0.0 copy-start.1
  0.6 3.8 %start_layers.1 = (f32[6144,128]{1,0:T(8,128)S(1)}, f32[8,96,128]{2,1,0:T(8,128)S(1)}, f32[4,96,128]{2,1,0:T(8,128)S(1)}, f32[4,96,128]{2,1,0:T(8,128)S(1)}, f32...) custom-call(s32[2,2]{1,0:T(2,128)} %sizes_any.5, ...), custom_call_target="tpu_custom_call" | custom-call | tf_op jit(solution)/shard_map/start_layers/pallas_call | solution.py:602
  4.4 2.1 %collective-permute-start = (f32[4,96,128]{2,1,0:T(8,128)S(1)}, f32[4,96,128]{2,1,0:T(8,128)S(1)}, u32[]{:S(2)}, u32[]{:S(2)}) collective-permute-start(f32[4,96,128]{2,1,0:T(8,128)S(1)} %get-tuple-element.20), channel_id=1, source_target_pairs={{0,4},{8,12},{16,20},{24,28},{4,0},{12,8},{20,16},{28,24},{1,5},{9... | collective-permute-start | bytes 589832 | tf_op jit(solution)/shard_map/ppermute | solution.py:598
  6.5 3.3 %collective-permute-start.1 = (f32[4,96,128]{2,1,0:T(8,128)S(1)}, f32[4,96,128]{2,1,0:T(8,128)S(1)}, u32[]{:S(2)}, u32[]{:S(2)}) collective-permute-start(f32[4,96,128]{2,1,0:T(8,128)S(1)} %get-tuple-element.21), channel_id=1, source_target_pairs={{4,8},{12,16},{20,24},{28,0},{8,4},{16,12},{24,20},{0,28},{5,9},{1... | collective-permute-start | bytes 589832 | tf_op jit(solution)/shard_map/ppermute | solution.py:599
  9.8 1.2 %collective-permute-start.2 = (f32[3,3,64,128]{3,2,1,0:T(8,128)S(1)}, f32[3,3,64,128]{3,2,1,0:T(8,128)S(1)}, u32[]{:S(2)}, u32[]{:S(2)}) collective-permute-start(f32[3,3,64,128]{3,2,1,0:T(8,128)S(1)} %get-tuple-element.22), channel_id=1, source_target_pairs={{0,1},{2,3},{1,0},{3,2},{4,5},{6,7},{5,4},{7,6},{8,9},{10,11},{9,8... | collective-permute-start | bytes 884744 | tf_op jit(solution)/shard_map/ppermute | solution.py:596
  11.1 3.2 %collective-permute-start.3 = (f32[3,3,64,128]{3,2,1,0:T(8,128)S(1)}, f32[3,3,64,128]{3,2,1,0:T(8,128)S(1)}, u32[]{:S(2)}, u32[]{:S(2)}) collective-permute-start(f32[3,3,64,128]{3,2,1,0:T(8,128)S(1)} %get-tuple-element.23), channel_id=1, source_target_pairs={{1,2},{2,1},{5,6},{6,5},{9,10},{10,9},{13,14},{14,13},{17,18},{18,... | collective-permute-start | bytes 884744 | tf_op jit(solution)/shard_map/ppermute | solution.py:597
  14.3 0.0 copy-done.1
  14.3 0.0 copy-start
  14.3 7.4 %volume_terms.2.volume = f32[6144,128]{1,0:T(8,128)S(1)} custom-call(f32[6144,128]{1,0:T(8,128)S(1)} %get-tuple-element.17.field, bf16[96,96]{1,0:T(8,128)(2,1)S(1)} %copy-done.1, bf16[6,768,256]{2,1,0:T(8,128)(2,1)S(1)} %get-tuple-element.18.weights), custom_call_target="tpu_custom_call" | custom-call | flops 10000000000 | bytes 8000000 | tf_op jit(solution)/shard_map/volume_terms/pallas_call | solution.py:621
  21.7 0.0 collective-permute-done.from_pair
  21.7 0.0 collective-permute-done.1.from_ring
  21.7 0.0 collective-permute-done.2.z_pair
  21.7 0.0 collective-permute-done.3.z_ring
  21.7 0.0 copy-done
  21.7 6.8 %finish_first.1 = (f32[2,3,32,4096]{3,2,1,0:T(8,128)}, f32[6144,128]{1,0:T(8,128)S(1)}, f32[8,96,128]{2,1,0:T(8,128)S(1)}, f32[4,96,128]{2,1,0:T(8,128)S(1)}, f3...) custom-call(s32[2,2]{1,0:T(2,128)} %sizes_any.5, s32[2,4]{1,0:T(2,128)} %partners_any.5, ...), custom_call_target="tpu_custom_call" | custom-call | tf_op jit(solution)/shard_map/finish_first/pallas_call | solution.py:646
  28.5 0.1 collective-permute-start.4
  28.6 1.3 %collective-permute-start.5 = (f32[4,96,128]{2,1,0:T(8,128)S(1)}, f32[4,96,128]{2,1,0:T(8,128)S(1)}, u32[]{:S(2)}, u32[]{:S(2)}) collective-permute-start(f32[4,96,128]{2,1,0:T(8,128)S(1)} %get-tuple-element.29), channel_id=1, source_target_pairs={{4,8},{12,16},{20,24},{28,0},{8,4},{16,12},{24,20},{0,28},{5,9},{1... | collective-permute-start | bytes 589832 | tf_op jit(solution)/shard_map/ppermute | solution.py:599
  30.0 0.0 collective-permute-start.6
  30.0 3.1 %collective-permute-start.7 = (f32[3,3,64,128]{3,2,1,0:T(8,128)S(1)}, f32[3,3,64,128]{3,2,1,0:T(8,128)S(1)}, u32[]{:S(2)}, u32[]{:S(2)}) collective-permute-start(f32[3,3,64,128]{3,2,1,0:T(8,128)S(1)} %get-tuple-element.31), channel_id=1, source_target_pairs={{1,2},{2,1},{5,6},{6,5},{9,10},{10,9},{13,14},{14,13},{17,18},{18,... | collective-permute-start | bytes 884744 | tf_op jit(solution)/shard_map/ppermute | solution.py:597
  33.0 7.4 %volume_terms.3.volume = f32[6144,128]{1,0:T(8,128)S(1)} custom-call(f32[6144,128]{1,0:T(8,128)S(1)} %get-tuple-element.26.field, bf16[96,96]{1,0:T(8,128)(2,1)S(1)} %copy-done.1, bf16[6,768,256]{2,1,0:T(8,128)(2,1)S(1)} %get-tuple-element.18.weights), custom_call_target="tpu_custom_call" | custom-call | flops 10000000000 | bytes 8000000 | tf_op jit(solution)/shard_map/volume_terms/pallas_call | solution.py:621
  40.4 0.0 collective-permute-done.4.from_pair
  40.4 0.0 collective-permute-done.5.from_ring
  40.4 0.0 collective-permute-done.6.z_pair
  40.4 0.0 collective-permute-done.7.z_ring
  40.5 5.6 %finish_last.1 = f32[2,3,32,4096]{3,2,1,0:T(8,128)} custom-call(s32[2,2]{1,0:T(2,128)} %sizes_any.5, s32[2,4]{1,0:T(2,128)} %partners_any.5, f32[2,16]{1,0:T(2,128)} %bitcast.3, f32[6144,128]{1,0:T(8,128)S(1)} %volume_terms.3.volume, f32[8,96,128]{2,1,0:T(8,128)S(1)} %get-tuple-element.27.own, f32[4,96,128]{2,1,0:T(8,128)S(1)} %collective-permute-done.4.from_pair, ...), custom_call_target="tpu_custom_call" | custom-call | tf_op jit(solution)/shard_map/finish_last/pallas_call | solution.py:646
Async XLA Ops:
  0.6 13.7 %copy-start.1 = (bf16[96,96]{1,0:T(8,128)(2,1)S(1)}, bf16[96,96]{1,0:T(8,128)(2,1)}, u32[]{:S(2)}) copy-start(bf16[96,96]{1,0:T(8,128)(2,1)} %constant.2.clone.z_table) | copy-start | bytes 55300
  4.4 17.3 %collective-permute-start = (f32[4,96,128]{2,1,0:T(8,128)S(1)}, f32[4,96,128]{2,1,0:T(8,128)S(1)}, u32[]{:S(2)}, u32[]{:S(2)}) collective-permute-start(f32[4,96,128]{2,1,0:T(8,128)S(1)} %get-tuple-element.20), channel_id=1, source_target_pairs={{0,4},{8,12},{16,20},{24,28},{4,0},{12,8},{20,16},{28,24},{1,5},{9... | collective-permute-start | bytes 589832 | tf_op jit(solution)/shard_map/ppermute | solution.py:598
  6.5 15.2 %collective-permute-start.1 = (f32[4,96,128]{2,1,0:T(8,128)S(1)}, f32[4,96,128]{2,1,0:T(8,128)S(1)}, u32[]{:S(2)}, u32[]{:S(2)}) collective-permute-start(f32[4,96,128]{2,1,0:T(8,128)S(1)} %get-tuple-element.21), channel_id=1, source_target_pairs={{4,8},{12,16},{20,24},{28,0},{8,4},{16,12},{24,20},{0,28},{5,9},{1... | collective-permute-start | bytes 589832 | tf_op jit(solution)/shard_map/ppermute | solution.py:599
  9.8 11.9 %collective-permute-start.2 = (f32[3,3,64,128]{3,2,1,0:T(8,128)S(1)}, f32[3,3,64,128]{3,2,1,0:T(8,128)S(1)}, u32[]{:S(2)}, u32[]{:S(2)}) collective-permute-start(f32[3,3,64,128]{3,2,1,0:T(8,128)S(1)} %get-tuple-element.22), channel_id=1, source_target_pairs={{0,1},{2,3},{1,0},{3,2},{4,5},{6,7},{5,4},{7,6},{8,9},{10,11},{9,8... | collective-permute-start | bytes 884744 | tf_op jit(solution)/shard_map/ppermute | solution.py:596
  11.1 10.7 %collective-permute-start.3 = (f32[3,3,64,128]{3,2,1,0:T(8,128)S(1)}, f32[3,3,64,128]{3,2,1,0:T(8,128)S(1)}, u32[]{:S(2)}, u32[]{:S(2)}) collective-permute-start(f32[3,3,64,128]{3,2,1,0:T(8,128)S(1)} %get-tuple-element.23), channel_id=1, source_target_pairs={{1,2},{2,1},{5,6},{6,5},{9,10},{10,9},{13,14},{14,13},{17,18},{18,... | collective-permute-start | bytes 884744 | tf_op jit(solution)/shard_map/ppermute | solution.py:597
  14.3 7.4 %copy-start = (f32[2,4,64,64]{3,2,1,0:T(8,128)S(1)}, f32[2,4,64,64]{3,2,1,0:T(8,128)}, u32[]{:S(2)}) copy-start(f32[2,4,64,64]{3,2,1,0:T(8,128)} %transfer.3) | copy-start | bytes 393220
  28.5 11.9 %collective-permute-start.4 = (f32[4,96,128]{2,1,0:T(8,128)S(1)}, f32[4,96,128]{2,1,0:T(8,128)S(1)}, u32[]{:S(2)}, u32[]{:S(2)}) collective-permute-start(f32[4,96,128]{2,1,0:T(8,128)S(1)} %get-tuple-element.28), channel_id=1, source_target_pairs={{0,4},{8,12},{16,20},{24,28},{4,0},{12,8},{20,16},{28,24},{1,5},{9... | collective-permute-start | bytes 589832 | tf_op jit(solution)/shard_map/ppermute | solution.py:598
  28.6 11.8 %collective-permute-start.5 = (f32[4,96,128]{2,1,0:T(8,128)S(1)}, f32[4,96,128]{2,1,0:T(8,128)S(1)}, u32[]{:S(2)}, u32[]{:S(2)}) collective-permute-start(f32[4,96,128]{2,1,0:T(8,128)S(1)} %get-tuple-element.29), channel_id=1, source_target_pairs={{4,8},{12,16},{20,24},{28,0},{8,4},{16,12},{24,20},{0,28},{5,9},{1... | collective-permute-start | bytes 589832 | tf_op jit(solution)/shard_map/ppermute | solution.py:599
  30.0 10.5 %collective-permute-start.6 = (f32[3,3,64,128]{3,2,1,0:T(8,128)S(1)}, f32[3,3,64,128]{3,2,1,0:T(8,128)S(1)}, u32[]{:S(2)}, u32[]{:S(2)}) collective-permute-start(f32[3,3,64,128]{3,2,1,0:T(8,128)S(1)} %get-tuple-element.30), channel_id=1, source_target_pairs={{0,1},{2,3},{1,0},{3,2},{4,5},{6,7},{5,4},{7,6},{8,9},{10,11},{9,8... | collective-permute-start | bytes 884744 | tf_op jit(solution)/shard_map/ppermute | solution.py:596
  30.0 10.5 %collective-permute-start.7 = (f32[3,3,64,128]{3,2,1,0:T(8,128)S(1)}, f32[3,3,64,128]{3,2,1,0:T(8,128)S(1)}, u32[]{:S(2)}, u32[]{:S(2)}) collective-permute-start(f32[3,3,64,128]{3,2,1,0:T(8,128)S(1)} %get-tuple-element.31), channel_id=1, source_target_pairs={{1,2},{2,1},{5,6},{6,5},{9,10},{10,9},{13,14},{14,13},{17,18},{18,... | collective-permute-start | bytes 884744 | tf_op jit(solution)/shard_map/ppermute | solution.py:597

commit v3 on v2

--- a/solution.py
+++ b/solution.py
@@ -76,7 +76,7 @@
 def layer_order():
     rows = lax.broadcasted_iota(jnp.int32, (512, 512), 0)
     cols = lax.broadcasted_iota(jnp.int32, (512, 512), 1)
-    x = (rows // 128) * 16 + (rows // 8) % 16
+    x = rows // 128 + 4 * ((rows // 8) % 16)
     return jnp.where(cols == (rows % 8) * 64 + x, 1.0, 0.0).astype(BF16)
 
 
@@ -102,46 +102,40 @@
     return jnp.dot(a, b, preferred_element_type=F32)
 
 
-def face_sides(partners_ref, me, groups):
+SIZES, SOURCES, SLOTS, SCALARS = 0, 4, 12, 20
+
+
+def fill_scalars(sizes_ref, partners_ref, lame_ref, scalars, factors, me, groups):
+    for p in range(2):
+        for axis in range(2):
+            scalars[SIZES + 2 * p + axis] = sizes_ref[p, axis]
     before = lax.rem(me + groups - 1, groups)
+    pair_side = 1 - me % 2
     codes = [partners_ref[k // FACES, k % FACES] for k in range(2 * FACES)]
-    sides = [jnp.where(code // (2 * FACES) == before, 0, 1) for code in codes]
-    return codes, sides
-
-
-def send_sources(partners_ref, me, groups):
-    codes, sides = face_sides(partners_ref, me, groups)
-    sources = [[jnp.int32(0)] * FACES for _ in range(2)]
+    ring = []
+    for code in codes:
+        side = jnp.where(code // (2 * FACES) == before, 0, 1)
+        ring.append(jnp.where(side == pair_side, 0, 1))
     for k in range(2 * FACES):
-        rank = jnp.int32(0)
+        sent, read = jnp.int32(0), jnp.int32(0)
         for other in range(2 * FACES):
             if other != k:
-                below = (sides[other] == sides[k]) & (codes[other] < codes[k])
-                rank = rank + jnp.where(below, 1, 0)
-        for side in range(2):
-            for slot in range(FACES):
-                hit = (sides[k] == side) & (rank == slot)
-                sources[side][slot] = jnp.where(hit, k, sources[side][slot])
-    return sources
-
-
-def receive_slots(partners_ref, me, groups):
-    _, sides = face_sides(partners_ref, me, groups)
-    slots = []
-    for k in range(2 * FACES):
-        rank = jnp.int32(0)
-        for other in range(k):
-            rank = rank + jnp.where(sides[other] == sides[k], 1, 0)
-        slots.append(rank)
-    return sides, slots
-
-
-def layer_select(sizes_ref):
+                same = ring[other] == ring[k]
+                sent = sent + jnp.where(same & (codes[other] < codes[k]), 1, 0)
+                if other < k:
+                    read = read + jnp.where(same, 1, 0)
+        scalars[SOURCES + ring[k] * FACES + sent] = jnp.int32(k)
+        scalars[SLOTS + k] = ring[k] * FACES + read
+        p = k // FACES
+        factors[k] = (PENALTY - 1.5) * (0.5 * (lame_ref[0, me * 2 + p] + lame_ref[0, codes[k] // FACES]))
+
+
+def layer_select(scalars):
     rows = lax.broadcasted_iota(jnp.int32, (LANES, LANES), 0)
     cols = lax.broadcasted_iota(jnp.int32, (LANES, LANES), 1)
     patch = (cols // 4) % 2
     layer = cols % 4
-    size_y = jnp.where(patch == 0, sizes_ref[0, 1], sizes_ref[1, 1])
+    size_y = jnp.where(patch == 0, scalars[SIZES + 1], scalars[SIZES + 3])
     at = jnp.where(layer < 2, layer, size_y + 1 - layer)
     base = jnp.where(rows == patch * PAD + at, 1.0, 0.0)
     return [jnp.where(cols // 8 == j, base, 0.0).astype(BF16) for j in range(16)]
@@ -157,8 +151,7 @@
     return jnp.concatenate(parts, axis=0)
 
 
-def send_layers(field, sizes_ref, partners_ref, order, own, to_pair, to_ring, z_pair, z_ring, groups, depth):
-    me = lax.axis_index("patch")
+def send_layers(field, scalars, order, own, to_pair, to_ring, z_pair, z_ring, depth):
     even_section = lax.axis_index("sect") % 2 == 0
     for c in range(COMPS):
         for d in range(HALO):
@@ -169,16 +162,16 @@
     outer, inner = row_at(field, 0, depth), row_at(field, 1, depth)
     own[0] = merge(outer, swap_halves(inner))
     own[FACES] = merge(swap_halves(outer), inner)
-    outer, inner = [row_at(field, sizes_ref[0, 0] - 1 - i, depth) for i in range(2)]
+    outer, inner = [row_at(field, scalars[SIZES] - 1 - i, depth) for i in range(2)]
     own[1] = merge(outer, swap_halves(inner))
-    outer, inner = [row_at(field, sizes_ref[1, 0] - 1 - i, depth) for i in range(2)]
+    outer, inner = [row_at(field, scalars[SIZES + 2] - 1 - i, depth) for i in range(2)]
     own[FACES + 1] = merge(swap_halves(outer), inner)
-    select = jnp.concatenate(layer_select(sizes_ref), axis=0)
+    select = jnp.concatenate(layer_select(scalars), axis=0)
     groups_rows = []
     for g in range(4):
         for c in range(COMPS):
-            base = c * PAD * depth + 16 * g * depth
-            wide = [field[base + j * depth : base + (j + 1) * depth, :] for j in range(16)]
+            starts = [(c * PAD + 4 * j + g) * depth for j in range(16)]
+            wide = [field[start : start + depth, :] for start in starts]
             groups_rows.append(jnp.concatenate(wide, axis=1))
     rows = jnp.concatenate(groups_rows, axis=0)
     count = rows.shape[0]
@@ -194,17 +187,15 @@
         for f in range(2):
             at = (p * 2 + f) * LANES
             own[p * FACES + 2 + f] = sorted_layers[:, at : at + LANES]
-    sources = send_sources(partners_ref, me, groups)
-    even = me % 2 == 0
     for slot in range(FACES):
-        to_pair[slot] = own[jnp.where(even, sources[1][slot], sources[0][slot])]
-        to_ring[slot] = own[jnp.where(even, sources[0][slot], sources[1][slot])]
-
-
-def active_lanes(sizes_ref):
+        to_pair[slot] = own[scalars[SOURCES + slot]]
+        to_ring[slot] = own[scalars[SOURCES + FACES + slot]]
+
+
+def active_lanes(scalars):
     lane = lane_iota()
-    size_x = jnp.where(lane < PAD, sizes_ref[0, 0], sizes_ref[1, 0])
-    size_y = jnp.where(lane < PAD, sizes_ref[0, 1], sizes_ref[1, 1])
+    size_x = jnp.where(lane < PAD, scalars[SIZES], scalars[SIZES + 2])
+    size_y = jnp.where(lane < PAD, scalars[SIZES + 1], scalars[SIZES + 3])
     return size_x, (lane % PAD) < size_y
 
 
@@ -267,7 +258,7 @@
 
 def start_kernel(
     groups, depth, sizes_any, partners_any, lame_any, disp_any,
-    field, own, to_pair, to_ring, z_pair, z_ring, weights, order,
+    field, own, to_pair, to_ring, z_pair, z_ring, weights, order, scalars, factors,
     sizes_ref, partners_ref, lame_ref, disp, sems,
 ):
     copies = []
@@ -283,8 +274,10 @@
     order[...] = layer_order()
     for copy in small:
         copy.wait()
-    fill_weights(lame_ref, lax.axis_index("patch"), weights)
-    size_x, in_y = active_lanes(sizes_ref)
+    me = lax.axis_index("patch")
+    fill_scalars(sizes_ref, partners_ref, lame_ref, scalars, factors, me, groups)
+    fill_weights(lame_ref, me, weights)
+    size_x, in_y = active_lanes(scalars)
     for c in range(COMPS):
         copies[c].wait()
         for k in range(PAD // 2):
@@ -297,7 +290,7 @@
             base = (c * PAD + 2 * k) * depth
             field[base : base + depth, :] = jnp.where(keep_even, even, 0.0)
             field[base + depth : base + 2 * depth, :] = jnp.where(keep_odd, odd, 0.0)
-    send_layers(field, sizes_ref, partners_ref, order, own, to_pair, to_ring, z_pair, z_ring, groups, depth)
+    send_layers(field, scalars, order, own, to_pair, to_ring, z_pair, z_ring, depth)
 
 
 def plane_sums(fields, weights):
@@ -328,7 +321,23 @@
     return total + ((mass(3) + mass(-3)) - (stiff(3) + stiff(-3))) + (slope(3) - slope(-3))
 
 
-def volume_kernel(depth, field, z_table, weights, out, sums_ref):
+def to_output(result, c, k, even, odd):
+    result[0, c, :, k * LANES : (k + 1) * LANES] = merge(even, swap_halves(odd))
+    result[1, c, :, k * LANES : (k + 1) * LANES] = merge(swap_halves(even), odd)
+
+
+def send_output(result, result_any, sems, part, parts):
+    lanes = pl.ds(part * (PAD * PAD // parts), PAD * PAD // parts)
+    copy = pltpu.make_async_copy(result.at[:, :, :, lanes], result_any.at[:, :, :, lanes], sems.at[part])
+    copy.start()
+    return copy
+
+
+OUT_PARTS = 4
+
+
+def volume_kernel(depth, field, z_table, weights, out, *rest):
+    result_any, sums_ref, result, sems = rest if len(rest) > 1 else (None, *rest, None, None)
     for i in range(9):
         for x in (0, 1, 2, PAD + 3, PAD + 4, PAD + 5):
             sums_ref[i, x] = jnp.zeros((depth, LANES), F32)
@@ -368,6 +377,7 @@
             out[start : start + 8, :] = result[j]
 
     done = 0
+    copies = []
     for block in range(PAD // XBLOCK + 1):
         x0 = block * XBLOCK
         pieces = []
@@ -380,6 +390,14 @@
                 sums_ref[c * 3 + kind, x0 + 3 : x0 + 3 + XBLOCK] = value.reshape(XBLOCK, depth, LANES)
         for piece in pieces:
             along_x(*piece)
+        if result_any is not None and x0 < PAD:
+            for k in range(x0 // 2, (x0 + XBLOCK) // 2):
+                for c in range(COMPS):
+                    start = (c * PAD + 2 * k) * depth
+                    to_output(result, c, k, field[start : start + depth, :], field[start + depth : start + 2 * depth, :])
+            copies.append(send_output(result, result_any, sems, block, PAD // XBLOCK))
+    for copy in copies:
+        copy.wait()
 
 
 def depth_edges(before, after):
@@ -409,23 +427,32 @@
 
 
 def finish_kernel(
-    groups, depth, last, sizes_any, partners_any, lame_any, volume, own, from_pair, from_ring, z_pair, z_ring,
-    transfer, weights, order, result_any, *rest,
+    depth, last, scalars, factors, volume, own, from_pair, from_ring, z_pair, z_ring, transfer, weights, order,
+    field, *rest,
 ):
     if last:
-        field, edge, result, sizes_ref, partners_ref, lame_ref, sems = rest
+        result_any, edge, result, sems = rest
     else:
-        field, *sends, edge, result, sizes_ref, partners_ref, lame_ref, sems = rest
-    small = [
-        pltpu.make_async_copy(sizes_any, sizes_ref, sems.at[0]),
-        pltpu.make_async_copy(partners_any, partners_ref, sems.at[1]),
-        pltpu.make_async_copy(lame_any, lame_ref, sems.at[2]),
-    ]
-    for copy in small:
-        copy.start()
-    me = lax.axis_index("patch")
-    pair_side = 1 - me % 2
+        *sends, edge = rest
     even_section = lax.axis_index("sect") % 2 == 0
+    terms = []
+    for k in range(2 * FACES):
+        slot = scalars[SLOTS + k]
+        far = jnp.where(slot < FACES, from_pair[lax.rem(slot, FACES)], from_ring[lax.rem(slot, FACES)])
+        mat = transfer[k // FACES, k % FACES]
+        zero = jnp.zeros((PAD, PAD), F32)
+        both = jnp.concatenate(
+            [jnp.concatenate([mat, zero], axis=1), jnp.concatenate([zero, mat], axis=1)], axis=0
+        )
+        far_high, far_low = split(far)
+        mat_high, mat_low = split(both)
+        moved = lax.dot_general(
+            jnp.concatenate([far_high, far_low, far_high], axis=1),
+            jnp.concatenate([mat_high, mat_high, mat_low], axis=1),
+            (((1,), (1,)), ((), ())),
+            preferred_element_type=F32,
+        )
+        terms.append(factors[k] * (own[k] - moved))
     fields = {}
     for c in range(COMPS):
         before = [jnp.where(even_section, z_ring[c, d], z_pair[c, d]) for d in range(HALO)]
@@ -441,29 +468,6 @@
         for z in range(2 * HALO):
             slot = z if z < HALO else z + 2
             edge[pl.ds(base + HALO * 8 + slot, PAD, stride=8), :] = value[z * PAD : (z + 1) * PAD]
-    for copy in small:
-        copy.wait()
-    sides, slots = receive_slots(partners_ref, me, groups)
-    terms = []
-    for p in range(2):
-        for f in range(FACES):
-            k = p * FACES + f
-            far = jnp.where(sides[k] == pair_side, from_pair[slots[k]], from_ring[slots[k]])
-            mu_face = 0.5 * (lame_ref[0, me * 2 + p] + lame_ref[0, partners_ref[p, f] // FACES])
-            mat = transfer[p, f]
-            zero = jnp.zeros((PAD, PAD), F32)
-            both = jnp.concatenate(
-                [jnp.concatenate([mat, zero], axis=1), jnp.concatenate([zero, mat], axis=1)], axis=0
-            )
-            far_high, far_low = split(far)
-            mat_high, mat_low = split(both)
-            moved = lax.dot_general(
-                jnp.concatenate([far_high, far_low, far_high], axis=1),
-                jnp.concatenate([mat_high, mat_high, mat_low], axis=1),
-                (((1,), (1,)), ((), ())),
-                preferred_element_type=F32,
-            )
-            terms.append(((PENALTY - 1.5) * mu_face) * (own[k] - moved))
     per = COMPS * depth
     stacked = jnp.concatenate([swap_halves(terms[p * FACES + 2 + f]) for p in range(2) for f in range(2)], axis=1)
     term_high, term_low = split(stacked)
@@ -476,8 +480,29 @@
     placed = placed[:per] + placed[per:]
     placed = jnp.concatenate([placed[:, g * LANES : (g + 1) * LANES] for g in range(4)], axis=0)
     placed_parts = jnp.concatenate(split(placed), axis=1)
-    select = layer_select(sizes_ref)
-    for j in range(0, 16, 2):
+    select = layer_select(scalars)
+
+    def add_row(x, addend):
+        for c in range(COMPS):
+            start = c * PAD * depth + x * depth
+            if not isinstance(x, int):
+                start = pl.multiple_of(start, depth)
+            field[pl.ds(start, depth), :] += addend[c * depth : (c + 1) * depth]
+
+    zero = jnp.zeros((per, LANES), F32)
+    one, two = terms[0], terms[FACES]
+    add_row(0, merge(swap_halves(one), two))
+    add_row(1, merge(one, swap_halves(two)))
+    one, two = terms[1], terms[FACES + 1]
+    add_row(scalars[SIZES] - 1, merge(swap_halves(one), zero))
+    add_row(scalars[SIZES] - 2, merge(one, zero))
+    add_row(scalars[SIZES + 2] - 1, merge(zero, two))
+    add_row(scalars[SIZES + 2] - 2, merge(zero, swap_halves(two)))
+    size_x, in_y = active_lanes(scalars)
+    slot_rows = lax.broadcasted_iota(jnp.int32, (8, LANES), 0)
+    copies = []
+    for x0 in range(0, PAD, XROWS):
+        j = x0 // 4
         pair = jnp.concatenate([select[j], select[j + 1]], axis=0)
         spread = lax.dot_general(
             placed_parts,
@@ -485,34 +510,7 @@
             (((1,), (1,)), ((), ())),
             preferred_element_type=F32,
         )
-        for g in range(4):
-            for c in range(COMPS):
-                for i in range(2):
-                    base = (c * PAD + 16 * g + j + i) * depth
-                    at = (g * COMPS + c) * depth
-                    piece = spread[at : at + depth, i * LANES : (i + 1) * LANES]
-                    field[base : base + depth, :] = volume[base : base + depth, :] + piece
-    def add_row(x, addend):
         for c in range(COMPS):
-            start = c * PAD * depth + x * depth
-            if not isinstance(x, int):
-                start = pl.multiple_of(start, depth)
-            field[pl.ds(start, depth), :] += addend[c * depth : (c + 1) * depth]
-
-    zero = jnp.zeros((per, LANES), F32)
-    one, two = terms[0], terms[FACES]
-    add_row(0, merge(swap_halves(one), two))
-    add_row(1, merge(one, swap_halves(two)))
-    one, two = terms[1], terms[FACES + 1]
-    add_row(sizes_ref[0, 0] - 1, merge(swap_halves(one), zero))
-    add_row(sizes_ref[0, 0] - 2, merge(one, zero))
-    add_row(sizes_ref[1, 0] - 1, merge(zero, two))
-    add_row(sizes_ref[1, 0] - 2, merge(zero, swap_halves(two)))
-    size_x, in_y = active_lanes(sizes_ref)
-    slot_rows = lax.broadcasted_iota(jnp.int32, (8, LANES), 0)
-    copies = []
-    for c in range(COMPS):
-        for x0 in range(0, PAD, XROWS):
             held = []
             for kind in range(3):
                 base = ((c * 3 + kind) * EDGE_X + x0) * 8
@@ -525,12 +523,14 @@
 
             def whole(x):
                 start = (c * PAD + x) * depth
+                row, col = ((x % 4) * COMPS + c) * depth, ((x - x0) // 4) * LANES
+                value = field[start : start + depth, :] + spread[row : row + depth, col : col + LANES]
                 edge_x = edges[x - x0]
                 value = jnp.concatenate(
                     [
-                        field[start : start + 8, :] + jnp.where(slot_rows < HALO, edge_x, 0.0),
-                        field[start + 8 : start + depth - 8, :],
-                        field[start + depth - 8 : start + depth, :] + jnp.where(slot_rows >= 8 - HALO, edge_x, 0.0),
+                        value[:8] + jnp.where(slot_rows < HALO, edge_x, 0.0),
+                        value[8 : depth - 8],
+                        value[depth - 8 :] + jnp.where(slot_rows >= 8 - HALO, edge_x, 0.0),
                     ],
                     axis=0,
                 )
@@ -541,17 +541,12 @@
 
             for k in range(x0 // 2, (x0 + XROWS) // 2):
                 even, odd = whole(2 * k), whole(2 * k + 1)
-                result[0, c, :, k * LANES : (k + 1) * LANES] = merge(even, swap_halves(odd))
-                result[1, c, :, k * LANES : (k + 1) * LANES] = merge(swap_halves(even), odd)
-            if (x0 + XROWS) % (PAD // 2) == 0:
-                lanes = pl.ds((x0 + XROWS - PAD // 2) * PAD, PAD * PAD // 2)
-                copy = pltpu.make_async_copy(
-                    result.at[:, c, :, lanes], result_any.at[:, c, :, lanes], sems.at[3 + len(copies)]
-                )
-                copy.start()
-                copies.append(copy)
+                if last:
+                    to_output(result, c, k, even, odd)
+        if last and (x0 + XROWS) % (PAD // OUT_PARTS) == 0:
+            copies.append(send_output(result, result_any, sems, x0 // (PAD // OUT_PARTS), OUT_PARTS))
     if not last:
-        send_layers(field, sizes_ref, partners_ref, order, *sends, groups, depth)
+        send_layers(field, scalars, order, *sends, depth)
     for copy in copies:
         copy.wait()
 
@@ -562,6 +557,7 @@
     sections = lax.axis_size("sect")
     rows = COMPS * PAD * depth
     per = COMPS * depth
+    smem = pl.BlockSpec(memory_space=pltpu.SMEM)
     vmem = pl.BlockSpec(memory_space=pltpu.VMEM)
     away = pl.BlockSpec(memory_space=pl.ANY)
     z_table = jnp.asarray(depth_table(depth))
@@ -572,6 +568,9 @@
 
     def near(values):
         return pltpu.with_memory_space_constraint(values, pltpu.VMEM)
+
+    def scalar(values):
+        return pltpu.with_memory_space_constraint(values, pltpu.SMEM)
 
     def far(values):
         return pltpu.with_memory_space_constraint(values, pltpu.HBM)
@@ -599,13 +598,14 @@
         from_ring = lax.ppermute(to_ring, "patch", both_ways([(i, (i + 1) % groups) for i in range(1, groups, 2)]))
         return own, from_pair, from_ring, z_pair, z_ring
 
-    field, *layers, weights, order = pl.pallas_call(
+    field, *layers, weights, order, scalars, factors = pl.pallas_call(
         functools.partial(start_kernel, groups, depth),
         out_shape=(field_shape,)
         + layer_shapes
-        + (shape(len(TILES), 6 * LANES, 2 * LANES, dtype=BF16), shape(512, 512, dtype=BF16)),
+        + (shape(len(TILES), 6 * LANES, 2 * LANES, dtype=BF16), shape(512, 512, dtype=BF16))
+        + (pltpu.SMEM((SCALARS,), jnp.int32), pltpu.SMEM((2 * FACES,), F32)),
         in_specs=[away] * 4,
-        out_specs=(vmem,) * 8,
+        out_specs=(vmem,) * 8 + (smem,) * 2,
         scratch_shapes=[
             pltpu.SMEM(patch_sizes.shape, jnp.int32),
             pltpu.SMEM(partners.shape, jnp.int32),
@@ -617,44 +617,50 @@
         name="start_layers",
     )(far(patch_sizes), far(partners), far(lame), far(displacement))
 
-    def volume(values):
+    def volume(values, with_output):
+        out_shape = (field_shape,)
+        scratch = [pltpu.VMEM((9, PAD + 6, depth, LANES), F32)]
+        if with_output:
+            out_shape = out_shape + (jax.ShapeDtypeStruct(displacement.shape, F32),)
+            scratch = scratch + [
+                pltpu.VMEM(displacement.shape, F32),
+                pltpu.SemaphoreType.DMA((PAD // XBLOCK,)),
+            ]
         return pl.pallas_call(
             functools.partial(volume_kernel, depth),
-            out_shape=field_shape,
+            out_shape=out_shape,
             in_specs=[vmem] * 3,
-            out_specs=vmem,
-            scratch_shapes=[pltpu.VMEM((9, PAD + 6, depth, LANES), F32)],
+            out_specs=(vmem, away)[: len(out_shape)],
+            scratch_shapes=scratch,
             compiler_params=params(28),
             cost_estimate=pl.CostEstimate(flops=10**10, bytes_accessed=8 * 10**6, transcendentals=0),
-            name="volume_terms",
+            name="volume_and_output" if with_output else "volume_terms",
         )(near(values), z_table, near(weights))
 
     def finish(volume_part, exchanged, last):
-        scratch = [
-            pltpu.VMEM((9 * EDGE_X * 8, LANES), F32),
-            pltpu.VMEM(displacement.shape, F32),
-            pltpu.SMEM(patch_sizes.shape, jnp.int32),
-            pltpu.SMEM(partners.shape, jnp.int32),
-            pltpu.SMEM(lame.shape, F32),
-            pltpu.SemaphoreType.DMA((3 + 2 * COMPS,)),
-        ]
-        out_shape = (jax.ShapeDtypeStruct(displacement.shape, F32),)
+        scratch = [pltpu.VMEM((9 * EDGE_X * 8, LANES), F32)]
         if last:
-            scratch = [pltpu.VMEM((rows, LANES), F32)] + scratch
+            out_shape = (field_shape, jax.ShapeDtypeStruct(displacement.shape, F32))
+            out_specs = (vmem, away)
+            scratch = scratch + [
+                pltpu.VMEM(displacement.shape, F32),
+                pltpu.SemaphoreType.DMA((OUT_PARTS,)),
+            ]
         else:
-            out_shape = out_shape + (field_shape,) + layer_shapes
+            out_shape = (field_shape,) + layer_shapes
+            out_specs = (vmem,) * 6
         return pl.pallas_call(
-            functools.partial(finish_kernel, groups, depth, last),
+            functools.partial(finish_kernel, depth, last),
             out_shape=out_shape,
-            in_specs=[away] * 3 + [vmem] * 9,
-            out_specs=(away,) + (vmem,) * (len(out_shape) - 1),
+            in_specs=[smem] * 2 + [vmem] * 9,
+            out_specs=out_specs,
             scratch_shapes=scratch,
+            input_output_aliases={2: 0},
             compiler_params=params(28),
             name="finish_last" if last else "finish_first",
         )(
-            far(patch_sizes),
-            far(partners),
-            far(lame),
+            scalar(scalars),
+            scalar(factors),
             near(volume_part),
             *[near(part) for part in exchanged],
             transfer,
@@ -662,8 +668,10 @@
             near(order),
         )
 
-    first_apply, field, *next_layers = finish(volume(field), exchange(layers), False)
-    (second_apply,) = finish(volume(field), exchange(next_layers), True)
+    (volume_part,) = volume(field, False)
+    field, *next_layers = finish(volume_part, exchange(layers), False)
+    volume_part, first_apply = volume(field, True)
+    _, second_apply = finish(volume_part, exchange(next_layers), True)
     return first_apply, second_apply
 
 

time: 46.4 us -> 43.8 us (0.944)
  Pallas kernels: 30.9 us -> 28.1 us
    pallas_call x4, Pallas kernels: 27.1 us -> 24.5 us  [the longest x2 15.8 us: volume(): pl.pallas_call(functools.partial(volume_kernel, depth), out_shape=out_sha...]
  transfers between devices with their start and end apart: 8 -> 8, of which waited for: 0 -> 0; matrix products, arithmetic and copies ran while one was open for 0% -> 0% of each run, Pallas kernels for 32% -> 36%
where the time goes in v3:
time: 43.8 us; the launch traced here: 43.7 us
  Pallas kernels  28.1 us (64%)
  starting transfers between devices  14.5 us (33%)
  between operations  0.96 us (2%)
    pallas_call x2, Pallas kernels, volume(): pl.pallas_call(functools.partial(volume_kernel, depth), out_shape=out_sha...  15.8 us
    pallas_call x2, Pallas kernels, finish(): pl.pallas_call(functools.partial(finish_kernel, depth, last), out_shape=o...  8.71 us
    ppermute x2, starting transfers between devices, exchange(): lax.ppermute(z_ring, 'sect', both_ways([(i, i + 1) for i in range(1, sect...  6.51 us
    ppermute x2, starting transfers between devices, exchange(): lax.ppermute(to_ring, 'patch', both_ways([(i, (i + 1) % groups) for i in...  4.63 us
    pallas_call x1, Pallas kernels, shards(): pl.pallas_call(functools.partial(start_kernel, groups, depth), out_shape=...  3.67 us
    ppermute x2, starting transfers between devices, exchange(): lax.ppermute(to_pair, 'patch', both_ways([(i, i + 1) for i in range(0, gr...  2.17 us
    ppermute x2, starting transfers between devices, exchange(): lax.ppermute(z_pair, 'sect', both_ways([(i, i + 1) for i in range(0, sect...  1.24 us
  transfers between devices with their start and end apart: 8, of which 0 were waited for; matrix products, arithmetic and copies ran while one was open for 0% of the time, Pallas kernels for 36%

profile of v3, /device:TPU:1, one launch (start us, length us, event | category | flops | bytes accessed | tf_op | source)
XLA Modules:
  0.0 43.7 jit_solution(17569179672785164469)
XLA Ops:
  0.6 0.0 copy-start.1
  0.6 3.7 %start_layers.1 = (f32[6144,128]{1,0:T(8,128)S(1)}, f32[8,96,128]{2,1,0:T(8,128)S(1)}, f32[4,96,128]{2,1,0:T(8,128)S(1)}, f32[4,96,128]{2,1,0:T(8,128)S(1)}, f32...) custom-call(s32[2,2]{1,0:T(2,128)} %sizes_any.1, ...), custom_call_target="tpu_custom_call" | custom-call | tf_op jit(solution)/shard_map/start_layers/pallas_call | solution.py:601
  4.3 2.1 %collective-permute-start = (f32[4,96,128]{2,1,0:T(8,128)S(1)}, f32[4,96,128]{2,1,0:T(8,128)S(1)}, u32[]{:S(2)}, u32[]{:S(2)}) collective-permute-start(f32[4,96,128]{2,1,0:T(8,128)S(1)} %get-tuple-element.26), channel_id=1, source_target_pairs={{0,4},{8,12},{16,20},{24,28},{4,0},{12,8},{20,16},{28,24},{1,5},{9... | collective-permute-start | bytes 589832 | tf_op jit(solution)/shard_map/ppermute | solution.py:597
  6.4 3.3 %collective-permute-start.1 = (f32[4,96,128]{2,1,0:T(8,128)S(1)}, f32[4,96,128]{2,1,0:T(8,128)S(1)}, u32[]{:S(2)}, u32[]{:S(2)}) collective-permute-start(f32[4,96,128]{2,1,0:T(8,128)S(1)} %get-tuple-element.27), channel_id=1, source_target_pairs={{4,8},{12,16},{20,24},{28,0},{8,4},{16,12},{24,20},{0,28},{5,9},{1... | collective-permute-start | bytes 589832 | tf_op jit(solution)/shard_map/ppermute | solution.py:598
  9.7 1.2 %collective-permute-start.2 = (f32[3,3,64,128]{3,2,1,0:T(8,128)S(1)}, f32[3,3,64,128]{3,2,1,0:T(8,128)S(1)}, u32[]{:S(2)}, u32[]{:S(2)}) collective-permute-start(f32[3,3,64,128]{3,2,1,0:T(8,128)S(1)} %get-tuple-element.28), channel_id=1, source_target_pairs={{0,1},{2,3},{1,0},{3,2},{4,5},{6,7},{5,4},{7,6},{8,9},{10,11},{9,8... | collective-permute-start | bytes 884744 | tf_op jit(solution)/shard_map/ppermute | solution.py:595
  11.0 3.2 %collective-permute-start.3 = (f32[3,3,64,128]{3,2,1,0:T(8,128)S(1)}, f32[3,3,64,128]{3,2,1,0:T(8,128)S(1)}, u32[]{:S(2)}, u32[]{:S(2)}) collective-permute-start(f32[3,3,64,128]{3,2,1,0:T(8,128)S(1)} %get-tuple-element.29), channel_id=1, source_target_pairs={{1,2},{2,1},{5,6},{6,5},{9,10},{10,9},{13,14},{14,13},{17,18},{18,... | collective-permute-start | bytes 884744 | tf_op jit(solution)/shard_map/ppermute | solution.py:596
  14.2 0.0 copy-done.1
  14.2 0.0 copy-start
  14.2 7.3 %volume_terms.1.volume = f32[6144,128]{1,0:T(8,128)S(1)} custom-call(f32[6144,128]{1,0:T(8,128)S(1)} %get-tuple-element.23.field, bf16[96,96]{1,0:T(8,128)(2,1)S(1)} %copy-done.1, bf16[6,768,256]{2,1,0:T(8,128)(2,1)S(1)} %get-tuple-element.24.weights), custom_call_target="tpu_custom_call" | custom-call | flops 10000000000 | bytes 8000000 | tf_op jit(solution)/shard_map/volume_terms/pallas_call | solution.py:629
  21.5 0.0 collective-permute-done.from_pair
  21.5 0.0 collective-permute-done.1.from_ring
  21.5 0.0 collective-permute-done.2.z_pair
  21.6 0.0 collective-permute-done.3.z_ring
  21.6 0.0 copy-done
  21.6 4.4 %finish_first.1 = (f32[6144,128]{1,0:T(8,128)S(1)}, f32[8,96,128]{2,1,0:T(8,128)S(1)}, f32[4,96,128]{2,1,0:T(8,128)S(1)}, f32[4,96,128]{2,1,0:T(8,128)S(1)}, f32...) custom-call(s32[20]{0:T(128)S(4)} %get-tuple-element.21.scalars, ...), custom_call_target="tpu_custom_call", output_to_operand_aliasing={{0}: (2, {})} | custom-call | tf_op jit(solution)/shard_map/finish_first/pallas_call | solution.py:652
  26.0 0.1 collective-permute-start.4
  26.0 1.3 %collective-permute-start.5 = (f32[4,96,128]{2,1,0:T(8,128)S(1)}, f32[4,96,128]{2,1,0:T(8,128)S(1)}, u32[]{:S(2)}, u32[]{:S(2)}) collective-permute-start(f32[4,96,128]{2,1,0:T(8,128)S(1)} %get-tuple-element.36), channel_id=1, source_target_pairs={{4,8},{12,16},{20,24},{28,0},{8,4},{16,12},{24,20},{0,28},{5,9},{1... | collective-permute-start | bytes 589832 | tf_op jit(solution)/shard_map/ppermute | solution.py:598
  27.4 0.0 collective-permute-start.6
  27.4 3.3 %collective-permute-start.7 = (f32[3,3,64,128]{3,2,1,0:T(8,128)S(1)}, f32[3,3,64,128]{3,2,1,0:T(8,128)S(1)}, u32[]{:S(2)}, u32[]{:S(2)}) collective-permute-start(f32[3,3,64,128]{3,2,1,0:T(8,128)S(1)} %get-tuple-element.38), channel_id=1, source_target_pairs={{1,2},{2,1},{5,6},{6,5},{9,10},{10,9},{13,14},{14,13},{17,18},{18,... | collective-permute-start | bytes 884744 | tf_op jit(solution)/shard_map/ppermute | solution.py:596
  30.7 8.4 %volume_and_output.1 = (f32[6144,128]{1,0:T(8,128)S(1)}, f32[2,3,32,4096]{3,2,1,0:T(8,128)}) custom-call(f32[6144,128]{1,0:T(8,128)S(1)} %get-tuple-element.31.field, bf16[96,96]{1,0:T(8,128)(2,1)S(1)} %copy-done.1, bf16[6,768,256]{2,1,0:T(8,128)(2,1)S(1)} %get-tuple-element.24.weights), custom_call_target="tpu_custom_call" | custom-call | flops 10000000000 | bytes 8000000 | tf_op jit(solution)/shard_map/volume_and_output/pallas_call | solution.py:629
  39.1 0.0 collective-permute-done.4.from_pair
  39.1 0.0 collective-permute-done.5.from_ring
  39.2 0.0 collective-permute-done.6.z_pair
  39.2 0.0 collective-permute-done.7.z_ring
  39.2 4.3 %finish_last.1 = (f32[6144,128]{1,0:T(8,128)S(1)}, f32[2,3,32,4096]{3,2,1,0:T(8,128)}) custom-call(s32[20]{0:T(128)S(4)} %get-tuple-element.21.scalars, f32[8]{0:T(128)S(4)} %get-tuple-element.22.factors, f32[6144,128]{1,0:T(8,128)S(1)} %get-tuple-element.33.volume, f32[8,96,128]{2,1,0:T(8,128)S(1)} %get-tuple-element.34.own, ...), custom_call_target="tpu_custom_call", output_to_operand_aliasing={{0}: (2, {})} | custom-call | tf_op jit(solution)/shard_map/finish_last/pallas_call | solution.py:652
Async XLA Ops:
  0.6 13.5 %copy-start.1 = (bf16[96,96]{1,0:T(8,128)(2,1)S(1)}, bf16[96,96]{1,0:T(8,128)(2,1)}, u32[]{:S(2)}) copy-start(bf16[96,96]{1,0:T(8,128)(2,1)} %constant.2.clone.z_table) | copy-start | bytes 55300
  4.3 17.2 %collective-permute-start = (f32[4,96,128]{2,1,0:T(8,128)S(1)}, f32[4,96,128]{2,1,0:T(8,128)S(1)}, u32[]{:S(2)}, u32[]{:S(2)}) collective-permute-start(f32[4,96,128]{2,1,0:T(8,128)S(1)} %get-tuple-element.26), channel_id=1, source_target_pairs={{0,4},{8,12},{16,20},{24,28},{4,0},{12,8},{20,16},{28,24},{1,5},{9... | collective-permute-start | bytes 589832 | tf_op jit(solution)/shard_map/ppermute | solution.py:597
  6.4 15.1 %collective-permute-start.1 = (f32[4,96,128]{2,1,0:T(8,128)S(1)}, f32[4,96,128]{2,1,0:T(8,128)S(1)}, u32[]{:S(2)}, u32[]{:S(2)}) collective-permute-start(f32[4,96,128]{2,1,0:T(8,128)S(1)} %get-tuple-element.27), channel_id=1, source_target_pairs={{4,8},{12,16},{20,24},{28,0},{8,4},{16,12},{24,20},{0,28},{5,9},{1... | collective-permute-start | bytes 589832 | tf_op jit(solution)/shard_map/ppermute | solution.py:598
  9.7 11.8 %collective-permute-start.2 = (f32[3,3,64,128]{3,2,1,0:T(8,128)S(1)}, f32[3,3,64,128]{3,2,1,0:T(8,128)S(1)}, u32[]{:S(2)}, u32[]{:S(2)}) collective-permute-start(f32[3,3,64,128]{3,2,1,0:T(8,128)S(1)} %get-tuple-element.28), channel_id=1, source_target_pairs={{0,1},{2,3},{1,0},{3,2},{4,5},{6,7},{5,4},{7,6},{8,9},{10,11},{9,8... | collective-permute-start | bytes 884744 | tf_op jit(solution)/shard_map/ppermute | solution.py:595
  11.0 10.6 %collective-permute-start.3 = (f32[3,3,64,128]{3,2,1,0:T(8,128)S(1)}, f32[3,3,64,128]{3,2,1,0:T(8,128)S(1)}, u32[]{:S(2)}, u32[]{:S(2)}) collective-permute-start(f32[3,3,64,128]{3,2,1,0:T(8,128)S(1)} %get-tuple-element.29), channel_id=1, source_target_pairs={{1,2},{2,1},{5,6},{6,5},{9,10},{10,9},{13,14},{14,13},{17,18},{18,... | collective-permute-start | bytes 884744 | tf_op jit(solution)/shard_map/ppermute | solution.py:596
  14.2 7.4 %copy-start = (f32[2,4,64,64]{3,2,1,0:T(8,128)S(1)}, f32[2,4,64,64]{3,2,1,0:T(8,128)}, u32[]{:S(2)}) copy-start(f32[2,4,64,64]{3,2,1,0:T(8,128)} %transfer.3) | copy-start | bytes 393220
  26.0 13.2 %collective-permute-start.4 = (f32[4,96,128]{2,1,0:T(8,128)S(1)}, f32[4,96,128]{2,1,0:T(8,128)S(1)}, u32[]{:S(2)}, u32[]{:S(2)}) collective-permute-start(f32[4,96,128]{2,1,0:T(8,128)S(1)} %get-tuple-element.35), channel_id=1, source_target_pairs={{0,4},{8,12},{16,20},{24,28},{4,0},{12,8},{20,16},{28,24},{1,5},{9... | collective-permute-start | bytes 589832 | tf_op jit(solution)/shard_map/ppermute | solution.py:597
  26.0 13.1 %collective-permute-start.5 = (f32[4,96,128]{2,1,0:T(8,128)S(1)}, f32[4,96,128]{2,1,0:T(8,128)S(1)}, u32[]{:S(2)}, u32[]{:S(2)}) collective-permute-start(f32[4,96,128]{2,1,0:T(8,128)S(1)} %get-tuple-element.36), channel_id=1, source_target_pairs={{4,8},{12,16},{20,24},{28,0},{8,4},{16,12},{24,20},{0,28},{5,9},{1... | collective-permute-start | bytes 589832 | tf_op jit(solution)/shard_map/ppermute | solution.py:598
  27.4 11.8 %collective-permute-start.6 = (f32[3,3,64,128]{3,2,1,0:T(8,128)S(1)}, f32[3,3,64,128]{3,2,1,0:T(8,128)S(1)}, u32[]{:S(2)}, u32[]{:S(2)}) collective-permute-start(f32[3,3,64,128]{3,2,1,0:T(8,128)S(1)} %get-tuple-element.37), channel_id=1, source_target_pairs={{0,1},{2,3},{1,0},{3,2},{4,5},{6,7},{5,4},{7,6},{8,9},{10,11},{9,8... | collective-permute-start | bytes 884744 | tf_op jit(solution)/shard_map/ppermute | solution.py:595
  27.4 11.8 %collective-permute-start.7 = (f32[3,3,64,128]{3,2,1,0:T(8,128)S(1)}, f32[3,3,64,128]{3,2,1,0:T(8,128)S(1)}, u32[]{:S(2)}, u32[]{:S(2)}) collective-permute-start(f32[3,3,64,128]{3,2,1,0:T(8,128)S(1)} %get-tuple-element.38), channel_id=1, source_target_pairs={{1,2},{2,1},{5,6},{6,5},{9,10},{10,9},{13,14},{14,13},{17,18},{18,... | collective-permute-start | bytes 884744 | tf_op jit(solution)/shard_map/ppermute | solution.py:596

commit v4 on v3

v4 whole, which is shorter than its diff:
```python
import functools

import jax
import jax.numpy as jnp
import ml_dtypes
import numpy as np
from jax import lax
from jax.experimental import pallas as pl
from jax.experimental.pallas import tpu as pltpu
from jax.sharding import PartitionSpec as P

PAD = 64
LANES = 128
HALO = 3
COMPS = 3
MAXN = 61
FACES = 4
MASS_INT = (2416.0, 1191.0, 120.0, 1.0)
STIFF_INT = (80.0, -15.0, -24.0, -1.0)
SLOPE_INT = (245.0, 56.0, 1.0)
MASS_DEN = 5040.0
STIFF_DEN = 120.0
SLOPE_DEN = 720.0
PENALTY = 3.0
PAIRS = PAD // 2
KEEP = (MAXN + 1) // 2
KBLOCK = 16
KROWS = 8
MIB = 1024 * 1024
F32 = jnp.float32
BF16 = jnp.bfloat16


def split_np(table):
    high = table.astype(ml_dtypes.bfloat16)
    low = (table - high.astype(np.float64)).astype(ml_dtypes.bfloat16)
    return high, low


def band_np(size, kind):
    table = np.zeros((size, size))
    for i in range(size):
        for d in range(0, 4):
            for sign in (1, -1):
                j = i + sign * d
                if 0 <= j < size:
                    if kind == "slope":
                        if d:
                            table[i, j] = sign * SLOPE_INT[d - 1] / SLOPE_DEN
                    elif kind == "mass":
                        table[i, j] = MASS_INT[d] / MASS_DEN
                    else:
                        table[i, j] = STIFF_INT[d] / STIFF_DEN
    return table


def depth_table(depth):
    table = np.concatenate([band_np(depth, k) for k in ("mass", "stiff", "slope")], axis=0)
    high, low = split_np(table)
    return np.concatenate([high, high, low], axis=1)


def in_kernel_bands():
    rows = lax.broadcasted_iota(jnp.int32, (LANES, LANES), 0)
    cols = lax.broadcasted_iota(jnp.int32, (LANES, LANES), 1)
    ahead = jnp.where(rows // PAD == cols // PAD, rows - cols, PAD)
    apart = jnp.abs(ahead)
    mass = jnp.zeros((LANES, LANES), F32)
    stiff, slope = mass, mass
    for d in range(4):
        mass = jnp.where(apart == d, MASS_INT[d] / MASS_DEN, mass)
        stiff = jnp.where(apart == d, STIFF_INT[d] / STIFF_DEN, stiff)
        if d:
            slope = jnp.where(ahead == d, SLOPE_INT[d - 1] / SLOPE_DEN, slope)
            slope = jnp.where(ahead == -d, -SLOPE_INT[d - 1] / SLOPE_DEN, slope)
    return mass, stiff, slope


def layer_order():
    rows = lax.broadcasted_iota(jnp.int32, (512, 512), 0)
    cols = lax.broadcasted_iota(jnp.int32, (512, 512), 1)
    x = 8 * ((rows // 8) % 8) + 2 * (rows // 128) + (rows // 4) % 2
    patch_layer = 4 * ((rows // 64) % 2) + rows % 4
    return jnp.where(cols == patch_layer * 64 + x, 1.0, 0.0).astype(BF16)


def split(values):
    high = values.astype(BF16)
    low = (values - high.astype(F32)).astype(BF16)
    return high, low


def lane_iota(shape=(1, LANES)):
    return lax.broadcasted_iota(jnp.int32, shape, len(shape) - 1)


def swap_halves(values):
    return pltpu.roll(values, PAD, axis=values.ndim - 1)


def merge(low_half, high_half):
    return jnp.where(lane_iota() < PAD, low_half, high_half)


def dot(a, b):
    return jnp.dot(a, b, preferred_element_type=F32)


SIZES, SOURCES, SLOTS, SCALARS = 0, 4, 12, 20


def fill_scalars(sizes_ref, partners_ref, lame_ref, scalars, factors, me, groups):
    for p in range(2):
        for axis in range(2):
            scalars[SIZES + 2 * p + axis] = sizes_ref[p, axis]
    before = lax.rem(me + groups - 1, groups)
    pair_side = 1 - me % 2
    codes = [partners_ref[k // FACES, k % FACES] for k in range(2 * FACES)]
    ring = []
    for code in codes:
        side = jnp.where(code // (2 * FACES) == before, 0, 1)
        ring.append(jnp.where(side == pair_side, 0, 1))
    for k in range(2 * FACES):
        sent, read = jnp.int32(0), jnp.int32(0)
        for other in range(2 * FACES):
            if other != k:
                same = ring[other] == ring[k]
                sent = sent + jnp.where(same & (codes[other] < codes[k]), 1, 0)
                if other < k:
                    read = read + jnp.where(same, 1, 0)
        scalars[SOURCES + ring[k] * FACES + sent] = jnp.int32(k)
        scalars[SLOTS + k] = ring[k] * FACES + read
        p = k // FACES
        factors[k] = (PENALTY - 1.5) * (0.5 * (lame_ref[0, me * 2 + p] + lame_ref[0, codes[k] // FACES]))


def layer_select(scalars):
    rows = lax.broadcasted_iota(jnp.int32, (LANES, LANES), 0)
    cols = lax.broadcasted_iota(jnp.int32, (LANES, LANES), 1)
    layer = cols % 4
    size_y = jnp.where(cols < PAD, scalars[SIZES + 1], scalars[SIZES + 3])
    at = jnp.where(layer < 2, layer, size_y + 1 - layer)
    base = jnp.where(rows == ((cols // 4) % 2) * PAD + at, 1.0, 0.0)
    return [jnp.where(cols // 8 == j, base, 0.0).astype(BF16) for j in range(16)]


def row_of(p, c, k, depth):
    row = ((p * COMPS + c) * PAIRS + k) * depth
    return row if isinstance(row, int) else pl.multiple_of(row, depth)


def pair_at(field, p, k, depth):
    return jnp.concatenate([field[pl.ds(row_of(p, c, k, depth), depth), :] for c in range(COMPS)], axis=0)


def last_pairs(scalars, p):
    size = scalars[SIZES + 2 * p]
    return lax.div(size - 1, 2), lax.div(size - 2, 2), lax.rem(size, 2) == 0


def send_layers(field, scalars, order, own, to_pair, to_ring, z_pair, z_ring, depth):
    even_section = lax.axis_index("sect") % 2 == 0
    for p in range(2):
        for c in range(COMPS):
            for d in range(HALO):
                start = row_of(p, c, 0, depth)
                low = field[pl.ds(start + d, PAIRS, stride=depth), :]
                high = field[pl.ds(start + depth - HALO + d, PAIRS, stride=depth), :]
                z_pair[p, c, d] = jnp.where(even_section, high, low)
                z_ring[p, c, d] = jnp.where(even_section, low, high)
        own[p * FACES] = pair_at(field, p, 0, depth)
        outer_pair, inner_pair, same = last_pairs(scalars, p)
        outer, inner = pair_at(field, p, outer_pair, depth), pair_at(field, p, inner_pair, depth)
        own[p * FACES + 1] = jnp.where(same, swap_halves(outer), merge(outer, inner))
    select = jnp.concatenate(layer_select(scalars), axis=0)
    groups_rows = []
    for g in range(4):
        for c in range(COMPS):
            starts = [row_of(p, c, 4 * j + g, depth) for p in range(2) for j in range(8)]
            groups_rows.append(jnp.concatenate([field[start : start + depth, :] for start in starts], axis=1))
    rows = jnp.concatenate(groups_rows, axis=0)
    count = rows.shape[0]
    row_high, row_low = split(rows)
    picked = dot(jnp.concatenate([row_high, row_low], axis=0), select)
    picked = picked[:count] + picked[count:]
    per = COMPS * depth
    picked = jnp.concatenate([picked[g * per : (g + 1) * per] for g in range(4)], axis=1)
    pick_high, pick_low = split(picked)
    sorted_layers = dot(jnp.concatenate([pick_high, pick_low], axis=0), order[...])
    sorted_layers = sorted_layers[:per] + sorted_layers[per:]
    for p in range(2):
        for f in range(2):
            at = (p * 2 + f) * LANES
            own[p * FACES + 2 + f] = sorted_layers[:, at : at + LANES]
    for slot in range(FACES):
        to_pair[slot] = own[scalars[SOURCES + slot]]
        to_ring[slot] = own[scalars[SOURCES + FACES + slot]]


def active_lanes(scalars, p):
    lane = lane_iota()
    in_y = (lane % PAD) < scalars[SIZES + 2 * p + 1]
    x_left = scalars[SIZES + 2 * p] - lane // PAD
    return lambda k: in_y & (x_left > 2 * k)


MASS, STIFF, SLOPE = 0, 1, 2
TILES = (
    (((0, MASS), (0, STIFF)), ((0, STIFF), (0, MASS))),
    (((1, MASS), (2, SLOPE)), ((0, SLOPE), (1, MASS))),
    (((1, MASS), (1, STIFF)), ((1, STIFF), (1, MASS))),
    (((0, MASS), None), ((1, SLOPE), None)),
    (((2, MASS), (2, STIFF)), ((2, STIFF), (2, MASS))),
    (((0, SLOPE), (1, SLOPE)), ((2, SLOPE), (2, MASS))),
)
TERMS = {
    ((0, MASS), (0, STIFF)): (MASS, "both"),
    ((0, MASS), (0, MASS)): (STIFF, "mu"),
    ((0, STIFF), (0, MASS)): (MASS, "mu"),
    ((1, MASS), (0, SLOPE)): (SLOPE, "grad"),
    ((2, SLOPE), (0, SLOPE)): (MASS, "grad"),
    ((1, MASS), (1, STIFF)): (MASS, "mu"),
    ((1, MASS), (1, MASS)): (STIFF, "both"),
    ((1, STIFF), (1, MASS)): (MASS, "mu"),
    ((2, SLOPE), (1, MASS)): (SLOPE, "grad"),
    ((0, MASS), (1, SLOPE)): (SLOPE, "grad"),
    ((2, MASS), (2, STIFF)): (MASS, "mu"),
    ((2, MASS), (2, MASS)): (STIFF, "mu"),
    ((2, STIFF), (2, MASS)): (MASS, "both"),
    ((1, SLOPE), (2, MASS)): (SLOPE, "grad"),
    ((0, SLOPE), (2, SLOPE)): (MASS, "grad"),
}
OUT_SCALE = {STIFF: 1.0 / STIFF_DEN, MASS: 1.0 / MASS_DEN, SLOPE: 1.0 / SLOPE_DEN}


def fill_weights(lame_ref, me, weights):
    tables = in_kernel_bands()
    for p in range(2):
        mu = lame_ref[0, me * 2 + p]
        grad = mu + lame_ref[1, me * 2 + p]
        factors = {"mu": mu, "both": mu + grad, "grad": -grad}
        placed = set()
        for t, (sources, targets) in enumerate(TILES):
            for i, source in enumerate(sources):
                for o, target in enumerate(targets):
                    term = TERMS.get((source, target))
                    if term is None or (source, target) in placed:
                        block = jnp.zeros((LANES, LANES), F32)
                    else:
                        placed.add((source, target))
                        block = tables[term[0]] * (factors[term[1]] * OUT_SCALE[target[1]])
                    block_high, block_low = split(block)
                    cols = slice(o * LANES, (o + 1) * LANES)
                    for part, piece in enumerate((block_high, block_high, block_low)):
                        at = part * 2 * LANES + i * LANES
                        weights[p * len(TILES) + t, at : at + LANES, cols] = piece


def start_kernel(
    groups, depth, sizes_any, partners_any, lame_any, disp_any,
    field, own, to_pair, to_ring, z_pair, z_ring, weights, order, scalars, factors,
    sizes_ref, partners_ref, lame_ref, disp, sems,
):
    copies = []
    for c in range(COMPS):
        copies.append(pltpu.make_async_copy(disp_any.at[:, c], disp.at[:, c], sems.at[c]))
    small = [
        pltpu.make_async_copy(sizes_any, sizes_ref, sems.at[COMPS]),
        pltpu.make_async_copy(partners_any, partners_ref, sems.at[COMPS + 1]),
        pltpu.make_async_copy(lame_any, lame_ref, sems.at[COMPS + 2]),
    ]
    for copy in small + copies:
        copy.start()
    order[...] = layer_order()
    for copy in small:
        copy.wait()
    me = lax.axis_index("patch")
    fill_scalars(sizes_ref, partners_ref, lame_ref, scalars, factors, me, groups)
    fill_weights(lame_ref, me, weights)
    keeps = [active_lanes(scalars, p) for p in range(2)]
    for c in range(COMPS):
        copies[c].wait()
        for p in range(2):
            for k in range(PAIRS):
                start = row_of(p, c, k, depth)
                value = disp[p, c, :, k * LANES : (k + 1) * LANES]
                field[start : start + depth, :] = jnp.where(keeps[p](k), value, 0.0)
    send_layers(field, scalars, order, own, to_pair, to_ring, z_pair, z_ring, depth)


def plane_sums(fields, weights, p, complete=None):
    sums = {}
    for t, (sources, targets) in enumerate(TILES):
        if sources[1] is None:
            high, low = fields[sources[0]]
            weight = jnp.concatenate(
                [weights[p * len(TILES) + t, part * 2 * LANES : part * 2 * LANES + LANES, :LANES] for part in range(3)],
                axis=0,
            )
        else:
            high, low = [jnp.concatenate([fields[s][part] for s in sources], axis=1) for part in range(2)]
            weight = weights[p * len(TILES) + t]
        out = dot(jnp.concatenate([high, low, high], axis=1), weight)
        for o, target in enumerate(targets):
            if target is not None:
                piece = out[:, o * LANES : (o + 1) * LANES]
                sums[target] = piece if target not in sums else sums[target] + piece
        if complete is not None and t % 2 == 1:
            complete(t // 2, [sums[(t // 2, kind)] for kind in range(3)])
    return sums


def band_x(stiff, mass, slope, count):
    def at(values, d, extra=0):
        return values[2 + d : 2 + d + count + extra]

    total = STIFF_INT[0] * at(stiff, 0) + MASS_INT[0] * at(mass, 0)
    total = total + STIFF_INT[2] * (at(stiff, 1) + at(stiff, -1))
    total = total + MASS_INT[2] * (at(mass, 1) + at(mass, -1))
    total = total + SLOPE_INT[1] * (at(slope, 1) - at(slope, -1))
    odd = STIFF_INT[1] * (at(stiff, 0, 1) + at(stiff, -1, 1))
    odd = odd + MASS_INT[1] * (at(mass, 0, 1) + at(mass, -1, 1))
    odd = odd + SLOPE_INT[0] * (at(slope, 0, 1) - at(slope, -1, 1))
    odd = odd + ((at(mass, 1, 1) + at(mass, -2, 1)) - (at(stiff, 1, 1) + at(stiff, -2, 1)))
    odd = odd + (at(slope, 1, 1) - at(slope, -2, 1))
    return total + swap_halves(merge(odd[1:], odd[:-1]))


def send_output(result, result_any, sems, part, parts):
    lanes = pl.ds(part * (PAD * PAD // parts), PAD * PAD // parts)
    copy = pltpu.make_async_copy(result.at[:, :, :, lanes], result_any.at[:, :, :, lanes], sems.at[part])
    copy.start()
    return copy


OUT_PARTS = 4
SUMS = (18, KEEP + 4)


def volume_kernel(depth, field, z_table, weights, *rest):
    copy = None
    if len(rest) == 2:
        out, sums_ref = rest
    else:
        finished, out, finished_any, sums_ref, sem = rest
        copy = pltpu.make_async_copy(finished, finished_any, sem)
        copy.start()
    for i in range(18):
        for k in (0, 1, KEEP + 2, KEEP + 3):
            sums_ref[i, k] = jnp.zeros((depth, LANES), F32)

    def along_z(p, k0, count):
        fields = {}
        for c in range(COMPS):
            starts = [row_of(p, c, k0 + j, depth) for j in range(count)]
            rows = [field[start : start + depth, :] for start in starts]
            high, low = split(jnp.concatenate(rows, axis=1))
            banded = dot(z_table[...], jnp.concatenate([high, low, high], axis=0))
            parts = split(banded)
            for kind in range(3):
                fields[(c, kind)] = tuple(
                    jnp.concatenate(
                        [
                            part[kind * depth : (kind + 1) * depth, j * LANES : (j + 1) * LANES]
                            for j in range(count)
                        ],
                        axis=0,
                    )
                    for part in parts
                )
        return fields

    def along_x(p, k0, count, c, z0):
        held = [sums_ref[p * 9 + c * 3 + kind, k0 : k0 + count + 4, z0 : z0 + 8, :] for kind in range(3)]
        total = band_x(held[STIFF], held[MASS], held[SLOPE], count)
        for j in range(count):
            start = row_of(p, c, k0 + j, depth) + z0
            out[start : start + 8, :] = total[j]

    blocks = [(p, k0, min(KBLOCK, KEEP - k0)) for p in range(2) for k0 in range(0, KEEP, KBLOCK)]
    done = [0, 0]
    ahead = along_z(*blocks[0])
    for i, (p, k0, count) in enumerate(blocks):
        fields = ahead
        if i + 1 < len(blocks):
            ahead = along_z(*blocks[i + 1])
        ready = KEEP if k0 + count == KEEP else k0 + count - 2
        first = done[p]
        while done[p] < KEEP and min(done[p] + KROWS, KEEP) <= ready:
            done[p] = min(done[p] + KROWS, KEEP)

        def complete(c, values):
            for kind in range(3):
                sums_ref[p * 9 + c * 3 + kind, k0 + 2 : k0 + 2 + count] = values[kind].reshape(count, depth, LANES)
            for k in range(first, done[p], KROWS):
                for z0 in range(0, depth, 8):
                    along_x(p, k, min(KROWS, KEEP - k), c, z0)

        plane_sums(fields, weights, p, complete)
    if copy is not None:
        copy.wait()


def depth_edges(before, after):
    mass, stiff, slope = [], [], []
    for table, den, out, sign in (
        (MASS_INT[1:], MASS_DEN, mass, 1.0),
        (STIFF_INT[1:], STIFF_DEN, stiff, 1.0),
        (SLOPE_INT, SLOPE_DEN, slope, -1.0),
    ):
        coef = [value / den for value in table]
        for z in range(3):
            total = None
            for d in range(z + 1, 4):
                piece = (sign * coef[d - 1]) * before[3 + z - d]
                total = piece if total is None else total + piece
            out.append(total)
        for z in range(3):
            total = None
            for d in range(3 - z, 4):
                piece = coef[d - 1] * after[z + d - 3]
                total = piece if total is None else total + piece
            out.append(total)
    return [jnp.concatenate(parts, axis=0) for parts in (mass, stiff, slope)]


EDGE_K = PAIRS + 4


def finish_kernel(
    depth, last, scalars, factors, volume, own, from_pair, from_ring, z_pair, z_ring, transfer, weights, order,
    field, *rest,
):
    if last:
        result_any, edge, result, sems = rest
    else:
        *sends, result, edge = rest
    even_section = lax.axis_index("sect") % 2 == 0
    terms = []
    for k in range(2 * FACES):
        slot = scalars[SLOTS + k]
        far = jnp.where(slot < FACES, from_pair[lax.rem(slot, FACES)], from_ring[lax.rem(slot, FACES)])
        mat = transfer[k // FACES, k % FACES]
        zero = jnp.zeros((PAD, PAD), F32)
        both = jnp.concatenate(
            [jnp.concatenate([mat, zero], axis=1), jnp.concatenate([zero, mat], axis=1)], axis=0
        )
        far_high, far_low = split(far)
        mat_high, mat_low = split(both)
        moved = lax.dot_general(
            jnp.concatenate([far_high, far_low, far_high], axis=1),
            jnp.concatenate([mat_high, mat_high, mat_low], axis=1),
            (((1,), (1,)), ((), ())),
            preferred_element_type=F32,
        )
        terms.append(factors[k] * (own[k] - moved))
    for p in range(2):
        fields = {}
        for c in range(COMPS):
            before = [jnp.where(even_section, z_ring[p, c, d], z_pair[p, c, d]) for d in range(HALO)]
            after = [jnp.where(even_section, z_pair[p, c, d], z_ring[p, c, d]) for d in range(HALO)]
            banded = depth_edges(before, after)
            for kind in range(3):
                fields[(c, kind)] = split(banded[kind])
        sums = plane_sums(fields, weights, p)
        for (c, kind), value in sums.items():
            base = (p * 9 + c * 3 + kind) * EDGE_K * 8
            edge[base : base + 16, :] = jnp.zeros((16, LANES), F32)
            edge[base + (2 + PAIRS) * 8 : base + EDGE_K * 8, :] = jnp.zeros((16, LANES), F32)
            for z in range(2 * HALO):
                slot = z if z < HALO else z + 2
                edge[pl.ds(base + 16 + slot, PAIRS, stride=8), :] = value[z * PAIRS : (z + 1) * PAIRS]
    per = COMPS * depth
    stacked = jnp.concatenate([swap_halves(terms[p * FACES + 2 + f]) for p in range(2) for f in range(2)], axis=1)
    term_high, term_low = split(stacked)
    placed = lax.dot_general(
        jnp.concatenate([term_high, term_low], axis=0),
        order[...],
        (((1,), (1,)), ((), ())),
        preferred_element_type=F32,
    )
    placed = placed[:per] + placed[per:]
    placed = jnp.concatenate([placed[:, g * LANES : (g + 1) * LANES] for g in range(4)], axis=0)
    placed_parts = jnp.concatenate(split(placed), axis=1)
    select = layer_select(scalars)

    def add_pair(p, k, addend):
        for c in range(COMPS):
            field[pl.ds(row_of(p, c, k, depth), depth), :] += addend[c * depth : (c + 1) * depth]

    zero = jnp.zeros((per, LANES), F32)
    for p in range(2):
        add_pair(p, 0, swap_halves(terms[p * FACES]))
        outer_pair, inner_pair, same = last_pairs(scalars, p)
        term = terms[p * FACES + 1]
        add_pair(p, outer_pair, jnp.where(same, term, merge(swap_halves(term), zero)))
        add_pair(p, inner_pair, jnp.where(same, zero, merge(zero, swap_halves(term))))
    keeps = [active_lanes(scalars, p) for p in range(2)]
    slot_rows = lax.broadcasted_iota(jnp.int32, (8, LANES), 0)
    copies = []
    for j in range(8):
        both = jnp.concatenate([select[j], select[8 + j]], axis=0)
        spread = lax.dot_general(
            placed_parts,
            jnp.concatenate([both, both], axis=1),
            (((1,), (1,)), ((), ())),
            preferred_element_type=F32,
        )
        for p in range(2):
            for c in range(COMPS):
                held = []
                for kind in range(3):
                    base = ((p * 9 + c * 3 + kind) * EDGE_K + 4 * j) * 8
                    held.append(edge[base : base + 64, :].reshape(8, 8, LANES))
                edges = band_x(held[STIFF], held[MASS], held[SLOPE], 4)
                for g in range(4):
                    k = 4 * j + g
                    start = row_of(p, c, k, depth)
                    row = (g * COMPS + c) * depth
                    value = field[start : start + depth, :] + spread[row : row + depth, p * LANES : (p + 1) * LANES]
                    value = jnp.concatenate(
                        [
                            value[:8] + jnp.where(slot_rows < HALO, edges[g], 0.0),
                            value[8 : depth - 8],
                            value[depth - 8 :] + jnp.where(slot_rows >= 8 - HALO, edges[g], 0.0),
                        ],
                        axis=0,
                    )
                    value = jnp.where(keeps[p](k), value, 0.0)
                    result[p, c, :, k * LANES : (k + 1) * LANES] = value
                    if not last:
                        field[start : start + depth, :] = value
        if last and (j + 1) % (8 // OUT_PARTS) == 0:
            copies.append(send_output(result, result_any, sems, j // (8 // OUT_PARTS), OUT_PARTS))
    if not last:
        send_layers(field, scalars, order, *sends, depth)
    for copy in copies:
        copy.wait()


def shards(displacement, lame_params, patch_sizes, partners, transfer):
    depth = displacement.shape[2]
    groups = lax.axis_size("patch")
    sections = lax.axis_size("sect")
    rows = 2 * COMPS * PAIRS * depth
    per = COMPS * depth
    smem = pl.BlockSpec(memory_space=pltpu.SMEM)
    vmem = pl.BlockSpec(memory_space=pltpu.VMEM)
    away = pl.BlockSpec(memory_space=pl.ANY)
    z_table = jnp.asarray(depth_table(depth))
    lame = lame_params.T

    def shape(*dims, dtype=F32):
        return pltpu.VMEM(dims, dtype)

    def near(values):
        return pltpu.with_memory_space_constraint(values, pltpu.VMEM)

    def scalar(values):
        return pltpu.with_memory_space_constraint(values, pltpu.SMEM)

    def far(values):
        return pltpu.with_memory_space_constraint(values, pltpu.HBM)

    def params(mib):
        return pltpu.CompilerParams(vmem_limit_bytes=mib * MIB)

    field_shape = shape(rows, LANES)
    layer_shapes = (
        shape(2 * FACES, per, LANES),
        shape(FACES, per, LANES),
        shape(FACES, per, LANES),
        shape(2, COMPS, HALO, PAIRS, LANES),
        shape(2, COMPS, HALO, PAIRS, LANES),
    )

    def both_ways(pairs):
        return pairs + [(j, i) for i, j in pairs]

    def exchange(layers):
        own, to_pair, to_ring, z_pair, z_ring = layers
        z_pair = lax.ppermute(z_pair, "sect", both_ways([(i, i + 1) for i in range(0, sections - 1, 2)]))
        z_ring = lax.ppermute(z_ring, "sect", both_ways([(i, i + 1) for i in range(1, sections - 1, 2)]))
        from_pair = lax.ppermute(to_pair, "patch", both_ways([(i, i + 1) for i in range(0, groups, 2)]))
        from_ring = lax.ppermute(to_ring, "patch", both_ways([(i, (i + 1) % groups) for i in range(1, groups, 2)]))
        return own, from_pair, from_ring, z_pair, z_ring

    field, *layers, weights, order, scalars, factors = pl.pallas_call(
        functools.partial(start_kernel, groups, depth),
        out_shape=(field_shape,)
        + layer_shapes
        + (shape(2 * len(TILES), 6 * LANES, 2 * LANES, dtype=BF16), shape(512, 512, dtype=BF16))
        + (pltpu.SMEM((SCALARS,), jnp.int32), pltpu.SMEM((2 * FACES,), F32)),
        in_specs=[away] * 4,
        out_specs=(vmem,) * 8 + (smem,) * 2,
        scratch_shapes=[
            pltpu.SMEM(patch_sizes.shape, jnp.int32),
            pltpu.SMEM(partners.shape, jnp.int32),
            pltpu.SMEM(lame.shape, F32),
            pltpu.VMEM(displacement.shape, F32),
            pltpu.SemaphoreType.DMA((COMPS + 3,)),
        ],
        compiler_params=params(24),
        name="start_layers",
    )(far(patch_sizes), far(partners), far(lame), far(displacement))

    def volume(values, finished=None):
        out_shape = (field_shape,)
        operands = (near(values), z_table, near(weights))
        scratch = [pltpu.VMEM(SUMS + (depth, LANES), F32)]
        if finished is not None:
            out_shape = out_shape + (jax.ShapeDtypeStruct(displacement.shape, F32),)
            operands = operands + (near(finished),)
            scratch = scratch + [pltpu.SemaphoreType.DMA(())]
        return pl.pallas_call(
            functools.partial(volume_kernel, depth),
            out_shape=out_shape,
            in_specs=[vmem] * len(operands),
            out_specs=(vmem, away)[: len(out_shape)],
            scratch_shapes=scratch,
            compiler_params=params(30),
            cost_estimate=pl.CostEstimate(flops=10**10, bytes_accessed=8 * 10**6, transcendentals=0),
            name="volume_terms" if finished is None else "volume_and_output",
        )(*operands)

    def finish(volume_part, exchanged, last):
        scratch = [pltpu.VMEM((18 * EDGE_K * 8, LANES), F32)]
        if last:
            out_shape = (field_shape, jax.ShapeDtypeStruct(displacement.shape, F32))
            out_specs = (vmem, away)
            scratch = scratch + [
                pltpu.VMEM(displacement.shape, F32),
                pltpu.SemaphoreType.DMA((OUT_PARTS,)),
            ]
        else:
            out_shape = (field_shape,) + layer_shapes + (shape(*displacement.shape),)
            out_specs = (vmem,) * 7
        return pl.pallas_call(
            functools.partial(finish_kernel, depth, last),
            out_shape=out_shape,
            in_specs=[smem] * 2 + [vmem] * 9,
            out_specs=out_specs,
            scratch_shapes=scratch,
            input_output_aliases={2: 0},
            compiler_params=params(30),
            name="finish_last" if last else "finish_first",
        )(
            scalar(scalars),
            scalar(factors),
            near(volume_part),
            *[near(part) for part in exchanged],
            transfer,
            near(weights),
            near(order),
        )

    (volume_part,) = volume(field)
    field, *next_layers, finished = finish(volume_part, exchange(layers), False)
    volume_part, first_apply = volume(field, finished)
    _, second_apply = finish(volume_part, exchange(next_layers), True)
    return first_apply, second_apply


def solution(mesh):
    return jax.shard_map(
        shards,
        mesh=mesh,
        in_specs=(
            P("patch", None, "sect", None),
            P(),
            P("patch", None),
            P("patch", None),
            P("patch", None, None, None),
        ),
        out_specs=(P("patch", None, "sect", None), P("patch", None, "sect", None)),
        check_vma=False,
    )
```

time: 43.8 us -> 41.3 us (0.943)
  Pallas kernels: 28.1 us -> 25.6 us
    pallas_call x2, Pallas kernels: 15.8 us -> 13.2 us  [volume(): pl.pallas_call(functools.partial(volume_kernel, depth), out_shape=out_sha...]
  transfers between devices with their start and end apart: 8 -> 8, of which waited for: 0 -> 0; matrix products, arithmetic and copies ran while one was open for 0% -> 0% of each run, Pallas kernels for 36% -> 32%
where the time goes in v4:
time: 41.3 us; the launch traced here: 41.1 us
  Pallas kernels  25.6 us (62%)
  starting transfers between devices  14.5 us (35%)
  between operations  0.96 us (2%)
    pallas_call x2, Pallas kernels, volume(): pl.pallas_call(functools.partial(volume_kernel, depth), out_shape=out_sha...  13.2 us
    pallas_call x2, Pallas kernels, finish(): pl.pallas_call(functools.partial(finish_kernel, depth, last), out_shape=o...  8.8 us
    ppermute x2, starting transfers between devices, exchange(): lax.ppermute(z_ring, 'sect', both_ways([(i, i + 1) for i in range(1, sect...  6.5 us
    ppermute x2, starting transfers between devices, exchange(): lax.ppermute(to_ring, 'patch', both_ways([(i, (i + 1) % groups) for i in...  4.63 us
    pallas_call x1, Pallas kernels, shards(): pl.pallas_call(functools.partial(start_kernel, groups, depth), out_shape=...  3.54 us
    ppermute x2, starting transfers between devices, exchange(): lax.ppermute(to_pair, 'patch', both_ways([(i, i + 1) for i in range(0, gr...  2.18 us
    ppermute x2, starting transfers between devices, exchange(): lax.ppermute(z_pair, 'sect', both_ways([(i, i + 1) for i in range(0, sect...  1.24 us
  transfers between devices with their start and end apart: 8, of which 0 were waited for; matrix products, arithmetic and copies ran while one was open for 0% of the time, Pallas kernels for 32%

profile of v4, /device:TPU:1, one launch (start us, length us, event | category | flops | bytes accessed | tf_op | source)
XLA Modules:
  0.0 41.1 jit_solution(13464072332690105257)
XLA Ops:
  0.6 0.0 copy-start.1
  0.6 3.5 %start_layers.1 = (f32[6144,128]{1,0:T(8,128)S(1)}, f32[8,96,128]{2,1,0:T(8,128)S(1)}, f32[4,96,128]{2,1,0:T(8,128)S(1)}, f32[4,96,128]{2,1,0:T(8,128)S(1)}, f32...) custom-call(s32[2,2]{1,0:T(2,128)} %sizes_any.1, ...), custom_call_target="tpu_custom_call" | custom-call | tf_op jit(solution)/shard_map/start_layers/pallas_call | solution.py:588
  4.2 2.1 %collective-permute-start = (f32[4,96,128]{2,1,0:T(8,128)S(1)}, f32[4,96,128]{2,1,0:T(8,128)S(1)}, u32[]{:S(2)}, u32[]{:S(2)}) collective-permute-start(f32[4,96,128]{2,1,0:T(8,128)S(1)} %get-tuple-element.27), channel_id=1, source_target_pairs={{0,4},{8,12},{16,20},{24,28},{4,0},{12,8},{20,16},{28,24},{1,5},{9... | collective-permute-start | bytes 589832 | tf_op jit(solution)/shard_map/ppermute | solution.py:584
  6.3 3.3 %collective-permute-start.1 = (f32[4,96,128]{2,1,0:T(8,128)S(1)}, f32[4,96,128]{2,1,0:T(8,128)S(1)}, u32[]{:S(2)}, u32[]{:S(2)}) collective-permute-start(f32[4,96,128]{2,1,0:T(8,128)S(1)} %get-tuple-element.28), channel_id=1, source_target_pairs={{4,8},{12,16},{20,24},{28,0},{8,4},{16,12},{24,20},{0,28},{5,9},{1... | collective-permute-start | bytes 589832 | tf_op jit(solution)/shard_map/ppermute | solution.py:585
  9.6 1.2 %collective-permute-start.2 = (f32[2,3,3,32,128]{4,3,2,1,0:T(8,128)S(1)}, f32[2,3,3,32,128]{4,3,2,1,0:T(8,128)S(1)}, u32[]{:S(2)}, u32[]{:S(2)}) collective-permute-start(f32[2,3,3,32,128]{4,3,2,1,0:T(8,128)S(1)} %get-tuple-element.29), channel_id=1, source_target_pairs={{0,1},{2,3},{1,0},{3,2},{4,5},{6,7},{5,4},{7,6},{8,9},{10,11},{9,8... | collective-permute-start | bytes 884744 | tf_op jit(solution)/shard_map/ppermute | solution.py:582
  10.8 3.2 %collective-permute-start.3 = (f32[2,3,3,32,128]{4,3,2,1,0:T(8,128)S(1)}, f32[2,3,3,32,128]{4,3,2,1,0:T(8,128)S(1)}, u32[]{:S(2)}, u32[]{:S(2)}) collective-permute-start(f32[2,3,3,32,128]{4,3,2,1,0:T(8,128)S(1)} %get-tuple-element.30), channel_id=1, source_target_pairs={{1,2},{2,1},{5,6},{6,5},{9,10},{10,9},{13,14},{14,13},{17,18},{18,... | collective-permute-start | bytes 884744 | tf_op jit(solution)/shard_map/ppermute | solution.py:583
  14.0 0.0 copy-done.1
  14.1 0.0 copy-start
  14.1 6.6 %volume_terms.1.volume = f32[6144,128]{1,0:T(8,128)S(1)} custom-call(f32[6144,128]{1,0:T(8,128)S(1)} %get-tuple-element.24.field, bf16[96,96]{1,0:T(8,128)(2,1)S(1)} %copy-done.1, bf16[12,768,256]{2,1,0:T(8,128)(2,1)S(1)} %get-tuple-element.25.weights), custom_call_target="tpu_custom_call" | custom-call | flops 10000000000 | bytes 8000000 | tf_op jit(solution)/shard_map/volume_terms/pallas_call | solution.py:615
  20.7 0.0 collective-permute-done.from_pair
  20.7 0.0 collective-permute-done.1.from_ring
  20.7 0.0 collective-permute-done.2.z_pair
  20.7 0.0 collective-permute-done.3.z_ring
  20.7 0.0 copy-done
  20.7 4.7 %finish_first.1 = (f32[6144,128]{1,0:T(8,128)S(1)}, f32[8,96,128]{2,1,0:T(8,128)S(1)}, f32[4,96,128]{2,1,0:T(8,128)S(1)}, f32[4,96,128]{2,1,0:T(8,128)S(1)}, f32...) custom-call(s32[20]{0:T(128)S(4)} %get-tuple-element.22.scalars, ...), custom_call_target="tpu_custom_call", output_to_operand_aliasing={{0}: (2, {})} | custom-call | tf_op jit(solution)/shard_map/finish_first/pallas_call | solution.py:638
  25.5 0.1 collective-permute-start.4
  25.5 1.3 %collective-permute-start.5 = (f32[4,96,128]{2,1,0:T(8,128)S(1)}, f32[4,96,128]{2,1,0:T(8,128)S(1)}, u32[]{:S(2)}, u32[]{:S(2)}) collective-permute-start(f32[4,96,128]{2,1,0:T(8,128)S(1)} %get-tuple-element.38), channel_id=1, source_target_pairs={{4,8},{12,16},{20,24},{28,0},{8,4},{16,12},{24,20},{0,28},{5,9},{1... | collective-permute-start | bytes 589832 | tf_op jit(solution)/shard_map/ppermute | solution.py:585
  26.9 0.0 collective-permute-start.6
  26.9 3.3 %collective-permute-start.7 = (f32[2,3,3,32,128]{4,3,2,1,0:T(8,128)S(1)}, f32[2,3,3,32,128]{4,3,2,1,0:T(8,128)S(1)}, u32[]{:S(2)}, u32[]{:S(2)}) collective-permute-start(f32[2,3,3,32,128]{4,3,2,1,0:T(8,128)S(1)} %get-tuple-element.40), channel_id=1, source_target_pairs={{1,2},{2,1},{5,6},{6,5},{9,10},{10,9},{13,14},{14,13},{17,18},{18,... | collective-permute-start | bytes 884744 | tf_op jit(solution)/shard_map/ppermute | solution.py:583
  30.2 6.6 %volume_and_output.1 = (f32[6144,128]{1,0:T(8,128)S(1)}, f32[2,3,32,4096]{3,2,1,0:T(8,128)}) custom-call(f32[6144,128]{1,0:T(8,128)S(1)} %get-tuple-element.32.field, bf16[96,96]{1,0:T(8,128)(2,1)S(1)} %copy-done.1, bf16[12,768,256]{2,1,0:T(8,128)(2,1)S(1)} %get-tuple-element.25.weights, f32[2,3,32,4096]{3,2,1,0:T(8,128)S(1)} %get-tuple-element.33.rest_0_), custom_call_target="tpu_custom_call" | custom-call | flops 10000000000 | bytes 8000000 | tf_op jit(solution)/shard_map/volume_and_output/pallas_call | solution.py:615
  36.8 0.0 collective-permute-done.4.from_pair
  36.8 0.0 collective-permute-done.5.from_ring
  36.8 0.0 collective-permute-done.6.z_pair
  36.8 0.0 collective-permute-done.7.z_ring
  36.9 4.1 %finish_last.1 = (f32[6144,128]{1,0:T(8,128)S(1)}, f32[2,3,32,4096]{3,2,1,0:T(8,128)}) custom-call(s32[20]{0:T(128)S(4)} %get-tuple-element.22.scalars, f32[8]{0:T(128)S(4)} %get-tuple-element.23.factors, f32[6144,128]{1,0:T(8,128)S(1)} %get-tuple-element.35.volume, f32[8,96,128]{2,1,0:T(8,128)S(1)} %get-tuple-element.36.own, ...), custom_call_target="tpu_custom_call", output_to_operand_aliasing={{0}: (2, {})} | custom-call | tf_op jit(solution)/shard_map/finish_last/pallas_call | solution.py:638
Async XLA Ops:
  0.6 13.4 %copy-start.1 = (bf16[96,96]{1,0:T(8,128)(2,1)S(1)}, bf16[96,96]{1,0:T(8,128)(2,1)}, u32[]{:S(2)}) copy-start(bf16[96,96]{1,0:T(8,128)(2,1)} %constant.2.clone.z_table) | copy-start | bytes 55300
  4.2 16.5 %collective-permute-start = (f32[4,96,128]{2,1,0:T(8,128)S(1)}, f32[4,96,128]{2,1,0:T(8,128)S(1)}, u32[]{:S(2)}, u32[]{:S(2)}) collective-permute-start(f32[4,96,128]{2,1,0:T(8,128)S(1)} %get-tuple-element.27), channel_id=1, source_target_pairs={{0,4},{8,12},{16,20},{24,28},{4,0},{12,8},{20,16},{28,24},{1,5},{9... | collective-permute-start | bytes 589832 | tf_op jit(solution)/shard_map/ppermute | solution.py:584
  6.3 14.4 %collective-permute-start.1 = (f32[4,96,128]{2,1,0:T(8,128)S(1)}, f32[4,96,128]{2,1,0:T(8,128)S(1)}, u32[]{:S(2)}, u32[]{:S(2)}) collective-permute-start(f32[4,96,128]{2,1,0:T(8,128)S(1)} %get-tuple-element.28), channel_id=1, source_target_pairs={{4,8},{12,16},{20,24},{28,0},{8,4},{16,12},{24,20},{0,28},{5,9},{1... | collective-permute-start | bytes 589832 | tf_op jit(solution)/shard_map/ppermute | solution.py:585
  9.6 11.1 %collective-permute-start.2 = (f32[2,3,3,32,128]{4,3,2,1,0:T(8,128)S(1)}, f32[2,3,3,32,128]{4,3,2,1,0:T(8,128)S(1)}, u32[]{:S(2)}, u32[]{:S(2)}) collective-permute-start(f32[2,3,3,32,128]{4,3,2,1,0:T(8,128)S(1)} %get-tuple-element.29), channel_id=1, source_target_pairs={{0,1},{2,3},{1,0},{3,2},{4,5},{6,7},{5,4},{7,6},{8,9},{10,11},{9,8... | collective-permute-start | bytes 884744 | tf_op jit(solution)/shard_map/ppermute | solution.py:582
  10.8 9.9 %collective-permute-start.3 = (f32[2,3,3,32,128]{4,3,2,1,0:T(8,128)S(1)}, f32[2,3,3,32,128]{4,3,2,1,0:T(8,128)S(1)}, u32[]{:S(2)}, u32[]{:S(2)}) collective-permute-start(f32[2,3,3,32,128]{4,3,2,1,0:T(8,128)S(1)} %get-tuple-element.30), channel_id=1, source_target_pairs={{1,2},{2,1},{5,6},{6,5},{9,10},{10,9},{13,14},{14,13},{17,18},{18,... | collective-permute-start | bytes 884744 | tf_op jit(solution)/shard_map/ppermute | solution.py:583
  14.1 6.7 %copy-start = (f32[2,4,64,64]{3,2,1,0:T(8,128)S(1)}, f32[2,4,64,64]{3,2,1,0:T(8,128)}, u32[]{:S(2)}) copy-start(f32[2,4,64,64]{3,2,1,0:T(8,128)} %transfer.3) | copy-start | bytes 393220
  25.5 11.4 %collective-permute-start.4 = (f32[4,96,128]{2,1,0:T(8,128)S(1)}, f32[4,96,128]{2,1,0:T(8,128)S(1)}, u32[]{:S(2)}, u32[]{:S(2)}) collective-permute-start(f32[4,96,128]{2,1,0:T(8,128)S(1)} %get-tuple-element.37), channel_id=1, source_target_pairs={{0,4},{8,12},{16,20},{24,28},{4,0},{12,8},{20,16},{28,24},{1,5},{9... | collective-permute-start | bytes 589832 | tf_op jit(solution)/shard_map/ppermute | solution.py:584
  25.5 11.3 %collective-permute-start.5 = (f32[4,96,128]{2,1,0:T(8,128)S(1)}, f32[4,96,128]{2,1,0:T(8,128)S(1)}, u32[]{:S(2)}, u32[]{:S(2)}) collective-permute-start(f32[4,96,128]{2,1,0:T(8,128)S(1)} %get-tuple-element.38), channel_id=1, source_target_pairs={{4,8},{12,16},{20,24},{28,0},{8,4},{16,12},{24,20},{0,28},{5,9},{1... | collective-permute-start | bytes 589832 | tf_op jit(solution)/shard_map/ppermute | solution.py:585
  26.9 10.0 %collective-permute-start.6 = (f32[2,3,3,32,128]{4,3,2,1,0:T(8,128)S(1)}, f32[2,3,3,32,128]{4,3,2,1,0:T(8,128)S(1)}, u32[]{:S(2)}, u32[]{:S(2)}) collective-permute-start(f32[2,3,3,32,128]{4,3,2,1,0:T(8,128)S(1)} %get-tuple-element.39), channel_id=1, source_target_pairs={{0,1},{2,3},{1,0},{3,2},{4,5},{6,7},{5,4},{7,6},{8,9},{10,11},{9,8... | collective-permute-start | bytes 884744 | tf_op jit(solution)/shard_map/ppermute | solution.py:582
  26.9 10.0 %collective-permute-start.7 = (f32[2,3,3,32,128]{4,3,2,1,0:T(8,128)S(1)}, f32[2,3,3,32,128]{4,3,2,1,0:T(8,128)S(1)}, u32[]{:S(2)}, u32[]{:S(2)}) collective-permute-start(f32[2,3,3,32,128]{4,3,2,1,0:T(8,128)S(1)} %get-tuple-element.40), channel_id=1, source_target_pairs={{1,2},{2,1},{5,6},{6,5},{9,10},{10,9},{13,14},{14,13},{17,18},{18,... | collective-permute-start | bytes 884744 | tf_op jit(solution)/shard_map/ppermute | solution.py:583

commit v5 on v4

--- a/solution.py
+++ b/solution.py
@@ -428,14 +428,15 @@
 
 
 def finish_kernel(
-    depth, last, scalars, factors, volume, own, from_pair, from_ring, z_pair, z_ring, transfer, weights, order,
+    depth, last, scalars, factors, volume, own, from_pair, z_ring, from_ring, z_pair, transfer, weights, order,
     field, *rest,
 ):
     if last:
         result_any, edge, result, sems = rest
     else:
         *sends, result, edge = rest
-    even_section = lax.axis_index("sect") % 2 == 0
+    section, sections = lax.axis_index("sect"), lax.axis_size("sect")
+    even_section = section % 2 == 0
     terms = []
     for k in range(2 * FACES):
         slot = scalars[SLOTS + k]
@@ -457,8 +458,11 @@
     for p in range(2):
         fields = {}
         for c in range(COMPS):
-            before = [jnp.where(even_section, z_ring[p, c, d], z_pair[p, c, d]) for d in range(HALO)]
-            after = [jnp.where(even_section, z_pair[p, c, d], z_ring[p, c, d]) for d in range(HALO)]
+            before, after = [], []
+            for d in range(HALO):
+                paired, ringed = z_pair[p, c, d], z_ring[p, c, d]
+                before.append(jnp.where(section == 0, 0.0, jnp.where(even_section, ringed, paired)))
+                after.append(jnp.where(section == sections - 1, 0.0, jnp.where(even_section, paired, ringed)))
             banded = depth_edges(before, after)
             for kind in range(3):
                 fields[(c, kind)] = split(banded[kind])
@@ -579,11 +583,11 @@
 
     def exchange(layers):
         own, to_pair, to_ring, z_pair, z_ring = layers
-        z_pair = lax.ppermute(z_pair, "sect", both_ways([(i, i + 1) for i in range(0, sections - 1, 2)]))
-        z_ring = lax.ppermute(z_ring, "sect", both_ways([(i, i + 1) for i in range(1, sections - 1, 2)]))
+        z_pair = lax.ppermute(z_pair, "sect", both_ways([(i, i + 1) for i in range(0, sections, 2)]))
+        z_ring = lax.ppermute(z_ring, "sect", both_ways([(i, (i + 1) % sections) for i in range(1, sections, 2)]))
         from_pair = lax.ppermute(to_pair, "patch", both_ways([(i, i + 1) for i in range(0, groups, 2)]))
         from_ring = lax.ppermute(to_ring, "patch", both_ways([(i, (i + 1) % groups) for i in range(1, groups, 2)]))
-        return own, from_pair, from_ring, z_pair, z_ring
+        return own, from_pair, z_ring, from_ring, z_pair
 
     field, *layers, weights, order, scalars, factors = pl.pallas_call(
         functools.partial(start_kernel, groups, depth),

time: 41.3 us -> 40.6 us (0.983); the launches traced: 41.1 us -> 39.8 us
  starting transfers between devices: 14.5 us -> 11 us
  waiting for transfers between devices: 0.02 us -> 2.09 us
    ppermute x2, starting transfers between devices: 6.5 us -> 4.17 us  [exchange(): lax.ppermute(z_ring, 'sect', both_ways([(i, (i + 1) % sections) for i in...]
    ppermute x2, waiting for transfers between devices: 0.01 us -> 1.59 us  [exchange(): lax.ppermute(z_ring, 'sect', both_ways([(i, (i + 1) % sections) for i in...]
    ppermute x2, starting transfers between devices: 1.24 us -> 0.01 us  [exchange(): lax.ppermute(z_pair, 'sect', both_ways([(i, i + 1) for i in range(0, sect...]
    ppermute x2, waiting for transfers between devices: 0.01 us -> 0.5 us  [exchange(): lax.ppermute(to_pair, 'patch', both_ways([(i, i + 1) for i in range(0, gr...]
  transfers between devices with their start and end apart: 8 -> 8, of which waited for: 0 -> 3; matrix products, arithmetic and copies ran while one was open for 0% -> 0% of each run, Pallas kernels for 32% -> 33%
where the time goes in v5:
time: 40.6 us; the launch traced here: 39.8 us
  Pallas kernels  25.8 us (64%)
  starting transfers between devices  11 us (27%)
  waiting for transfers between devices  2.09 us (5%)
  between operations  0.86 us (2%)
    pallas_call x2, Pallas kernels, volume(): pl.pallas_call(functools.partial(volume_kernel, depth), out_shape=out_sha...  13.2 us
    pallas_call x2, Pallas kernels, finish(): pl.pallas_call(functools.partial(finish_kernel, depth, last), out_shape=o...  9.03 us
    ppermute x2, starting transfers between devices, exchange(): lax.ppermute(to_ring, 'patch', both_ways([(i, (i + 1) % groups) for i in...  4.64 us
    ppermute x2, starting transfers between devices, exchange(): lax.ppermute(z_ring, 'sect', both_ways([(i, (i + 1) % sections) for i in...  4.17 us
    pallas_call x1, Pallas kernels, shards(): pl.pallas_call(functools.partial(start_kernel, groups, depth), out_shape=...  3.54 us
    ppermute x2, starting transfers between devices, exchange(): lax.ppermute(to_pair, 'patch', both_ways([(i, i + 1) for i in range(0, gr...  2.18 us
    ppermute x2, waiting for transfers between devices, exchange(): lax.ppermute(z_ring, 'sect', both_ways([(i, (i + 1) % sections) for i in...  1.59 us
  transfers between devices with their start and end apart: 8, of which 3 were waited for; matrix products, arithmetic and copies ran while one was open for 0% of the time, Pallas kernels for 33%

profile of v5, /device:TPU:1, one launch (start us, length us, event | category | flops | bytes accessed | tf_op | source)
XLA Modules:
  0.0 39.8 jit_solution(4085352958564501369)
XLA Ops:
  0.6 0.0 copy-start.1
  0.6 3.5 %start_layers.1 = (f32[6144,128]{1,0:T(8,128)S(1)}, f32[8,96,128]{2,1,0:T(8,128)S(1)}, f32[4,96,128]{2,1,0:T(8,128)S(1)}, f32[4,96,128]{2,1,0:T(8,128)S(1)}, f32...) custom-call(s32[2,2]{1,0:T(2,128)} %sizes_any.1, ...), custom_call_target="tpu_custom_call" | custom-call | tf_op jit(solution)/shard_map/start_layers/pallas_call | solution.py:592
  4.2 2.1 %collective-permute-start = (f32[4,96,128]{2,1,0:T(8,128)S(1)}, f32[4,96,128]{2,1,0:T(8,128)S(1)}, u32[]{:S(2)}, u32[]{:S(2)}) collective-permute-start(f32[4,96,128]{2,1,0:T(8,128)S(1)} %get-tuple-element.27), channel_id=1, source_target_pairs={{0,4},{8,12},{16,20},{24,28},{4,0},{12,8},{20,16},{28,24},{1,5},{9... | collective-permute-start | bytes 589832 | tf_op jit(solution)/shard_map/ppermute | solution.py:588
  6.3 3.3 %collective-permute-start.2 = (f32[4,96,128]{2,1,0:T(8,128)S(1)}, f32[4,96,128]{2,1,0:T(8,128)S(1)}, u32[]{:S(2)}, u32[]{:S(2)}) collective-permute-start(f32[4,96,128]{2,1,0:T(8,128)S(1)} %get-tuple-element.29), channel_id=1, source_target_pairs={{4,8},{12,16},{20,24},{28,0},{8,4},{16,12},{24,20},{0,28},{5,9},{1... | collective-permute-start | bytes 589832 | tf_op jit(solution)/shard_map/ppermute | solution.py:589
  9.6 2.4 %collective-permute-start.1 = (f32[2,3,3,32,128]{4,3,2,1,0:T(8,128)S(1)}, f32[2,3,3,32,128]{4,3,2,1,0:T(8,128)S(1)}, u32[]{:S(2)}, u32[]{:S(2)}) collective-permute-start(f32[2,3,3,32,128]{4,3,2,1,0:T(8,128)S(1)} %get-tuple-element.28), channel_id=1, source_target_pairs={{1,2},{3,0},{2,1},{0,3},{5,6},{7,4},{6,5},{4,7},{9,10},{11,8},{10,... | collective-permute-start | bytes 884744 | tf_op jit(solution)/shard_map/ppermute | solution.py:587
  12.0 0.0 collective-permute-start.3
  12.0 0.0 copy-done.1
  12.0 0.0 copy-start
  12.0 6.6 %volume_terms.1.volume = f32[6144,128]{1,0:T(8,128)S(1)} custom-call(f32[6144,128]{1,0:T(8,128)S(1)} %get-tuple-element.24.field, bf16[96,96]{1,0:T(8,128)(2,1)S(1)} %copy-done.1, bf16[12,768,256]{2,1,0:T(8,128)(2,1)S(1)} %get-tuple-element.25.weights), custom_call_target="tpu_custom_call" | custom-call | flops 10000000000 | bytes 8000000 | tf_op jit(solution)/shard_map/volume_terms/pallas_call | solution.py:619
  18.6 0.0 collective-permute-done.from_pair
  18.6 0.0 collective-permute-done.2.from_ring
  18.6 1.1 %collective-permute-done.1.z_ring = f32[2,3,3,32,128]{4,3,2,1,0:T(8,128)S(1)} collective-permute-done((f32[2,3,3,32,128]{4,3,2,1,0:T(8,128)S(1)}, f32[2,3,3,32,128]{4,3,2,1,0:T(8,128)S(1)}, u32[]{:S(2)}, u32[]{:S(2)}) %collective-permute-start.1) | collective-permute-done | bytes 294944 | tf_op jit(solution)/shard_map/ppermute | solution.py:587
  19.7 0.0 collective-permute-done.3.z_pair
  19.7 0.0 copy-done
  19.7 4.9 %finish_first.1 = (f32[6144,128]{1,0:T(8,128)S(1)}, f32[8,96,128]{2,1,0:T(8,128)S(1)}, f32[4,96,128]{2,1,0:T(8,128)S(1)}, f32[4,96,128]{2,1,0:T(8,128)S(1)}, f32...) custom-call(s32[20]{0:T(128)S(4)} %get-tuple-element.22.scalars, ...), custom_call_target="tpu_custom_call", output_to_operand_aliasing={{0}: (2, {})} | custom-call | tf_op jit(solution)/shard_map/finish_first/pallas_call | solution.py:642
  24.6 0.1 collective-permute-start.4
  24.7 1.3 %collective-permute-start.6 = (f32[4,96,128]{2,1,0:T(8,128)S(1)}, f32[4,96,128]{2,1,0:T(8,128)S(1)}, u32[]{:S(2)}, u32[]{:S(2)}) collective-permute-start(f32[4,96,128]{2,1,0:T(8,128)S(1)} %get-tuple-element.39), channel_id=1, source_target_pairs={{4,8},{12,16},{20,24},{28,0},{8,4},{16,12},{24,20},{0,28},{5,9},{1... | collective-permute-start | bytes 589832 | tf_op jit(solution)/shard_map/ppermute | solution.py:589
  26.0 1.8 %collective-permute-start.5 = (f32[2,3,3,32,128]{4,3,2,1,0:T(8,128)S(1)}, f32[2,3,3,32,128]{4,3,2,1,0:T(8,128)S(1)}, u32[]{:S(2)}, u32[]{:S(2)}) collective-permute-start(f32[2,3,3,32,128]{4,3,2,1,0:T(8,128)S(1)} %get-tuple-element.38), channel_id=1, source_target_pairs={{1,2},{3,0},{2,1},{0,3},{5,6},{7,4},{6,5},{4,7},{9,10},{11,8},{10,... | collective-permute-start | bytes 884744 | tf_op jit(solution)/shard_map/ppermute | solution.py:587
  27.9 0.0 collective-permute-start.7
  27.9 6.6 %volume_and_output.1 = (f32[6144,128]{1,0:T(8,128)S(1)}, f32[2,3,32,4096]{3,2,1,0:T(8,128)}) custom-call(f32[6144,128]{1,0:T(8,128)S(1)} %get-tuple-element.32.field, bf16[96,96]{1,0:T(8,128)(2,1)S(1)} %copy-done.1, bf16[12,768,256]{2,1,0:T(8,128)(2,1)S(1)} %get-tuple-element.25.weights, f32[2,3,32,4096]{3,2,1,0:T(8,128)S(1)} %get-tuple-element.33.rest_0_), custom_call_target="tpu_custom_call" | custom-call | flops 10000000000 | bytes 8000000 | tf_op jit(solution)/shard_map/volume_and_output/pallas_call | solution.py:619
  34.5 0.5 %collective-permute-done.4.from_pair = f32[4,96,128]{2,1,0:T(8,128)S(1)} collective-permute-done((f32[4,96,128]{2,1,0:T(8,128)S(1)}, f32[4,96,128]{2,1,0:T(8,128)S(1)}, u32[]{:S(2)}, u32[]{:S(2)}) %collective-permute-start.4) | collective-permute-done | bytes 196640 | tf_op jit(solution)/shard_map/ppermute | solution.py:588
  35.0 0.0 collective-permute-done.6.from_ring
  35.0 0.5 %collective-permute-done.5.z_ring = f32[2,3,3,32,128]{4,3,2,1,0:T(8,128)S(1)} collective-permute-done((f32[2,3,3,32,128]{4,3,2,1,0:T(8,128)S(1)}, f32[2,3,3,32,128]{4,3,2,1,0:T(8,128)S(1)}, u32[]{:S(2)}, u32[]{:S(2)}) %collective-permute-start.5) | collective-permute-done | bytes 294944 | tf_op jit(solution)/shard_map/ppermute | solution.py:587
  35.5 0.0 collective-permute-done.7.z_pair
  35.5 4.1 %finish_last.1 = (f32[6144,128]{1,0:T(8,128)S(1)}, f32[2,3,32,4096]{3,2,1,0:T(8,128)}) custom-call(s32[20]{0:T(128)S(4)} %get-tuple-element.22.scalars, f32[8]{0:T(128)S(4)} %get-tuple-element.23.factors, f32[6144,128]{1,0:T(8,128)S(1)} %get-tuple-element.35.volume, f32[8,96,128]{2,1,0:T(8,128)S(1)} %get-tuple-element.36.own, ...), custom_call_target="tpu_custom_call", output_to_operand_aliasing={{0}: (2, {})} | custom-call | tf_op jit(solution)/shard_map/finish_last/pallas_call | solution.py:642
Async XLA Ops:
  0.6 11.3 %copy-start.1 = (bf16[96,96]{1,0:T(8,128)(2,1)S(1)}, bf16[96,96]{1,0:T(8,128)(2,1)}, u32[]{:S(2)}) copy-start(bf16[96,96]{1,0:T(8,128)(2,1)} %constant.2.clone.z_table) | copy-start | bytes 55300
  4.2 14.4 %collective-permute-start = (f32[4,96,128]{2,1,0:T(8,128)S(1)}, f32[4,96,128]{2,1,0:T(8,128)S(1)}, u32[]{:S(2)}, u32[]{:S(2)}) collective-permute-start(f32[4,96,128]{2,1,0:T(8,128)S(1)} %get-tuple-element.27), channel_id=1, source_target_pairs={{0,4},{8,12},{16,20},{24,28},{4,0},{12,8},{20,16},{28,24},{1,5},{9... | collective-permute-start | bytes 589832 | tf_op jit(solution)/shard_map/ppermute | solution.py:588
  6.3 12.3 %collective-permute-start.2 = (f32[4,96,128]{2,1,0:T(8,128)S(1)}, f32[4,96,128]{2,1,0:T(8,128)S(1)}, u32[]{:S(2)}, u32[]{:S(2)}) collective-permute-start(f32[4,96,128]{2,1,0:T(8,128)S(1)} %get-tuple-element.29), channel_id=1, source_target_pairs={{4,8},{12,16},{20,24},{28,0},{8,4},{16,12},{24,20},{0,28},{5,9},{1... | collective-permute-start | bytes 589832 | tf_op jit(solution)/shard_map/ppermute | solution.py:589
  9.6 10.1 %collective-permute-start.1 = (f32[2,3,3,32,128]{4,3,2,1,0:T(8,128)S(1)}, f32[2,3,3,32,128]{4,3,2,1,0:T(8,128)S(1)}, u32[]{:S(2)}, u32[]{:S(2)}) collective-permute-start(f32[2,3,3,32,128]{4,3,2,1,0:T(8,128)S(1)} %get-tuple-element.28), channel_id=1, source_target_pairs={{1,2},{3,0},{2,1},{0,3},{5,6},{7,4},{6,5},{4,7},{9,10},{11,8},{10,... | collective-permute-start | bytes 884744 | tf_op jit(solution)/shard_map/ppermute | solution.py:587
  12.0 7.7 %collective-permute-start.3 = (f32[2,3,3,32,128]{4,3,2,1,0:T(8,128)S(1)}, f32[2,3,3,32,128]{4,3,2,1,0:T(8,128)S(1)}, u32[]{:S(2)}, u32[]{:S(2)}) collective-permute-start(f32[2,3,3,32,128]{4,3,2,1,0:T(8,128)S(1)} %get-tuple-element.30), channel_id=1, source_target_pairs={{0,1},{2,3},{1,0},{3,2},{4,5},{6,7},{5,4},{7,6},{8,9},{10,11},{9,8... | collective-permute-start | bytes 884744 | tf_op jit(solution)/shard_map/ppermute | solution.py:586
  12.0 7.7 %copy-start = (f32[2,4,64,64]{3,2,1,0:T(8,128)S(1)}, f32[2,4,64,64]{3,2,1,0:T(8,128)}, u32[]{:S(2)}) copy-start(f32[2,4,64,64]{3,2,1,0:T(8,128)} %transfer.3) | copy-start | bytes 393220
  24.6 10.4 %collective-permute-start.4 = (f32[4,96,128]{2,1,0:T(8,128)S(1)}, f32[4,96,128]{2,1,0:T(8,128)S(1)}, u32[]{:S(2)}, u32[]{:S(2)}) collective-permute-start(f32[4,96,128]{2,1,0:T(8,128)S(1)} %get-tuple-element.37), channel_id=1, source_target_pairs={{0,4},{8,12},{16,20},{24,28},{4,0},{12,8},{20,16},{28,24},{1,5},{9... | collective-permute-start | bytes 589832 | tf_op jit(solution)/shard_map/ppermute | solution.py:588
  24.7 10.3 %collective-permute-start.6 = (f32[4,96,128]{2,1,0:T(8,128)S(1)}, f32[4,96,128]{2,1,0:T(8,128)S(1)}, u32[]{:S(2)}, u32[]{:S(2)}) collective-permute-start(f32[4,96,128]{2,1,0:T(8,128)S(1)} %get-tuple-element.39), channel_id=1, source_target_pairs={{4,8},{12,16},{20,24},{28,0},{8,4},{16,12},{24,20},{0,28},{5,9},{1... | collective-permute-start | bytes 589832 | tf_op jit(solution)/shard_map/ppermute | solution.py:589
  26.0 9.5 %collective-permute-start.5 = (f32[2,3,3,32,128]{4,3,2,1,0:T(8,128)S(1)}, f32[2,3,3,32,128]{4,3,2,1,0:T(8,128)S(1)}, u32[]{:S(2)}, u32[]{:S(2)}) collective-permute-start(f32[2,3,3,32,128]{4,3,2,1,0:T(8,128)S(1)} %get-tuple-element.38), channel_id=1, source_target_pairs={{1,2},{3,0},{2,1},{0,3},{5,6},{7,4},{6,5},{4,7},{9,10},{11,8},{10,... | collective-permute-start | bytes 884744 | tf_op jit(solution)/shard_map/ppermute | solution.py:587
  27.9 7.7 %collective-permute-start.7 = (f32[2,3,3,32,128]{4,3,2,1,0:T(8,128)S(1)}, f32[2,3,3,32,128]{4,3,2,1,0:T(8,128)S(1)}, u32[]{:S(2)}, u32[]{:S(2)}) collective-permute-start(f32[2,3,3,32,128]{4,3,2,1,0:T(8,128)S(1)} %get-tuple-element.40), channel_id=1, source_target_pairs={{0,1},{2,3},{1,0},{3,2},{4,5},{6,7},{5,4},{7,6},{8,9},{10,11},{9,8... | collective-permute-start | bytes 884744 | tf_op jit(solution)/shard_map/ppermute | solution.py:586

commit v6 on v5

--- a/solution.py
+++ b/solution.py
@@ -428,7 +428,7 @@
 
 
 def finish_kernel(
-    depth, last, scalars, factors, volume, own, from_pair, z_ring, from_ring, z_pair, transfer, weights, order,
+    depth, last, scalars, factors, volume, own, from_pair, from_ring, z_pair, z_ring, transfer, weights, order,
     field, *rest,
 ):
     if last:
@@ -587,7 +587,7 @@
         z_ring = lax.ppermute(z_ring, "sect", both_ways([(i, (i + 1) % sections) for i in range(1, sections, 2)]))
         from_pair = lax.ppermute(to_pair, "patch", both_ways([(i, i + 1) for i in range(0, groups, 2)]))
         from_ring = lax.ppermute(to_ring, "patch", both_ways([(i, (i + 1) % groups) for i in range(1, groups, 2)]))
-        return own, from_pair, z_ring, from_ring, z_pair
+        return own, from_pair, from_ring, z_pair, z_ring
 
     field, *layers, weights, order, scalars, factors = pl.pallas_call(
         functools.partial(start_kernel, groups, depth),

time: 40.6 us -> 40.4 us (level)
    ppermute x2, starting transfers between devices: 0.01 us -> 2.15 us  [exchange(): lax.ppermute(z_pair, 'sect', both_ways([(i, i + 1) for i in range(0, sect...]
    ppermute x2, starting transfers between devices: 4.17 us -> 2.25 us  [exchange(): lax.ppermute(z_ring, 'sect', both_ways([(i, (i + 1) % sections) for i in...]
where the time goes in v6:
time: 40.4 us; the launch traced here: 39.9 us
  Pallas kernels  25.8 us (64%)
  starting transfers between devices  11.2 us (28%)
  waiting for transfers between devices  1.95 us (5%)
  between operations  0.87 us (2%)
    pallas_call x2, Pallas kernels, volume(): pl.pallas_call(functools.partial(volume_kernel, depth), out_shape=out_sha...  13.2 us
    pallas_call x2, Pallas kernels, finish(): pl.pallas_call(functools.partial(finish_kernel, depth, last), out_shape=o...  9.03 us
    ppermute x2, starting transfers between devices, exchange(): lax.ppermute(to_ring, 'patch', both_ways([(i, (i + 1) % groups) for i in...  4.64 us
    pallas_call x1, Pallas kernels, shards(): pl.pallas_call(functools.partial(start_kernel, groups, depth), out_shape=...  3.55 us
    ppermute x2, starting transfers between devices, exchange(): lax.ppermute(z_ring, 'sect', both_ways([(i, (i + 1) % sections) for i in...  2.25 us
    ppermute x2, starting transfers between devices, exchange(): lax.ppermute(to_pair, 'patch', both_ways([(i, i + 1) for i in range(0, gr...  2.17 us
    ppermute x2, starting transfers between devices, exchange(): lax.ppermute(z_pair, 'sect', both_ways([(i, i + 1) for i in range(0, sect...  2.15 us
    ppermute x2, waiting for transfers between devices, exchange(): lax.ppermute(z_ring, 'sect', both_ways([(i, (i + 1) % sections) for i in...  1.27 us
  transfers between devices with their start and end apart: 8, of which 3 were waited for; matrix products, arithmetic and copies ran while one was open for 0% of the time, Pallas kernels for 33%

profile of v6, /device:TPU:1, one launch (start us, length us, event | category | flops | bytes accessed | tf_op | source)
XLA Modules:
  0.0 39.9 jit_solution(899714406878679901)
XLA Ops:
  0.6 0.0 copy-start.1
  0.6 3.5 %start_layers.1 = (f32[6144,128]{1,0:T(8,128)S(1)}, f32[8,96,128]{2,1,0:T(8,128)S(1)}, f32[4,96,128]{2,1,0:T(8,128)S(1)}, f32[4,96,128]{2,1,0:T(8,128)S(1)}, f32...) custom-call(s32[2,2]{1,0:T(2,128)} %sizes_any.1, ...), custom_call_target="tpu_custom_call" | custom-call | tf_op jit(solution)/shard_map/start_layers/pallas_call | solution.py:592
  4.2 2.1 %collective-permute-start = (f32[4,96,128]{2,1,0:T(8,128)S(1)}, f32[4,96,128]{2,1,0:T(8,128)S(1)}, u32[]{:S(2)}, u32[]{:S(2)}) collective-permute-start(f32[4,96,128]{2,1,0:T(8,128)S(1)} %get-tuple-element.27), channel_id=1, source_target_pairs={{0,4},{8,12},{16,20},{24,28},{4,0},{12,8},{20,16},{28,24},{1,5},{9... | collective-permute-start | bytes 589832 | tf_op jit(solution)/shard_map/ppermute | solution.py:588
  6.3 3.3 %collective-permute-start.1 = (f32[4,96,128]{2,1,0:T(8,128)S(1)}, f32[4,96,128]{2,1,0:T(8,128)S(1)}, u32[]{:S(2)}, u32[]{:S(2)}) collective-permute-start(f32[4,96,128]{2,1,0:T(8,128)S(1)} %get-tuple-element.28), channel_id=1, source_target_pairs={{4,8},{12,16},{20,24},{28,0},{8,4},{16,12},{24,20},{0,28},{5,9},{1... | collective-permute-start | bytes 589832 | tf_op jit(solution)/shard_map/ppermute | solution.py:589
  9.6 1.2 %collective-permute-start.2 = (f32[2,3,3,32,128]{4,3,2,1,0:T(8,128)S(1)}, f32[2,3,3,32,128]{4,3,2,1,0:T(8,128)S(1)}, u32[]{:S(2)}, u32[]{:S(2)}) collective-permute-start(f32[2,3,3,32,128]{4,3,2,1,0:T(8,128)S(1)} %get-tuple-element.29), channel_id=1, source_target_pairs={{0,1},{2,3},{1,0},{3,2},{4,5},{6,7},{5,4},{7,6},{8,9},{10,11},{9,8... | collective-permute-start | bytes 884744 | tf_op jit(solution)/shard_map/ppermute | solution.py:586
  10.8 1.1 %collective-permute-start.3 = (f32[2,3,3,32,128]{4,3,2,1,0:T(8,128)S(1)}, f32[2,3,3,32,128]{4,3,2,1,0:T(8,128)S(1)}, u32[]{:S(2)}, u32[]{:S(2)}) collective-permute-start(f32[2,3,3,32,128]{4,3,2,1,0:T(8,128)S(1)} %get-tuple-element.30), channel_id=1, source_target_pairs={{1,2},{3,0},{2,1},{0,3},{5,6},{7,4},{6,5},{4,7},{9,10},{11,8},{10,... | collective-permute-start | bytes 884744 | tf_op jit(solution)/shard_map/ppermute | solution.py:587
  12.0 0.0 copy-done.1
  12.0 0.0 copy-start
  12.0 6.6 %volume_terms.1.volume = f32[6144,128]{1,0:T(8,128)S(1)} custom-call(f32[6144,128]{1,0:T(8,128)S(1)} %get-tuple-element.24.field, bf16[96,96]{1,0:T(8,128)(2,1)S(1)} %copy-done.1, bf16[12,768,256]{2,1,0:T(8,128)(2,1)S(1)} %get-tuple-element.25.weights), custom_call_target="tpu_custom_call" | custom-call | flops 10000000000 | bytes 8000000 | tf_op jit(solution)/shard_map/volume_terms/pallas_call | solution.py:619
  18.6 0.0 collective-permute-done.from_pair
  18.6 0.0 collective-permute-done.1.from_ring
  18.6 0.0 collective-permute-done.2.z_pair
  18.6 0.8 %collective-permute-done.3.z_ring = f32[2,3,3,32,128]{4,3,2,1,0:T(8,128)S(1)} collective-permute-done((f32[2,3,3,32,128]{4,3,2,1,0:T(8,128)S(1)}, f32[2,3,3,32,128]{4,3,2,1,0:T(8,128)S(1)}, u32[]{:S(2)}, u32[]{:S(2)}) %collective-permute-start.3) | collective-permute-done | bytes 294944 | tf_op jit(solution)/shard_map/ppermute | solution.py:587
  19.5 0.0 copy-done
  19.5 4.9 %finish_first.1 = (f32[6144,128]{1,0:T(8,128)S(1)}, f32[8,96,128]{2,1,0:T(8,128)S(1)}, f32[4,96,128]{2,1,0:T(8,128)S(1)}, f32[4,96,128]{2,1,0:T(8,128)S(1)}, f32...) custom-call(s32[20]{0:T(128)S(4)} %get-tuple-element.22.scalars, ...), custom_call_target="tpu_custom_call", output_to_operand_aliasing={{0}: (2, {})} | custom-call | tf_op jit(solution)/shard_map/finish_first/pallas_call | solution.py:642
  24.4 0.1 collective-permute-start.4
  24.5 1.3 %collective-permute-start.5 = (f32[4,96,128]{2,1,0:T(8,128)S(1)}, f32[4,96,128]{2,1,0:T(8,128)S(1)}, u32[]{:S(2)}, u32[]{:S(2)}) collective-permute-start(f32[4,96,128]{2,1,0:T(8,128)S(1)} %get-tuple-element.38), channel_id=1, source_target_pairs={{4,8},{12,16},{20,24},{28,0},{8,4},{16,12},{24,20},{0,28},{5,9},{1... | collective-permute-start | bytes 589832 | tf_op jit(solution)/shard_map/ppermute | solution.py:589
  25.8 0.9 %collective-permute-start.6 = (f32[2,3,3,32,128]{4,3,2,1,0:T(8,128)S(1)}, f32[2,3,3,32,128]{4,3,2,1,0:T(8,128)S(1)}, u32[]{:S(2)}, u32[]{:S(2)}) collective-permute-start(f32[2,3,3,32,128]{4,3,2,1,0:T(8,128)S(1)} %get-tuple-element.39), channel_id=1, source_target_pairs={{0,1},{2,3},{1,0},{3,2},{4,5},{6,7},{5,4},{7,6},{8,9},{10,11},{9,8... | collective-permute-start | bytes 884744 | tf_op jit(solution)/shard_map/ppermute | solution.py:586
  26.7 1.1 %collective-permute-start.7 = (f32[2,3,3,32,128]{4,3,2,1,0:T(8,128)S(1)}, f32[2,3,3,32,128]{4,3,2,1,0:T(8,128)S(1)}, u32[]{:S(2)}, u32[]{:S(2)}) collective-permute-start(f32[2,3,3,32,128]{4,3,2,1,0:T(8,128)S(1)} %get-tuple-element.40), channel_id=1, source_target_pairs={{1,2},{3,0},{2,1},{0,3},{5,6},{7,4},{6,5},{4,7},{9,10},{11,8},{10,... | collective-permute-start | bytes 884744 | tf_op jit(solution)/shard_map/ppermute | solution.py:587
  27.9 6.6 %volume_and_output.1 = (f32[6144,128]{1,0:T(8,128)S(1)}, f32[2,3,32,4096]{3,2,1,0:T(8,128)}) custom-call(f32[6144,128]{1,0:T(8,128)S(1)} %get-tuple-element.32.field, bf16[96,96]{1,0:T(8,128)(2,1)S(1)} %copy-done.1, bf16[12,768,256]{2,1,0:T(8,128)(2,1)S(1)} %get-tuple-element.25.weights, f32[2,3,32,4096]{3,2,1,0:T(8,128)S(1)} %get-tuple-element.33.rest_0_), custom_call_target="tpu_custom_call" | custom-call | flops 10000000000 | bytes 8000000 | tf_op jit(solution)/shard_map/volume_and_output/pallas_call | solution.py:619
  34.5 0.7 %collective-permute-done.4.from_pair = f32[4,96,128]{2,1,0:T(8,128)S(1)} collective-permute-done((f32[4,96,128]{2,1,0:T(8,128)S(1)}, f32[4,96,128]{2,1,0:T(8,128)S(1)}, u32[]{:S(2)}, u32[]{:S(2)}) %collective-permute-start.4) | collective-permute-done | bytes 196640 | tf_op jit(solution)/shard_map/ppermute | solution.py:588
  35.2 0.0 collective-permute-done.5.from_ring
  35.2 0.0 collective-permute-done.6.z_pair
  35.2 0.4 %collective-permute-done.7.z_ring = f32[2,3,3,32,128]{4,3,2,1,0:T(8,128)S(1)} collective-permute-done((f32[2,3,3,32,128]{4,3,2,1,0:T(8,128)S(1)}, f32[2,3,3,32,128]{4,3,2,1,0:T(8,128)S(1)}, u32[]{:S(2)}, u32[]{:S(2)}) %collective-permute-start.7) | collective-permute-done | bytes 294944 | tf_op jit(solution)/shard_map/ppermute | solution.py:587
  35.6 4.1 %finish_last.1 = (f32[6144,128]{1,0:T(8,128)S(1)}, f32[2,3,32,4096]{3,2,1,0:T(8,128)}) custom-call(s32[20]{0:T(128)S(4)} %get-tuple-element.22.scalars, f32[8]{0:T(128)S(4)} %get-tuple-element.23.factors, f32[6144,128]{1,0:T(8,128)S(1)} %get-tuple-element.35.volume, f32[8,96,128]{2,1,0:T(8,128)S(1)} %get-tuple-element.36.own, ...), custom_call_target="tpu_custom_call", output_to_operand_aliasing={{0}: (2, {})} | custom-call | tf_op jit(solution)/shard_map/finish_last/pallas_call | solution.py:642
Async XLA Ops:
  0.6 11.3 %copy-start.1 = (bf16[96,96]{1,0:T(8,128)(2,1)S(1)}, bf16[96,96]{1,0:T(8,128)(2,1)}, u32[]{:S(2)}) copy-start(bf16[96,96]{1,0:T(8,128)(2,1)} %constant.2.clone.z_table) | copy-start | bytes 55300
  4.2 14.4 %collective-permute-start = (f32[4,96,128]{2,1,0:T(8,128)S(1)}, f32[4,96,128]{2,1,0:T(8,128)S(1)}, u32[]{:S(2)}, u32[]{:S(2)}) collective-permute-start(f32[4,96,128]{2,1,0:T(8,128)S(1)} %get-tuple-element.27), channel_id=1, source_target_pairs={{0,4},{8,12},{16,20},{24,28},{4,0},{12,8},{20,16},{28,24},{1,5},{9... | collective-permute-start | bytes 589832 | tf_op jit(solution)/shard_map/ppermute | solution.py:588
  6.3 12.3 %collective-permute-start.1 = (f32[4,96,128]{2,1,0:T(8,128)S(1)}, f32[4,96,128]{2,1,0:T(8,128)S(1)}, u32[]{:S(2)}, u32[]{:S(2)}) collective-permute-start(f32[4,96,128]{2,1,0:T(8,128)S(1)} %get-tuple-element.28), channel_id=1, source_target_pairs={{4,8},{12,16},{20,24},{28,0},{8,4},{16,12},{24,20},{0,28},{5,9},{1... | collective-permute-start | bytes 589832 | tf_op jit(solution)/shard_map/ppermute | solution.py:589
  9.6 9.0 %collective-permute-start.2 = (f32[2,3,3,32,128]{4,3,2,1,0:T(8,128)S(1)}, f32[2,3,3,32,128]{4,3,2,1,0:T(8,128)S(1)}, u32[]{:S(2)}, u32[]{:S(2)}) collective-permute-start(f32[2,3,3,32,128]{4,3,2,1,0:T(8,128)S(1)} %get-tuple-element.29), channel_id=1, source_target_pairs={{0,1},{2,3},{1,0},{3,2},{4,5},{6,7},{5,4},{7,6},{8,9},{10,11},{9,8... | collective-permute-start | bytes 884744 | tf_op jit(solution)/shard_map/ppermute | solution.py:586
  10.8 8.6 %collective-permute-start.3 = (f32[2,3,3,32,128]{4,3,2,1,0:T(8,128)S(1)}, f32[2,3,3,32,128]{4,3,2,1,0:T(8,128)S(1)}, u32[]{:S(2)}, u32[]{:S(2)}) collective-permute-start(f32[2,3,3,32,128]{4,3,2,1,0:T(8,128)S(1)} %get-tuple-element.30), channel_id=1, source_target_pairs={{1,2},{3,0},{2,1},{0,3},{5,6},{7,4},{6,5},{4,7},{9,10},{11,8},{10,... | collective-permute-start | bytes 884744 | tf_op jit(solution)/shard_map/ppermute | solution.py:587
  12.0 7.5 %copy-start = (f32[2,4,64,64]{3,2,1,0:T(8,128)S(1)}, f32[2,4,64,64]{3,2,1,0:T(8,128)}, u32[]{:S(2)}) copy-start(f32[2,4,64,64]{3,2,1,0:T(8,128)} %transfer.3) | copy-start | bytes 393220
  24.4 10.8 %collective-permute-start.4 = (f32[4,96,128]{2,1,0:T(8,128)S(1)}, f32[4,96,128]{2,1,0:T(8,128)S(1)}, u32[]{:S(2)}, u32[]{:S(2)}) collective-permute-start(f32[4,96,128]{2,1,0:T(8,128)S(1)} %get-tuple-element.37), channel_id=1, source_target_pairs={{0,4},{8,12},{16,20},{24,28},{4,0},{12,8},{20,16},{28,24},{1,5},{9... | collective-permute-start | bytes 589832 | tf_op jit(solution)/shard_map/ppermute | solution.py:588
  24.5 10.7 %collective-permute-start.5 = (f32[4,96,128]{2,1,0:T(8,128)S(1)}, f32[4,96,128]{2,1,0:T(8,128)S(1)}, u32[]{:S(2)}, u32[]{:S(2)}) collective-permute-start(f32[4,96,128]{2,1,0:T(8,128)S(1)} %get-tuple-element.38), channel_id=1, source_target_pairs={{4,8},{12,16},{20,24},{28,0},{8,4},{16,12},{24,20},{0,28},{5,9},{1... | collective-permute-start | bytes 589832 | tf_op jit(solution)/shard_map/ppermute | solution.py:589
  25.8 9.3 %collective-permute-start.6 = (f32[2,3,3,32,128]{4,3,2,1,0:T(8,128)S(1)}, f32[2,3,3,32,128]{4,3,2,1,0:T(8,128)S(1)}, u32[]{:S(2)}, u32[]{:S(2)}) collective-permute-start(f32[2,3,3,32,128]{4,3,2,1,0:T(8,128)S(1)} %get-tuple-element.39), channel_id=1, source_target_pairs={{0,1},{2,3},{1,0},{3,2},{4,5},{6,7},{5,4},{7,6},{8,9},{10,11},{9,8... | collective-permute-start | bytes 884744 | tf_op jit(solution)/shard_map/ppermute | solution.py:586
  26.7 8.9 %collective-permute-start.7 = (f32[2,3,3,32,128]{4,3,2,1,0:T(8,128)S(1)}, f32[2,3,3,32,128]{4,3,2,1,0:T(8,128)S(1)}, u32[]{:S(2)}, u32[]{:S(2)}) collective-permute-start(f32[2,3,3,32,128]{4,3,2,1,0:T(8,128)S(1)} %get-tuple-element.40), channel_id=1, source_target_pairs={{1,2},{3,0},{2,1},{0,3},{5,6},{7,4},{6,5},{4,7},{9,10},{11,8},{10,... | collective-permute-start | bytes 884744 | tf_op jit(solution)/shard_map/ppermute | solution.py:587

commit v7 on v6

--- a/solution.py
+++ b/solution.py
@@ -569,7 +569,7 @@
     def params(mib):
         return pltpu.CompilerParams(vmem_limit_bytes=mib * MIB)
 
-    field_shape = shape(rows, LANES)
+    field_shape = shape(rows + depth, LANES)
     layer_shapes = (
         shape(2 * FACES, per, LANES),
         shape(FACES, per, LANES),

time: 40.4 us -> 40.4 us (level)
  no operation moved by 1% of the time
where the time goes in v7:
time: 40.4 us; the launch traced here: 39.9 us
  Pallas kernels  25.8 us (64%)
  starting transfers between devices  11.2 us (28%)
  waiting for transfers between devices  1.96 us (5%)
  between operations  0.87 us (2%)
    pallas_call x2, Pallas kernels, volume(): pl.pallas_call(functools.partial(volume_kernel, depth), out_shape=out_sha...  13.2 us
    pallas_call x2, Pallas kernels, finish(): pl.pallas_call(functools.partial(finish_kernel, depth, last), out_shape=o...  9.04 us
    ppermute x2, starting transfers between devices, exchange(): lax.ppermute(to_ring, 'patch', both_ways([(i, (i + 1) % groups) for i in...  4.63 us
    pallas_call x1, Pallas kernels, shards(): pl.pallas_call(functools.partial(start_kernel, groups, depth), out_shape=...  3.55 us
    ppermute x2, starting transfers between devices, exchange(): lax.ppermute(z_ring, 'sect', both_ways([(i, (i + 1) % sections) for i in...  2.26 us
    ppermute x2, starting transfers between devices, exchange(): lax.ppermute(to_pair, 'patch', both_ways([(i, i + 1) for i in range(0, gr...  2.18 us
    ppermute x2, starting transfers between devices, exchange(): lax.ppermute(z_pair, 'sect', both_ways([(i, i + 1) for i in range(0, sect...  2.14 us
    ppermute x2, waiting for transfers between devices, exchange(): lax.ppermute(z_ring, 'sect', both_ways([(i, (i + 1) % sections) for i in...  1.26 us
  transfers between devices with their start and end apart: 8, of which 3 were waited for; matrix products, arithmetic and copies ran while one was open for 0% of the time, Pallas kernels for 33%

profile of v7, /device:TPU:1, one launch (start us, length us, event | category | flops | bytes accessed | tf_op | source)
XLA Modules:
  0.0 39.9 jit_solution(1707424275650809092)
XLA Ops:
  0.6 0.0 copy-start.1
  0.6 3.5 %start_layers.1 = (f32[6176,128]{1,0:T(8,128)S(1)}, f32[8,96,128]{2,1,0:T(8,128)S(1)}, f32[4,96,128]{2,1,0:T(8,128)S(1)}, f32[4,96,128]{2,1,0:T(8,128)S(1)}, f32...) custom-call(s32[2,2]{1,0:T(2,128)} %sizes_any.1, ...), custom_call_target="tpu_custom_call" | custom-call | tf_op jit(solution)/shard_map/start_layers/pallas_call | solution.py:592
  4.2 2.1 %collective-permute-start = (f32[4,96,128]{2,1,0:T(8,128)S(1)}, f32[4,96,128]{2,1,0:T(8,128)S(1)}, u32[]{:S(2)}, u32[]{:S(2)}) collective-permute-start(f32[4,96,128]{2,1,0:T(8,128)S(1)} %get-tuple-element.27), channel_id=1, source_target_pairs={{0,4},{8,12},{16,20},{24,28},{4,0},{12,8},{20,16},{28,24},{1,5},{9... | collective-permute-start | bytes 589832 | tf_op jit(solution)/shard_map/ppermute | solution.py:588
  6.3 3.3 %collective-permute-start.1 = (f32[4,96,128]{2,1,0:T(8,128)S(1)}, f32[4,96,128]{2,1,0:T(8,128)S(1)}, u32[]{:S(2)}, u32[]{:S(2)}) collective-permute-start(f32[4,96,128]{2,1,0:T(8,128)S(1)} %get-tuple-element.28), channel_id=1, source_target_pairs={{4,8},{12,16},{20,24},{28,0},{8,4},{16,12},{24,20},{0,28},{5,9},{1... | collective-permute-start | bytes 589832 | tf_op jit(solution)/shard_map/ppermute | solution.py:589
  9.6 1.2 %collective-permute-start.2 = (f32[2,3,3,32,128]{4,3,2,1,0:T(8,128)S(1)}, f32[2,3,3,32,128]{4,3,2,1,0:T(8,128)S(1)}, u32[]{:S(2)}, u32[]{:S(2)}) collective-permute-start(f32[2,3,3,32,128]{4,3,2,1,0:T(8,128)S(1)} %get-tuple-element.29), channel_id=1, source_target_pairs={{0,1},{2,3},{1,0},{3,2},{4,5},{6,7},{5,4},{7,6},{8,9},{10,11},{9,8... | collective-permute-start | bytes 884744 | tf_op jit(solution)/shard_map/ppermute | solution.py:586
  10.8 1.1 %collective-permute-start.3 = (f32[2,3,3,32,128]{4,3,2,1,0:T(8,128)S(1)}, f32[2,3,3,32,128]{4,3,2,1,0:T(8,128)S(1)}, u32[]{:S(2)}, u32[]{:S(2)}) collective-permute-start(f32[2,3,3,32,128]{4,3,2,1,0:T(8,128)S(1)} %get-tuple-element.30), channel_id=1, source_target_pairs={{1,2},{3,0},{2,1},{0,3},{5,6},{7,4},{6,5},{4,7},{9,10},{11,8},{10,... | collective-permute-start | bytes 884744 | tf_op jit(solution)/shard_map/ppermute | solution.py:587
  12.0 0.0 copy-done.1
  12.0 0.0 copy-start
  12.0 6.6 %volume_terms.1.volume = f32[6176,128]{1,0:T(8,128)S(1)} custom-call(f32[6176,128]{1,0:T(8,128)S(1)} %get-tuple-element.24.field, bf16[96,96]{1,0:T(8,128)(2,1)S(1)} %copy-done.1, bf16[12,768,256]{2,1,0:T(8,128)(2,1)S(1)} %get-tuple-element.25.weights), custom_call_target="tpu_custom_call" | custom-call | flops 10000000000 | bytes 8000000 | tf_op jit(solution)/shard_map/volume_terms/pallas_call | solution.py:619
  18.6 0.0 collective-permute-done.from_pair
  18.6 0.0 collective-permute-done.1.from_ring
  18.6 0.0 collective-permute-done.2.z_pair
  18.6 0.8 %collective-permute-done.3.z_ring = f32[2,3,3,32,128]{4,3,2,1,0:T(8,128)S(1)} collective-permute-done((f32[2,3,3,32,128]{4,3,2,1,0:T(8,128)S(1)}, f32[2,3,3,32,128]{4,3,2,1,0:T(8,128)S(1)}, u32[]{:S(2)}, u32[]{:S(2)}) %collective-permute-start.3) | collective-permute-done | bytes 294944 | tf_op jit(solution)/shard_map/ppermute | solution.py:587
  19.5 0.0 copy-done
  19.5 4.9 %finish_first.1 = (f32[6176,128]{1,0:T(8,128)S(1)}, f32[8,96,128]{2,1,0:T(8,128)S(1)}, f32[4,96,128]{2,1,0:T(8,128)S(1)}, f32[4,96,128]{2,1,0:T(8,128)S(1)}, f32...) custom-call(s32[20]{0:T(128)S(4)} %get-tuple-element.22.scalars, ...), custom_call_target="tpu_custom_call", output_to_operand_aliasing={{0}: (2, {})} | custom-call | tf_op jit(solution)/shard_map/finish_first/pallas_call | solution.py:642
  24.4 0.1 collective-permute-start.4
  24.5 1.3 %collective-permute-start.5 = (f32[4,96,128]{2,1,0:T(8,128)S(1)}, f32[4,96,128]{2,1,0:T(8,128)S(1)}, u32[]{:S(2)}, u32[]{:S(2)}) collective-permute-start(f32[4,96,128]{2,1,0:T(8,128)S(1)} %get-tuple-element.38), channel_id=1, source_target_pairs={{4,8},{12,16},{20,24},{28,0},{8,4},{16,12},{24,20},{0,28},{5,9},{1... | collective-permute-start | bytes 589832 | tf_op jit(solution)/shard_map/ppermute | solution.py:589
  25.8 0.9 %collective-permute-start.6 = (f32[2,3,3,32,128]{4,3,2,1,0:T(8,128)S(1)}, f32[2,3,3,32,128]{4,3,2,1,0:T(8,128)S(1)}, u32[]{:S(2)}, u32[]{:S(2)}) collective-permute-start(f32[2,3,3,32,128]{4,3,2,1,0:T(8,128)S(1)} %get-tuple-element.39), channel_id=1, source_target_pairs={{0,1},{2,3},{1,0},{3,2},{4,5},{6,7},{5,4},{7,6},{8,9},{10,11},{9,8... | collective-permute-start | bytes 884744 | tf_op jit(solution)/shard_map/ppermute | solution.py:586
  26.7 1.1 %collective-permute-start.7 = (f32[2,3,3,32,128]{4,3,2,1,0:T(8,128)S(1)}, f32[2,3,3,32,128]{4,3,2,1,0:T(8,128)S(1)}, u32[]{:S(2)}, u32[]{:S(2)}) collective-permute-start(f32[2,3,3,32,128]{4,3,2,1,0:T(8,128)S(1)} %get-tuple-element.40), channel_id=1, source_target_pairs={{1,2},{3,0},{2,1},{0,3},{5,6},{7,4},{6,5},{4,7},{9,10},{11,8},{10,... | collective-permute-start | bytes 884744 | tf_op jit(solution)/shard_map/ppermute | solution.py:587
  27.9 6.6 %volume_and_output.1 = (f32[6176,128]{1,0:T(8,128)S(1)}, f32[2,3,32,4096]{3,2,1,0:T(8,128)}) custom-call(f32[6176,128]{1,0:T(8,128)S(1)} %get-tuple-element.32.field, bf16[96,96]{1,0:T(8,128)(2,1)S(1)} %copy-done.1, bf16[12,768,256]{2,1,0:T(8,128)(2,1)S(1)} %get-tuple-element.25.weights, f32[2,3,32,4096]{3,2,1,0:T(8,128)S(1)} %get-tuple-element.33.rest_0_), custom_call_target="tpu_custom_call" | custom-call | flops 10000000000 | bytes 8000000 | tf_op jit(solution)/shard_map/volume_and_output/pallas_call | solution.py:619
  34.5 0.7 %collective-permute-done.4.from_pair = f32[4,96,128]{2,1,0:T(8,128)S(1)} collective-permute-done((f32[4,96,128]{2,1,0:T(8,128)S(1)}, f32[4,96,128]{2,1,0:T(8,128)S(1)}, u32[]{:S(2)}, u32[]{:S(2)}) %collective-permute-start.4) | collective-permute-done | bytes 196640 | tf_op jit(solution)/shard_map/ppermute | solution.py:588
  35.2 0.0 collective-permute-done.5.from_ring
  35.2 0.0 collective-permute-done.6.z_pair
  35.2 0.4 %collective-permute-done.7.z_ring = f32[2,3,3,32,128]{4,3,2,1,0:T(8,128)S(1)} collective-permute-done((f32[2,3,3,32,128]{4,3,2,1,0:T(8,128)S(1)}, f32[2,3,3,32,128]{4,3,2,1,0:T(8,128)S(1)}, u32[]{:S(2)}, u32[]{:S(2)}) %collective-permute-start.7) | collective-permute-done | bytes 294944 | tf_op jit(solution)/shard_map/ppermute | solution.py:587
  35.6 4.1 %finish_last.1 = (f32[6176,128]{1,0:T(8,128)S(1)}, f32[2,3,32,4096]{3,2,1,0:T(8,128)}) custom-call(s32[20]{0:T(128)S(4)} %get-tuple-element.22.scalars, f32[8]{0:T(128)S(4)} %get-tuple-element.23.factors, f32[6176,128]{1,0:T(8,128)S(1)} %get-tuple-element.35.volume, f32[8,96,128]{2,1,0:T(8,128)S(1)} %get-tuple-element.36.own, ...), custom_call_target="tpu_custom_call", output_to_operand_aliasing={{0}: (2, {})} | custom-call | tf_op jit(solution)/shard_map/finish_last/pallas_call | solution.py:642
Async XLA Ops:
  0.6 11.3 %copy-start.1 = (bf16[96,96]{1,0:T(8,128)(2,1)S(1)}, bf16[96,96]{1,0:T(8,128)(2,1)}, u32[]{:S(2)}) copy-start(bf16[96,96]{1,0:T(8,128)(2,1)} %constant.2.clone.z_table) | copy-start | bytes 55300
  4.2 14.4 %collective-permute-start = (f32[4,96,128]{2,1,0:T(8,128)S(1)}, f32[4,96,128]{2,1,0:T(8,128)S(1)}, u32[]{:S(2)}, u32[]{:S(2)}) collective-permute-start(f32[4,96,128]{2,1,0:T(8,128)S(1)} %get-tuple-element.27), channel_id=1, source_target_pairs={{0,4},{8,12},{16,20},{24,28},{4,0},{12,8},{20,16},{28,24},{1,5},{9... | collective-permute-start | bytes 589832 | tf_op jit(solution)/shard_map/ppermute | solution.py:588
  6.3 12.3 %collective-permute-start.1 = (f32[4,96,128]{2,1,0:T(8,128)S(1)}, f32[4,96,128]{2,1,0:T(8,128)S(1)}, u32[]{:S(2)}, u32[]{:S(2)}) collective-permute-start(f32[4,96,128]{2,1,0:T(8,128)S(1)} %get-tuple-element.28), channel_id=1, source_target_pairs={{4,8},{12,16},{20,24},{28,0},{8,4},{16,12},{24,20},{0,28},{5,9},{1... | collective-permute-start | bytes 589832 | tf_op jit(solution)/shard_map/ppermute | solution.py:589
  9.6 9.0 %collective-permute-start.2 = (f32[2,3,3,32,128]{4,3,2,1,0:T(8,128)S(1)}, f32[2,3,3,32,128]{4,3,2,1,0:T(8,128)S(1)}, u32[]{:S(2)}, u32[]{:S(2)}) collective-permute-start(f32[2,3,3,32,128]{4,3,2,1,0:T(8,128)S(1)} %get-tuple-element.29), channel_id=1, source_target_pairs={{0,1},{2,3},{1,0},{3,2},{4,5},{6,7},{5,4},{7,6},{8,9},{10,11},{9,8... | collective-permute-start | bytes 884744 | tf_op jit(solution)/shard_map/ppermute | solution.py:586
  10.8 8.6 %collective-permute-start.3 = (f32[2,3,3,32,128]{4,3,2,1,0:T(8,128)S(1)}, f32[2,3,3,32,128]{4,3,2,1,0:T(8,128)S(1)}, u32[]{:S(2)}, u32[]{:S(2)}) collective-permute-start(f32[2,3,3,32,128]{4,3,2,1,0:T(8,128)S(1)} %get-tuple-element.30), channel_id=1, source_target_pairs={{1,2},{3,0},{2,1},{0,3},{5,6},{7,4},{6,5},{4,7},{9,10},{11,8},{10,... | collective-permute-start | bytes 884744 | tf_op jit(solution)/shard_map/ppermute | solution.py:587
  12.0 7.5 %copy-start = (f32[2,4,64,64]{3,2,1,0:T(8,128)S(1)}, f32[2,4,64,64]{3,2,1,0:T(8,128)}, u32[]{:S(2)}) copy-start(f32[2,4,64,64]{3,2,1,0:T(8,128)} %transfer.3) | copy-start | bytes 393220
  24.4 10.8 %collective-permute-start.4 = (f32[4,96,128]{2,1,0:T(8,128)S(1)}, f32[4,96,128]{2,1,0:T(8,128)S(1)}, u32[]{:S(2)}, u32[]{:S(2)}) collective-permute-start(f32[4,96,128]{2,1,0:T(8,128)S(1)} %get-tuple-element.37), channel_id=1, source_target_pairs={{0,4},{8,12},{16,20},{24,28},{4,0},{12,8},{20,16},{28,24},{1,5},{9... | collective-permute-start | bytes 589832 | tf_op jit(solution)/shard_map/ppermute | solution.py:588
  24.5 10.7 %collective-permute-start.5 = (f32[4,96,128]{2,1,0:T(8,128)S(1)}, f32[4,96,128]{2,1,0:T(8,128)S(1)}, u32[]{:S(2)}, u32[]{:S(2)}) collective-permute-start(f32[4,96,128]{2,1,0:T(8,128)S(1)} %get-tuple-element.38), channel_id=1, source_target_pairs={{4,8},{12,16},{20,24},{28,0},{8,4},{16,12},{24,20},{0,28},{5,9},{1... | collective-permute-start | bytes 589832 | tf_op jit(solution)/shard_map/ppermute | solution.py:589
  25.8 9.4 %collective-permute-start.6 = (f32[2,3,3,32,128]{4,3,2,1,0:T(8,128)S(1)}, f32[2,3,3,32,128]{4,3,2,1,0:T(8,128)S(1)}, u32[]{:S(2)}, u32[]{:S(2)}) collective-permute-start(f32[2,3,3,32,128]{4,3,2,1,0:T(8,128)S(1)} %get-tuple-element.39), channel_id=1, source_target_pairs={{0,1},{2,3},{1,0},{3,2},{4,5},{6,7},{5,4},{7,6},{8,9},{10,11},{9,8... | collective-permute-start | bytes 884744 | tf_op jit(solution)/shard_map/ppermute | solution.py:586
  26.7 8.9 %collective-permute-start.7 = (f32[2,3,3,32,128]{4,3,2,1,0:T(8,128)S(1)}, f32[2,3,3,32,128]{4,3,2,1,0:T(8,128)S(1)}, u32[]{:S(2)}, u32[]{:S(2)}) collective-permute-start(f32[2,3,3,32,128]{4,3,2,1,0:T(8,128)S(1)} %get-tuple-element.40), channel_id=1, source_target_pairs={{1,2},{3,0},{2,1},{0,3},{5,6},{7,4},{6,5},{4,7},{9,10},{11,8},{10,... | collective-permute-start | bytes 884744 | tf_op jit(solution)/shard_map/ppermute | solution.py:587
